TPU v7x, 256 devices: a whole 4x4x8 slice. The times are simulated.
256 devices in a mesh: ta: 8 (over y, core), ha: 4 (over x), wa: 8 (over z).
Axes of the slice: x: 4, y: 4, z: 8, core: 2. Of those that a mesh axis runs over, the one named last changes fastest.
Arguments:
- latent: bfloat16 [32, 16, 64, 512], P('ta', 'ha', 'wa'), may hold values from -6 to 6
- cotangent: bfloat16 [32, 32, 128, 512], P('ta', 'ha', 'wa'), may hold values from -6 to 6
- conv_bias: float32 [512], replicated, may hold values from -3 to 3
- conv_weight: bfloat16 [3, 3, 3, 512, 512], P(None, None, None, ('ha', 'wa')), may hold values from -0.0546875 to 0.0546875
- up_weight: bfloat16 [3, 3, 512, 512], P(None, None, ('ha', 'wa')), may hold values from -0.09375 to 0.09375
Outputs:
- latent_grad: bfloat16 [32, 16, 64, 512], P('ta', 'ha', 'wa')
All inputs are finite; a program needn't handle non-finite values.
Results may differ from a plain program's by a relative error of at most 0.0049.
Values may be sent and summed in bfloat16 or wider, within the bound.
No kernel may reach another device: no remote copies, remote signals or barrier semaphores. Data moves between devices by JAX's collectives and lax.ppermute only.
A program may use at most 128 MiB of HBM per device.

v0:
```python
import jax
import jax.numpy as jnp
from jax import lax
from jax.sharding import PartitionSpec as P


def passed_along(block, axis, distance):
    devices = range(lax.axis_size(axis))
    route = [(i - distance, i) for i in devices if i - distance in devices]
    return lax.ppermute(block, axis, route)


def extended(x, sides, width):
    for axis, dim in sides:
        devices, length = (lax.axis_size(axis), x.shape[dim])
        up = [(i, (i + 1) % devices) for i in range(devices - 1)]
        down = [(j, i) for i, j in up]
        last = lax.slice_in_dim(x, length - width, length, axis=dim)
        initial = lax.slice_in_dim(x, 0, width, axis=dim)
        before = lax.ppermute(last, axis, up)
        after = lax.ppermute(initial, axis, down)
        x = jnp.concatenate([before, x, after], axis=dim)
    return x


def conv_taps(padded, weight, backward):
    depth = weight.shape[0]
    frames = padded.shape[0] - depth + 1
    row_count = padded.shape[1] - 2
    col_count = padded.shape[2] - 2
    out_chan = weight.shape[3] if backward else weight.shape[4]
    summed = jnp.zeros((frames * row_count * col_count, out_chan), jnp.float32)
    for tap_t in range(depth):
        for tap_h in range(3):
            for tap_w in range(3):
                if backward:
                    off_t, off_h, off_w = (depth - 1 - tap_t, 2 - tap_h, 2 - tap_w)
                else:
                    off_t, off_h, off_w = (tap_t, tap_h, tap_w)
                window = padded[
                    off_t : off_t + frames, off_h : off_h + row_count, off_w : off_w + col_count
                ]
                window = window.reshape(-1, padded.shape[3])
                kernel = weight[tap_t, tap_h, tap_w]
                if backward:
                    summed = summed + lax.dot_general(
                        window, kernel, (((1,), (1,)), ((), ())), preferred_element_type=jnp.float32
                    )
                else:
                    summed = summed + jnp.dot(window, kernel, preferred_element_type=jnp.float32)
    return summed.reshape(frames, row_count, col_count, out_chan)


def from_neighbor(frames_pair, step_by):
    return passed_along(frames_pair, "ta", step_by)


def with_rims(field, rim_width):
    return extended(field, (("ha", 1), ("wa", 2)), rim_width)


def on_device(latent, cotangent, conv_bias, conv_weight, up_weight):
    local_t, local_h, local_w, chans = latent.shape
    rim_width = 1
    at_start = lax.axis_index("ta") == 0
    conv_full, up_full = (
        lax.all_gather(conv_weight, ("ha", "wa"), axis=3, tiled=True),
        lax.all_gather(up_weight, ("ha", "wa"), axis=2, tiled=True),
    )
    past_frames = from_neighbor(latent[local_t - 2 :], 1)
    first_frame = jnp.concatenate([latent[:1], latent[:1]], axis=0)
    past_frames = jnp.where(at_start, first_frame, past_frames)
    latent_ext = jnp.concatenate([past_frames, latent], axis=0)
    latent_rim = with_rims(latent_ext, rim_width)
    pre_act = conv_taps(latent_rim, conv_full, False) + conv_bias
    cot_rim = with_rims(cotangent, 2 * rim_width - 1)
    fine_rows = cot_rim.shape[1] - 2
    fine_cols = cot_rim.shape[2] - 2
    grad_up = conv_taps(cot_rim, up_full[None], True)
    grad_act = grad_up.reshape(local_t, fine_rows // 2, 2, fine_cols // 2, 2, chans).sum(
        axis=(2, 4)
    )
    sigmoid_h = jax.nn.sigmoid(pre_act)
    grad_pre = (grad_act * sigmoid_h * (1.0 + pre_act * (1.0 - sigmoid_h))).astype(jnp.bfloat16)
    grad_rim = with_rims(grad_pre, 1)
    later_frames = from_neighbor(grad_rim[:2], -1)
    grad_ext = jnp.concatenate([grad_rim, later_frames], axis=0)
    own_grad = conv_taps(grad_ext, conv_full, True)

    def pad_terms(operand):
        lead = jnp.concatenate([jnp.zeros_like(operand[:2]), operand[:2]], axis=0)
        both = conv_taps(lead, conv_full, True)
        return both[0] + both[1]

    def no_terms(operand):
        return jnp.zeros((local_h, local_w, chans), jnp.float32)

    pad_grad = lax.cond(at_start, pad_terms, no_terms, grad_rim)
    own_grad = own_grad.at[0].add(pad_grad)
    return own_grad.astype(jnp.bfloat16)


def solution(mesh):
    in_specs = (
        P("ta", "ha", "wa", None),
        P("ta", "ha", "wa", None),
        P(),
        P(None, None, None, ("ha", "wa"), None),
        P(None, None, ("ha", "wa"), None),
    )
    out_specs = P("ta", "ha", "wa", None)
    return jax.shard_map(
        on_device, mesh=mesh, in_specs=in_specs, out_specs=out_specs, check_vma=False
    )
```

profile of v0, /device:TPU:34, one launch (start us, length us, event | category | flops | bytes accessed | tf_op | source)
XLA Modules:
  0.0 347.6 jit_solution(15236710265888101942)
XLA Ops:
  8.9 3.4 collective-permute-start
  12.3 2.4 collective-permute-start.1
  18.5 1.6 pad_maximum_fusion.5
  20.3 2.0 collective-permute-start.2
  22.3 3.8 %collective-permute-start.3 = (bf16[4,10,1,512]{3,2,1,0:T(2,128)(2,1)S(1)}, bf16[4,10,1,512]{3,2,1,0:T(2,128)(2,1)S(1)}, u32[]{:S(2)}, u32[]{:S(2)}) collective-permute-start(bf16[4,10,1,512]{3,2,1,0:T(2,128)(2,1)S(1)} %get-tuple-element.55), channel_id=1, source_target_pairs={{0,1},{1,2},{2,3},{3,4},{4,5},{5,6},{6,7},{8,9},{9,10},{10,11},{11... | collective-permute-start | bytes 122888 | tf_op jit(solution)/shard_map/ppermute | solution.py:20
  26.1 1.6 pad_maximum_fusion.11
  28.5 2.5 collective-permute-start.6
  31.0 3.5 %collective-permute-start.5 = (bf16[6,1,8,512]{3,2,1,0:T(8,128)(2,1)S(1)}, bf16[6,1,8,512]{3,2,1,0:T(8,128)(2,1)S(1)}, u32[]{:S(2)}, u32[]{:S(2)}) collective-permute-start(bf16[6,1,8,512]{3,2,1,0:T(8,128)(2,1)S(1)} %get-tuple-element.122), channel_id=1, source_target_pairs={{0,8},{8,16},{16,24},{1,9},{9,17},{17,25},{2,10},{10,18},{18,26},{... | collective-permute-start | bytes 147464 | tf_op jit(solution)/shard_map/ppermute | solution.py:20
  34.5 2.1 pad_maximum_fusion.4
  38.7 1.9 collective-permute-start.8
  40.6 3.9 %collective-permute-start.7 = (bf16[6,6,1,512]{3,2,1,0:T(2,128)(2,1)S(1)}, bf16[6,6,1,512]{3,2,1,0:T(2,128)(2,1)S(1)}, u32[]{:S(2)}, u32[]{:S(2)}) collective-permute-start(bf16[6,6,1,512]{3,2,1,0:T(2,128)(2,1)S(1)} %get-tuple-element.106), channel_id=1, source_target_pairs={{0,1},{1,2},{2,3},{3,4},{4,5},{5,6},{6,7},{8,9},{9,10},{10,11},{11... | collective-permute-start | bytes 110600 | tf_op jit(solution)/shard_map/ppermute | solution.py:20
  48.4 1.5 fusion.99
  49.9 45.0 %all-gather.3.cloned.1.call-done = bf16[3,3,512,512]{3,2,1,0:T(8,128)(2,1)} async-done(((bf16[3,3,16,512]{3,2,1,0:T(8,128)(2,1)}), bf16[3,3,512,512]{3,2,1,0:T(8,128)(2,1)}) %all-gather.3.cloned.1.call-update) | async-done | bytes 4718608 | tf_op jit(solution)/shard_map/all_gather | solution.py:68
  94.9 1.7 fusion.82
  96.6 1.5 fusion.83
  98.1 1.5 fusion.84
  99.6 1.7 convolution_add_fusion.31
  101.3 1.7 convolution_add_fusion.30
  103.0 1.5 convolution_add_fusion.29
  104.5 1.5 convolution_add_fusion.28
  106.0 1.5 convolution_add_fusion.27
  107.5 1.6 fusion.75
  110.6 109.6 %all-gather.5.cloned.1.call-done = bf16[3,3,3,512,512]{4,3,2,1,0:T(8,128)(2,1)} async-done(((bf16[3,3,3,16,512]{4,3,2,1,0:T(8,128)(2,1)}), bf16[3,3,3,512,512]{4,3,2,1,0:T(8,128)(2,1)}) %all-gather.5.cloned.1.call-update) | async-done | bytes 14155792 | tf_op jit(solution)/shard_map/all_gather | solution.py:67
  220.2 1.5 fusion.86
  221.7 1.6 convolution_add_fusion.81
  223.4 1.8 convolution_add_fusion.80
  226.5 1.3 convolution_add_fusion.78
  227.9 1.3 convolution_add_fusion.77
  229.2 1.3 convolution_add_fusion.76
  230.6 1.3 convolution_add_fusion.75
  231.9 1.3 convolution_add_fusion.74
  233.3 1.3 convolution_add_fusion.73
  234.7 1.3 convolution_add_fusion.72
  236.0 1.3 convolution_add_fusion.71
  237.4 1.3 convolution_add_fusion.70
  245.1 3.7 %collective-permute-start.10 = (bf16[4,1,8,512]{3,2,1,0:T(8,128)(2,1)S(1)}, bf16[4,1,8,512]{3,2,1,0:T(8,128)(2,1)S(1)}, u32[]{:S(2)}, u32[]{:S(2)}) collective-permute-start(bf16[4,1,8,512]{3,2,1,0:T(8,128)(2,1)S(1)} %get-tuple-element.126), channel_id=1, source_target_pairs={{8,0},{16,8},{24,16},{9,1},{17,9},{25,17},{10,2},{18,10},{26,18},{... | collective-permute-start | bytes 98312 | tf_op jit(solution)/shard_map/ppermute | solution.py:21
  248.8 2.1 collective-permute-start.9
  251.0 3.6 %collective-permute-done.9 = bf16[4,1,8,512]{3,2,1,0:T(8,128)(2,1)S(1)} collective-permute-done((bf16[4,1,8,512]{3,2,1,0:T(8,128)(2,1)S(1)}, bf16[4,1,8,512]{3,2,1,0:T(8,128)(2,1)S(1)}, u32[]{:S(2)}, u32[]{:S(2)}) %collective-permute-start.9) | collective-permute-done | bytes 32800 | tf_op jit(solution)/shard_map/ppermute | solution.py:20
  254.7 4.1 %collective-permute-start.12 = (bf16[4,6,1,512]{3,2,1,0:T(2,128)(2,1)S(1)}, bf16[4,6,1,512]{3,2,1,0:T(2,128)(2,1)S(1)}, u32[]{:S(2)}, u32[]{:S(2)}) collective-permute-start(bf16[4,6,1,512]{3,2,1,0:T(2,128)(2,1)S(1)} %get-tuple-element.115), channel_id=1, source_target_pairs={{1,0},{2,1},{3,2},{4,3},{5,4},{6,5},{7,6},{9,8},{10,9},{11,10},{12... | collective-permute-start | bytes 73736 | tf_op jit(solution)/shard_map/ppermute | solution.py:21
  258.9 1.9 collective-permute-start.11
  260.8 4.0 %collective-permute-done.11 = bf16[4,6,1,512]{3,2,1,0:T(2,128)(2,1)S(1)} collective-permute-done((bf16[4,6,1,512]{3,2,1,0:T(2,128)(2,1)S(1)}, bf16[4,6,1,512]{3,2,1,0:T(2,128)(2,1)S(1)}, u32[]{:S(2)}, u32[]{:S(2)}) %collective-permute-start.11) | collective-permute-done | bytes 24608 | tf_op jit(solution)/shard_map/ppermute | solution.py:20
  266.6 36.1 %conditional.1 = (f32[1,4,8,512]{3,2,1,0:T(8,128)S(1)}) conditional(s32[]{:T(128)} %convert_element_type.14, () %tuple.17, (bf16[4,6,10,512]{3,2,1,0:T(8,128)(2,1)S(1)}, bf16[3,3,3,512,512]{4,3,2,1,0:T(8,128)(2,1)}) %tuple.18), branch_computations={%region_1.2_spmd, %region_2.3_spmd} | conditional | flops 906838016 | bytes 24616968 | solution.py:98
  306.1 1.4 fusion.85
  310.2 1.3 convolution_add_fusion.53
  329.2 1.3 convolution_add_fusion.39
  331.9 1.4 fusion.76
  334.6 1.3 convolution_add_fusion.35
  338.7 1.3 fusion.77
  (137 shorter events, 89.2 us)
Async XLA Ops:
  6.5 88.4 %all-gather.3.cloned.1.call-start = ((), (), s32[]{:S(2)}) async-start(), calls=%async_computation | async-start | bytes 4866048 | tf_op jit(solution)/shard_map/all_gather | solution.py:68
  7.3 212.9 %all-gather.5.cloned.1.call-start = ((), (), s32[]{:S(2)}) async-start(), calls=%async_computation.1 | async-start | bytes 14598144 | tf_op jit(solution)/shard_map/all_gather | solution.py:67
  8.9 8.8 %collective-permute-start = (bf16[4,1,16,512]{3,2,1,0:T(8,128)(2,1)S(1)}, bf16[4,1,16,512]{3,2,1,0:T(8,128)(2,1)S(1)}, u32[]{:S(2)}, u32[]{:S(2)}) collective-permute-start(bf16[4,1,16,512]{3,2,1,0:T(8,128)(2,1)S(1)} %get-tuple-element.96), channel_id=1, source_target_pairs={{0,8},{8,16},{16,24},{1,9},{9,17},{17,25},{2,10},{10,18},{18,26},{... | collective-permute-start | bytes 196616 | tf_op jit(solution)/shard_map/ppermute | solution.py:20
  12.3 6.2 %collective-permute-start.1 = (bf16[4,1,16,512]{3,2,1,0:T(8,128)(2,1)S(1)}, bf16[4,1,16,512]{3,2,1,0:T(8,128)(2,1)S(1)}, u32[]{:S(2)}, u32[]{:S(2)}) collective-permute-start(bf16[4,1,16,512]{3,2,1,0:T(8,128)(2,1)S(1)} %get-tuple-element.95), channel_id=1, source_target_pairs={{8,0},{16,8},{24,16},{9,1},{17,9},{25,17},{10,2},{18,10},{26,18},{... | collective-permute-start | bytes 196616 | tf_op jit(solution)/shard_map/ppermute | solution.py:21
  15.6 10.5 %collective-permute-start.4 = (bf16[2,4,8,512]{3,2,1,0:T(8,128)(2,1)S(1)}, bf16[2,4,8,512]{3,2,1,0:T(8,128)(2,1)S(1)}, u32[]{:S(2)}, u32[]{:S(2)}) collective-permute-start(bf16[2,4,8,512]{3,2,1,0:T(8,128)(2,1)S(1)} %slice.606), channel_id=1, source_target_pairs={{0,32},{32,64},{64,96},{96,128},{128,160},{160,192},{192,224},{1,3... | collective-permute-start | bytes 196616 | tf_op jit(solution)/shard_map/ppermute | solution.py:10
  20.3 14.3 %collective-permute-start.2 = (bf16[4,10,1,512]{3,2,1,0:T(2,128)(2,1)S(1)}, bf16[4,10,1,512]{3,2,1,0:T(2,128)(2,1)S(1)}, u32[]{:S(2)}, u32[]{:S(2)}) collective-permute-start(bf16[4,10,1,512]{3,2,1,0:T(2,128)(2,1)S(1)} %get-tuple-element.54), channel_id=1, source_target_pairs={{1,0},{2,1},{3,2},{4,3},{5,4},{6,5},{7,6},{9,8},{10,9},{11,10},{12... | collective-permute-start | bytes 122888 | tf_op jit(solution)/shard_map/ppermute | solution.py:21
  22.3 12.2 %collective-permute-start.3 = (bf16[4,10,1,512]{3,2,1,0:T(2,128)(2,1)S(1)}, bf16[4,10,1,512]{3,2,1,0:T(2,128)(2,1)S(1)}, u32[]{:S(2)}, u32[]{:S(2)}) collective-permute-start(bf16[4,10,1,512]{3,2,1,0:T(2,128)(2,1)S(1)} %get-tuple-element.55), channel_id=1, source_target_pairs={{0,1},{1,2},{2,3},{3,4},{4,5},{5,6},{6,7},{8,9},{9,10},{10,11},{11... | collective-permute-start | bytes 122888 | tf_op jit(solution)/shard_map/ppermute | solution.py:20
  28.5 8.2 %collective-permute-start.6 = (bf16[6,1,8,512]{3,2,1,0:T(8,128)(2,1)S(1)}, bf16[6,1,8,512]{3,2,1,0:T(8,128)(2,1)S(1)}, u32[]{:S(2)}, u32[]{:S(2)}) collective-permute-start(bf16[6,1,8,512]{3,2,1,0:T(8,128)(2,1)S(1)} %get-tuple-element.121), channel_id=1, source_target_pairs={{8,0},{16,8},{24,16},{9,1},{17,9},{25,17},{10,2},{18,10},{26,18},{... | collective-permute-start | bytes 147464 | tf_op jit(solution)/shard_map/ppermute | solution.py:21
  31.0 73.5 %copy-start.2 = (bf16[4,8,16,512]{3,2,1,0:T(8,128)(2,1)S(1)}, bf16[4,8,16,512]{3,2,1,0:T(8,128)(2,1)}, u32[]{:S(2)}) copy-start(bf16[4,8,16,512]{3,2,1,0:T(8,128)(2,1)} %param.10) | copy-start | bytes 1572868
  31.0 6.6 %collective-permute-start.5 = (bf16[6,1,8,512]{3,2,1,0:T(8,128)(2,1)S(1)}, bf16[6,1,8,512]{3,2,1,0:T(8,128)(2,1)S(1)}, u32[]{:S(2)}, u32[]{:S(2)}) collective-permute-start(bf16[6,1,8,512]{3,2,1,0:T(8,128)(2,1)S(1)} %get-tuple-element.122), channel_id=1, source_target_pairs={{0,8},{8,16},{16,24},{1,9},{9,17},{17,25},{2,10},{10,18},{18,26},{... | collective-permute-start | bytes 147464 | tf_op jit(solution)/shard_map/ppermute | solution.py:20
  38.7 7.7 %collective-permute-start.8 = (bf16[6,6,1,512]{3,2,1,0:T(2,128)(2,1)S(1)}, bf16[6,6,1,512]{3,2,1,0:T(2,128)(2,1)S(1)}, u32[]{:S(2)}, u32[]{:S(2)}) collective-permute-start(bf16[6,6,1,512]{3,2,1,0:T(2,128)(2,1)S(1)} %get-tuple-element.105), channel_id=1, source_target_pairs={{1,0},{2,1},{3,2},{4,3},{5,4},{6,5},{7,6},{9,8},{10,9},{11,10},{12... | collective-permute-start | bytes 110600 | tf_op jit(solution)/shard_map/ppermute | solution.py:21
  40.6 6.5 %collective-permute-start.7 = (bf16[6,6,1,512]{3,2,1,0:T(2,128)(2,1)S(1)}, bf16[6,6,1,512]{3,2,1,0:T(2,128)(2,1)S(1)}, u32[]{:S(2)}, u32[]{:S(2)}) collective-permute-start(bf16[6,6,1,512]{3,2,1,0:T(2,128)(2,1)S(1)} %get-tuple-element.106), channel_id=1, source_target_pairs={{0,1},{1,2},{2,3},{3,4},{4,5},{5,6},{6,7},{8,9},{9,10},{10,11},{11... | collective-permute-start | bytes 110600 | tf_op jit(solution)/shard_map/ppermute | solution.py:20
  109.1 133.3 %copy-start.9 = (bf16[4,4,8,512]{3,2,1,0:T(8,128)(2,1)S(1)}, bf16[4,4,8,512]{3,2,1,0:T(8,128)(2,1)}, u32[]{:S(2)}) copy-start(bf16[4,4,8,512]{3,2,1,0:T(8,128)(2,1)} %get-tuple-element.77) | copy-start | bytes 393220
  109.2 133.5 %copy-start.8 = (bf16[4,4,8,512]{3,2,1,0:T(8,128)(2,1)S(1)}, bf16[4,4,8,512]{3,2,1,0:T(8,128)(2,1)}, u32[]{:S(2)}) copy-start(bf16[4,4,8,512]{3,2,1,0:T(8,128)(2,1)} %get-tuple-element.138) | copy-start | bytes 393220
  109.2 133.7 %copy-start.3 = (bf16[4,4,8,512]{3,2,1,0:T(8,128)(2,1)S(1)}, bf16[4,4,8,512]{3,2,1,0:T(8,128)(2,1)}, u32[]{:S(2)}) copy-start(bf16[4,4,8,512]{3,2,1,0:T(8,128)(2,1)} %get-tuple-element.131) | copy-start | bytes 393220
  109.2 134.0 %copy-start.7 = (bf16[4,4,8,512]{3,2,1,0:T(8,128)(2,1)S(1)}, bf16[4,4,8,512]{3,2,1,0:T(8,128)(2,1)}, u32[]{:S(2)}) copy-start(bf16[4,4,8,512]{3,2,1,0:T(8,128)(2,1)} %get-tuple-element.76) | copy-start | bytes 393220
  109.2 134.2 %copy-start.6 = (bf16[4,4,8,512]{3,2,1,0:T(8,128)(2,1)S(1)}, bf16[4,4,8,512]{3,2,1,0:T(8,128)(2,1)}, u32[]{:S(2)}) copy-start(bf16[4,4,8,512]{3,2,1,0:T(8,128)(2,1)} %get-tuple-element.139) | copy-start | bytes 393220
  109.2 134.5 %copy-start.1 = (bf16[4,4,8,512]{3,2,1,0:T(8,128)(2,1)S(1)}, bf16[4,4,8,512]{3,2,1,0:T(8,128)(2,1)}, u32[]{:S(2)}) copy-start(bf16[4,4,8,512]{3,2,1,0:T(8,128)(2,1)} %param.9) | copy-start | bytes 393220
  109.8 134.1 %copy-start.5 = (bf16[4,4,8,512]{3,2,1,0:T(8,128)(2,1)S(1)}, bf16[4,4,8,512]{3,2,1,0:T(8,128)(2,1)}, u32[]{:S(2)}) copy-start(bf16[4,4,8,512]{3,2,1,0:T(8,128)(2,1)} %get-tuple-element.75) | copy-start | bytes 393220
  110.6 133.5 %copy-start.4 = (bf16[4,4,8,512]{3,2,1,0:T(8,128)(2,1)S(1)}, bf16[4,4,8,512]{3,2,1,0:T(8,128)(2,1)}, u32[]{:S(2)}) copy-start(bf16[4,4,8,512]{3,2,1,0:T(8,128)(2,1)} %get-tuple-element.140) | copy-start | bytes 393220
  220.2 18.5 %copy-start = (bf16[3,3,3,512,512]{4,3,2,1,0:T(8,128)(2,1)S(1)}, bf16[3,3,3,512,512]{4,3,2,1,0:T(8,128)(2,1)}, u32[]{:S(2)}) copy-start(bf16[3,3,3,512,512]{4,3,2,1,0:T(8,128)(2,1)} %all-gather.5.cloned.1.call-done) | copy-start | bytes 42467332
  223.3 21.3 %copy-start.10 = (bf16[4,4,8,512]{3,2,1,0:T(8,128)(2,1)S(1)}, bf16[4,4,8,512]{3,2,1,0:T(8,128)(2,1)}, u32[]{:S(2)}) copy-start(bf16[4,4,8,512]{3,2,1,0:T(8,128)(2,1)} %get-tuple-element.74) | copy-start | bytes 393220
  223.3 21.3 %copy-start.11 = (f32[512]{0:T(512)S(1)}, f32[512]{0:T(512)}, u32[]{:S(2)}) copy-start(f32[512]{0:T(512)} %param.11) | copy-start | bytes 6148
  245.1 5.9 %collective-permute-start.10 = (bf16[4,1,8,512]{3,2,1,0:T(8,128)(2,1)S(1)}, bf16[4,1,8,512]{3,2,1,0:T(8,128)(2,1)S(1)}, u32[]{:S(2)}, u32[]{:S(2)}) collective-permute-start(bf16[4,1,8,512]{3,2,1,0:T(8,128)(2,1)S(1)} %get-tuple-element.126), channel_id=1, source_target_pairs={{8,0},{16,8},{24,16},{9,1},{17,9},{25,17},{10,2},{18,10},{26,18},{... | collective-permute-start | bytes 98312 | tf_op jit(solution)/shard_map/ppermute | solution.py:21
  248.8 5.8 %collective-permute-start.9 = (bf16[4,1,8,512]{3,2,1,0:T(8,128)(2,1)S(1)}, bf16[4,1,8,512]{3,2,1,0:T(8,128)(2,1)S(1)}, u32[]{:S(2)}, u32[]{:S(2)}) collective-permute-start(bf16[4,1,8,512]{3,2,1,0:T(8,128)(2,1)S(1)} %get-tuple-element.125), channel_id=1, source_target_pairs={{0,8},{8,16},{16,24},{1,9},{9,17},{17,25},{2,10},{10,18},{18,26},{... | collective-permute-start | bytes 98312 | tf_op jit(solution)/shard_map/ppermute | solution.py:20
  254.7 6.1 %collective-permute-start.12 = (bf16[4,6,1,512]{3,2,1,0:T(2,128)(2,1)S(1)}, bf16[4,6,1,512]{3,2,1,0:T(2,128)(2,1)S(1)}, u32[]{:S(2)}, u32[]{:S(2)}) collective-permute-start(bf16[4,6,1,512]{3,2,1,0:T(2,128)(2,1)S(1)} %get-tuple-element.115), channel_id=1, source_target_pairs={{1,0},{2,1},{3,2},{4,3},{5,4},{6,5},{7,6},{9,8},{10,9},{11,10},{12... | collective-permute-start | bytes 73736 | tf_op jit(solution)/shard_map/ppermute | solution.py:21
  258.9 6.0 %collective-permute-start.11 = (bf16[4,6,1,512]{3,2,1,0:T(2,128)(2,1)S(1)}, bf16[4,6,1,512]{3,2,1,0:T(2,128)(2,1)S(1)}, u32[]{:S(2)}, u32[]{:S(2)}) collective-permute-start(bf16[4,6,1,512]{3,2,1,0:T(2,128)(2,1)S(1)} %get-tuple-element.116), channel_id=1, source_target_pairs={{0,1},{1,2},{2,3},{3,4},{4,5},{5,6},{6,7},{8,9},{9,10},{10,11},{11... | collective-permute-start | bytes 73736 | tf_op jit(solution)/shard_map/ppermute | solution.py:20
  265.3 40.2 %collective-permute-start.13 = (bf16[2,6,10,512]{3,2,1,0:T(8,128)(2,1)S(1)}, bf16[2,6,10,512]{3,2,1,0:T(8,128)(2,1)S(1)}, u32[]{:S(2)}, u32[]{:S(2)}) collective-permute-start(bf16[2,6,10,512]{3,2,1,0:T(8,128)(2,1)S(1)} %slice.776), channel_id=1, source_target_pairs={{32,0},{64,32},{96,64},{128,96},{160,128},{192,160},{224,192},{33,... | collective-permute-start | bytes 368648 | tf_op jit(solution)/shard_map/ppermute | solution.py:10
Sparse Core Ops, SparseCore 0:
  9.9 84.9 all-gather.2
  97.5 122.6 all-gather.4
where the time goes:
time: 352 us; the launch traced here: 348 us
  waiting for transfers between devices  166 us (47%)
  matrix products  111 us (32%)
  starting transfers between devices  38 us (11%)
  between operations  14.4 us (4%)
  other arithmetic  11.9 us (3%)
  local copies, waits for them, and re-layouts  6.22 us (2%)
    all_gather x1, waiting for transfers between devices, on_device(): lax.all_gather(conv_weight, ('ha', 'wa'), axis=3, tiled=True)  110 us
    dot_general x63, matrix products, conv_taps(): lax.dot_general(window, kernel, (((1,), (1,)), ((), ())), preferred_eleme...  86.3 us
    all_gather x1, waiting for transfers between devices, on_device(): lax.all_gather(up_weight, ('ha', 'wa'), axis=2, tiled=True)  45 us
    dot_general x27, matrix products, conv_taps(): jnp.dot(window, kernel, preferred_element_type=jnp.float32)  24.5 us
    ppermute x6, starting transfers between devices, extended(): before = lax.ppermute(last, axis, up)  18.7 us
    ppermute x6, starting transfers between devices, extended(): after = lax.ppermute(initial, axis, down)  16.7 us
    ppermute x6, waiting for transfers between devices, extended(): before = lax.ppermute(last, axis, up)  9.3 us
    concatenate x9, other arithmetic, extended(): x = jnp.concatenate([before, x, after], axis=dim)  7.7 us
  transfers between devices with their start and end apart: 16, of which 7 were waited for; matrix products, arithmetic and copies ran while one was open for 20% of the time, Pallas kernels for 0%

commit v1 on v0

v1 whole, which is shorter than its diff:
```python
import functools

import jax
import jax.numpy as jnp
from jax import lax
from jax.experimental import pallas as pl
from jax.experimental.pallas import tpu as pltpu
from jax.sharding import PartitionSpec as P

F32, BF16 = jnp.float32, jnp.bfloat16
LANES = 128
VMEM_LIMIT = 48 * 1024 * 1024


def roll_rows(x, shift):
    return pltpu.roll(x, shift, x.ndim - 2)


def row_in_block(shape):
    return lax.broadcasted_iota(jnp.int32, shape, len(shape) - 2) % 4


def from_above(x):
    prev = jnp.concatenate([jnp.zeros_like(x[:, :1]), x[:, :-1]], axis=1)
    n = x.shape[2]
    return jnp.where(row_in_block(x.shape) == 0, roll_rows(prev, n - 3), roll_rows(x, 1))


def from_below(x):
    later = jnp.concatenate([x[:, 1:], jnp.zeros_like(x[:, :1])], axis=1)
    n = x.shape[2]
    return jnp.where(row_in_block(x.shape) == 3, roll_rows(later, 3), roll_rows(x, n - 1))


def weight_copies(own_ref, other_ref, groups, first, w_ref, sem):
    n_wa, n_ha, half, shard, _ = own_ref.shape
    core = lax.rem(lax.axis_index("ta"), 2)
    spans = [
        (max(first, part * half), min(first + groups, (part + 1) * half), part) for part in (0, 1)
    ]
    spans = [s for s in spans if s[0] < s[1]]

    def each(action):
        for index, (lo, hi, part) in enumerate(spans):
            for holder, src in ((part, own_ref), (1 - part, other_ref)):

                @pl.when(core == holder)
                def _(lo=lo, hi=hi, part=part, src=src, index=index):
                    for wa in range(n_wa):
                        for ha in range(n_ha):
                            row = ha * n_wa * shard + wa * shard
                            copy = pltpu.make_async_copy(
                                src.at[wa, ha, pl.ds(lo - part * half, hi - lo)],
                                w_ref.at[pl.ds(lo - first, hi - lo), pl.ds(row, shard)],
                                sem.at[index, wa, ha],
                            )
                            getattr(copy, action)()

    return functools.partial(each, "start"), functools.partial(each, "wait")


def up_kernel(cot_ref, own_ref, other_ref, out_ref, w_ref, rows_ref, sem):
    start, wait = weight_copies(own_ref, other_ref, 3, 9, w_ref, sem)
    start()
    n_ha = cot_ref.shape[0]
    for par in range(2):
        cot = jnp.stack([cot_ref[x, par] for x in range(n_ha)], axis=1).astype(F32)
        even, odd = cot[:, :, 0], cot[:, :, 1]
        rows_ref[par, :, :, :, 0:LANES] = odd + from_below(even)
        rows_ref[par, :, :, :, LANES : 2 * LANES] = even + odd
        rows_ref[par, :, :, :, 2 * LANES : 3 * LANES] = even + from_above(odd)
    wait()
    total = None
    for b in range(3):
        box = None
        for e in (1 - b, 2 - b):
            par, off = (e + 1) % 2, (e + 1) // 2
            part = rows_ref[par, off : off + 8]
            box = part if box is None else box + part
        box = box.reshape(-1, 3 * LANES)
        high = box.astype(BF16)
        low = (box - high.astype(F32)).astype(BF16)
        for piece in (high, low):
            term = lax.dot_general(
                piece, w_ref[b], (((1,), (1,)), ((), ())), preferred_element_type=F32
            )
            total = term if total is None else total + term
    for x in range(n_ha):
        out_ref[x] = total[:, x * LANES : (x + 1) * LANES].astype(BF16)


def fwd_kernel(lat_ref, own_ref, other_ref, bias_ref, act_ref, out_ref, w_ref, win_ref, sem):
    start, wait = weight_copies(own_ref, other_ref, 9, 0, w_ref, sem)
    start()
    n_ha = lat_ref.shape[0]
    for x in range(n_ha):
        for pair in range(5):
            two = lat_ref[x, pair * 48 : pair * 48 + 48, :].astype(F32)
            for one in range(2):
                for k in range(3):
                    lo = one * 24 + 4 * k
                    win_ref[k, 2 * pair + one, x] = two[lo : lo + 16].astype(BF16)
    wait()
    total = None
    for k in range(3):
        for b in range(3):
            window = win_ref[k, b : b + 8].reshape(-1, win_ref.shape[-1])
            term = jnp.dot(window, w_ref[3 * k + b], preferred_element_type=F32)
            total = term if total is None else total + term
    total = total.reshape(8, n_ha, 16, 3 * LANES)
    pre = (
        from_above(total[..., :LANES])
        + total[..., LANES : 2 * LANES]
        + from_below(total[..., 2 * LANES :])
        + bias_ref[...].reshape(1, 1, 1, LANES)
    )
    grad = act_ref[0].astype(F32)
    for x in range(1, n_ha):
        grad = grad + act_ref[x].astype(F32)
    grad = grad.reshape(pre.shape)
    sig = 1.0 / (1.0 + jnp.exp(-pre))
    out_ref[...] = (grad * sig * (1.0 + pre * (1.0 - sig))).astype(BF16)


def bwd_kernel(g_ref, later_ref, left_ref, right_ref, own_ref, other_ref, out_ref, w_ref, win_ref, sem):
    start, wait = weight_copies(own_ref, other_ref, 9, 0, w_ref, sem)
    start()
    n_ha = g_ref.shape[1]
    at_start = (lax.axis_index("ta") == 0).astype(F32)
    grad = jnp.concatenate([g_ref[...].astype(F32), later_ref[...].astype(F32)], axis=2)
    grad = jnp.concatenate(
        [left_ref[...].astype(F32)[None], grad, right_ref[...].astype(F32)[None]], axis=0
    )
    zero, one, two = grad[:, :, 0:4], grad[:, :, 4:8], grad[:, :, 8:12]
    windows = [
        grad[:, :, 0:16],
        jnp.concatenate([one + at_start * zero, grad[:, :, 8:20]], axis=2),
        jnp.concatenate([two + at_start * (zero + one), grad[:, :, 12:24]], axis=2),
    ]
    for shift in range(3):
        x = windows[shift]
        win_ref[shift, :, :, :, 0:LANES] = from_below(x).astype(BF16)
        win_ref[shift, :, :, :, LANES : 2 * LANES] = x.astype(BF16)
        win_ref[shift, :, :, :, 2 * LANES : 3 * LANES] = from_above(x).astype(BF16)
    wait()
    total = None
    for k in range(3):
        for b in range(3):
            window = win_ref[2 - k, 2 - b : 10 - b].reshape(-1, 3 * LANES)
            term = lax.dot_general(
                window, w_ref[3 * k + b], (((1,), (1,)), ((), ())), preferred_element_type=F32
            )
            total = term if total is None else total + term
    total = total.astype(BF16).reshape(8, n_ha, 16, -1)
    for x in range(n_ha):
        out_ref[x] = total[:, x]


def call(kernel, out_shape, specs, scratch):
    return pl.pallas_call(
        kernel,
        out_shape=out_shape,
        in_specs=specs,
        out_specs=pl.BlockSpec(memory_space=pltpu.VMEM),
        scratch_shapes=scratch,
        compiler_params=pltpu.CompilerParams(vmem_limit_bytes=VMEM_LIMIT),
    )


def shifted(x, axis, step):
    n = lax.axis_size(axis)
    return lax.ppermute(x, axis, [(i, i + step) for i in range(n) if 0 <= i + step < n])


def on_device(latent, cotangent, conv_bias, conv_weight, up_weight):
    frames, rows, cols, chans = latent.shape
    n_ta, n_ha, n_wa = (lax.axis_size(a) for a in ("ta", "ha", "wa"))
    ta, ha = lax.axis_index("ta"), lax.axis_index("ha")
    shard = conv_weight.shape[3]
    core = lax.rem(ta, 2)

    conv_g = conv_weight.reshape(3, 3, 3, shard, n_ha, LANES).transpose(4, 0, 2, 3, 1, 5)
    up_g = up_weight.reshape(3, 3, shard, n_ha, LANES).transpose(3, 1, 2, 0, 4)
    groups = jnp.concatenate(
        [conv_g.reshape(n_ha, 9, shard, 3 * LANES), up_g.reshape(n_ha, 3, shard, 3 * LANES)], axis=1
    )
    groups = lax.dynamic_slice_in_dim(groups, 6 * core, 6, axis=1)
    groups = lax.all_to_all(groups, "ha", 0, 0)
    w_own = lax.all_gather(groups, "wa", axis=0)
    w_other = lax.ppermute(w_own, "ta", [(i, i ^ 1) for i in range(n_ta)])

    past = shifted(latent[frames - 2 :], "ta", 1)
    past = jnp.where(ta == 0, jnp.broadcast_to(latent[:1], past.shape), past)
    ext = jnp.concatenate([past, latent], axis=0)

    def edge(col_l, col_c):
        return jnp.concatenate(
            [ext[:, :, col_l].reshape(-1, chans), cotangent[:, :, col_c].reshape(-1, chans)], axis=0
        )

    split = (frames + 2) * rows
    left = shifted(edge(cols - 1, 2 * cols - 1), "wa", 1)
    right = shifted(edge(0, 0), "wa", -1)

    def lat_col(x):
        return x[:split].reshape(frames + 2, rows, 1, chans)

    def cot_col(x):
        return x[split:].reshape(frames, 2 * rows, 1, chans)

    lat = jnp.concatenate([lat_col(left), ext, lat_col(right)], axis=2)
    lat = lat.transpose(2, 0, 1, 3).reshape((cols + 2) * split, chans)
    lat = lax.all_gather(lat, "ha", axis=0)
    cot = jnp.concatenate([cot_col(left), cotangent, cot_col(right)], axis=2)
    cot = cot.reshape(frames, rows, 2, cols + 1, 2, n_ha, LANES).transpose(5, 4, 3, 2, 0, 1, 6)
    cot = cot.reshape(n_ha, 2, cols + 1, 2, frames * rows, LANES)
    cot = lax.all_to_all(cot, "ha", 0, 0)

    vmem, anywhere = pl.BlockSpec(memory_space=pltpu.VMEM), pl.BlockSpec(memory_space=pl.ANY)
    points = cols * n_ha * frames * rows
    sem = pltpu.SemaphoreType.DMA((2, n_wa, n_ha))
    w_conv = pltpu.VMEM((9, chans, 3 * LANES), BF16)

    act = call(
        up_kernel,
        jax.ShapeDtypeStruct((n_ha, points, LANES), BF16),
        [vmem, anywhere, anywhere],
        [
            pltpu.VMEM((3, chans, 3 * LANES), BF16),
            pltpu.VMEM((2, cols + 1, n_ha, frames * rows, 3 * LANES), F32),
            sem,
        ],
    )(cot, w_own, w_other)
    act = lax.all_to_all(act, "ha", 0, 0)

    bias = lax.dynamic_slice_in_dim(conv_bias, ha * LANES, LANES).reshape(1, LANES)
    grad = call(
        fwd_kernel,
        jax.ShapeDtypeStruct((cols, n_ha, frames * rows, LANES), BF16),
        [vmem, anywhere, anywhere, vmem, vmem],
        [w_conv, pltpu.VMEM((3, cols + 2, n_ha, frames * rows, chans), BF16), sem],
    )(lat, w_own, w_other, bias, act)

    later = shifted(grad[:, :, : 2 * rows], "ta", -1)
    g_left = shifted(jnp.concatenate([grad[cols - 1], later[cols - 1]], axis=1), "wa", 1)
    g_right = shifted(jnp.concatenate([grad[0], later[0]], axis=1), "wa", -1)

    out = call(
        bwd_kernel,
        jax.ShapeDtypeStruct((n_ha, cols, frames * rows, chans), BF16),
        [vmem, vmem, vmem, vmem, anywhere, anywhere],
        [w_conv, pltpu.VMEM((3, cols + 2, n_ha, frames * rows, 3 * LANES), BF16), sem],
    )(grad, later, g_left, g_right, w_own, w_other)
    out = lax.all_to_all(out, "ha", 0, 0)
    out = out.astype(F32).sum(axis=0).reshape(cols, frames, rows, chans)
    return out.transpose(1, 2, 0, 3).astype(BF16)


def solution(mesh):
    in_specs = (
        P("ta", "ha", "wa", None),
        P("ta", "ha", "wa", None),
        P(),
        P(None, None, None, ("ha", "wa"), None),
        P(None, None, ("ha", "wa"), None),
    )
    return jax.shard_map(
        on_device, mesh=mesh, in_specs=in_specs, out_specs=P("ta", "ha", "wa", None), check_vma=False
    )
```

time: 352 us -> 164 us (0.47)
  the two profiles are of different devices: /device:TPU:34 before, /device:TPU:104 now
where the time goes in v1:
time: 164 us; the launch traced here: 163 us
  waiting for transfers between devices  59.8 us (36%)
  blocking collectives  41.2 us (25%)
  starting transfers between devices  25.6 us (16%)
  Pallas kernels  15.5 us (9%)
  between operations  13.7 us (8%)
  local copies, waits for them, and re-layouts  5.66 us (3%)
    all_gather x1, waiting for transfers between devices, on_device(): w_own = lax.all_gather(groups, 'wa', axis=0)  40.8 us
    all_gather x1, blocking collectives, on_device(): lat = lax.all_gather(lat, 'ha', axis=0)  17.4 us
    ppermute x6, starting transfers between devices, shifted(): lax.ppermute(x, axis, [(i, i + step) for i in range(n) if 0 <= i + step <...  17.2 us
    all_to_all x1, blocking collectives, on_device(): out = lax.all_to_all(out, 'ha', 0, 0)  12.6 us
    all_to_all x1, blocking collectives, on_device(): groups = lax.all_to_all(groups, 'ha', 0, 0)  11.2 us
    ppermute x6, waiting for transfers between devices, shifted(): lax.ppermute(x, axis, [(i, i + step) for i in range(n) if 0 <= i + step <...  10.7 us
    all_to_all x1, waiting for transfers between devices, on_device(): cot = lax.all_to_all(cot, 'ha', 0, 0)  8.3 us
    pallas_call x1, Pallas kernels, on_device(): call(fwd_kernel, jax.ShapeDtypeStruct((cols, n_ha, frames * rows, LANES),...  6.04 us
  transfers between devices with their start and end apart: 10, of which 7 were waited for; matrix products, arithmetic and copies ran while one was open for 2% of the time, Pallas kernels for 0%

profile of v1, /device:TPU:104, one launch (start us, length us, event | category | flops | bytes accessed | tf_op | source)
XLA Modules:
  0.0 162.7 jit_solution(8618499514187626092)
XLA Ops:
  6.5 1.2 reshape.37
  7.7 0.4 copy.44
  8.1 0.4 reshape.38
  8.5 0.0 copy-start.2
  8.5 0.0 copy-start.3
  8.5 0.1 copy.45
  8.7 0.1 reshape.40
  8.8 0.1 fusion
  8.9 11.2 %all_to_all.20 = bf16[4,6,16,384]{3,2,1,0:T(8,128)(2,1)} all-to-all(bf16[4,6,16,384]{3,2,1,0:T(8,128)(2,1)S(1)} %fusion), channel_id=1, replica_groups=mesh['ta'=8,'ha'=4,'wa'=8] {'ha'}, dimensions={0} | all-to-all | bytes 589824 | tf_op jit(solution)/shard_map/all_to_all | solution.py:188
  20.2 0.0 all-gather.3.cloned.1.call-update
  20.2 40.8 %all-gather.3.cloned.1.call-done = bf16[32,6,16,384]{3,2,1,0:T(8,128)(2,1)} async-done(((bf16[4,6,16,384]{3,2,1,0:T(8,128)(2,1)}), bf16[32,6,16,384]{3,2,1,0:T(8,128)(2,1)}) %all-gather.3.cloned.1.call-update) | async-done | bytes 2359312 | tf_op jit(solution)/shard_map/all_gather | solution.py:189
  61.0 0.0 collective-permute-start.3
  61.0 2.4 %collective-permute-start = (bf16[2,4,8,512]{3,2,1,0:T(8,128)(2,1)S(1)}, bf16[2,4,8,512]{3,2,1,0:T(8,128)(2,1)S(1)}, u32[]{:S(2)}, u32[]{:S(2)}) collective-permute-start(bf16[2,4,8,512]{3,2,1,0:T(8,128)(2,1)S(1)} %slice.46), channel_id=1, source_target_pairs={{0,32},{32,64},{64,96},{96,128},{128,160},{160,192},{192,224},{1,3... | collective-permute-start | bytes 196616 | tf_op jit(solution)/shard_map/ppermute | solution.py:172
  63.4 0.1 fusion.2
  63.6 3.0 %collective-permute-done = bf16[2,4,8,512]{3,2,1,0:T(8,128)(2,1)S(1)} collective-permute-done((bf16[2,4,8,512]{3,2,1,0:T(8,128)(2,1)S(1)}, bf16[2,4,8,512]{3,2,1,0:T(8,128)(2,1)S(1)}, u32[]{:S(2)}, u32[]{:S(2)}) %collective-permute-start) | collective-permute-done | bytes 65568 | tf_op jit(solution)/shard_map/ppermute | solution.py:172
  66.6 0.3 maximum_reduce_fusion
  66.9 3.0 %collective-permute-start.1 = (bf16[56,512]{1,0:T(8,128)(2,1)S(1)}, bf16[56,512]{1,0:T(8,128)(2,1)S(1)}, u32[]{:S(2)}, u32[]{:S(2)}) collective-permute-start(bf16[56,512]{1,0:T(8,128)(2,1)S(1)} %pad_maximum_fusion.1), channel_id=1, source_target_pairs={{0,1},{1,2},{2,3},{3,4},{4,5},{5,6},{6,7},{8,9},{9,10},{10,11},{11... | collective-permute-start | bytes 172040 | tf_op jit(solution)/shard_map/ppermute | solution.py:172
  69.9 2.8 %collective-permute-start.2 = (bf16[56,512]{1,0:T(8,128)(2,1)S(1)}, bf16[56,512]{1,0:T(8,128)(2,1)S(1)}, u32[]{:S(2)}, u32[]{:S(2)}) collective-permute-start(bf16[56,512]{1,0:T(8,128)(2,1)S(1)} %pad_maximum_fusion.2), channel_id=1, source_target_pairs={{1,0},{2,1},{3,2},{4,3},{5,4},{6,5},{7,6},{9,8},{10,9},{11,10},{12... | collective-permute-start | bytes 172040 | tf_op jit(solution)/shard_map/ppermute | solution.py:172
  72.8 0.2 collective-permute-done.1
  73.0 0.1 copy.28
  73.0 4.2 %collective-permute-done.2 = bf16[56,512]{1,0:T(8,128)(2,1)S(1)} collective-permute-done((bf16[56,512]{1,0:T(8,128)(2,1)S(1)}, bf16[56,512]{1,0:T(8,128)(2,1)S(1)}, u32[]{:S(2)}, u32[]{:S(2)}) %collective-permute-start.2) | collective-permute-done | bytes 57376 | tf_op jit(solution)/shard_map/ppermute | solution.py:172
  77.2 0.1 copy.29
  77.3 0.4 pad_maximum_fusion
  77.7 0.3 reshape.49
  78.0 1.1 copy.31
  79.1 4.2 %all-to-all-start.1 = ((bf16[4,2,9,2,16,128]{5,4,3,2,1,0:T(8,128)(2,1)}), bf16[4,2,9,2,16,128]{5,4,3,2,1,0:T(8,128)(2,1)S(1)}, u32[]{:S(2)}, u32[]{:S(2)}) async-start(bf16[4,2,9,2,16,128]{5,4,3,2,1,0:T(8,128)(2,1)} %bitcast.12), calls=%async_computation.1 | async-start | bytes 1179648 | tf_op jit(solution)/shard_map/all_to_all | solution.py:217
  83.3 0.0 copy-done
  83.3 0.1 dynamic-slice_bitcast_fusion.bias_ref
  83.4 8.3 %all-to-all-done.1.cot_ref = bf16[4,2,9,2,16,128]{5,4,3,2,1,0:T(8,128)(2,1)S(1)} async-done(((bf16[4,2,9,2,16,128]{5,4,3,2,1,0:T(8,128)(2,1)}), bf16[4,2,9,2,16,128]{5,4,3,2,1,0:T(8,128)(2,1)S(1)}, u32[]{:S(2)}, u32[]{:S(2)}) %all-to-all-start.1) | async-done | bytes 589856 | tf_op jit(solution)/shard_map/all_to_all | solution.py:217
  91.7 0.0 collective-permute-done.3.other_ref
  91.7 4.4 %shard_map.55 = bf16[4,512,128]{2,1,0:T(8,128)(2,1)} custom-call(bf16[4,2,9,2,16,128]{5,4,3,2,1,0:T(8,128)(2,1)S(1)} %all-to-all-done.1.cot_ref, bf16[8,4,6,16,384]{4,3,2,1,0:T(8,128)(2,1)S(1)} %bitcast.42, bf16[8,4,6,16,384]{4,3,2,1,0:T(8,128)(2,1)} %collective-permute-done.3.other_ref), custom_call_target="tpu_custom_call" | custom-call | tf_op jit(solution)/shard_map/pallas_call | solution.py:224
  96.2 4.1 %all-to-all-start.2 = ((bf16[4,512,128]{2,1,0:T(8,128)(2,1)}), bf16[4,512,128]{2,1,0:T(8,128)(2,1)}, u32[]{:S(2)}, u32[]{:S(2)}) async-start(bf16[4,512,128]{2,1,0:T(8,128)(2,1)} %shard_map.55), calls=%async_computation.2 | async-start | bytes 1048576 | tf_op jit(solution)/shard_map/all_to_all | solution.py:234
  100.3 0.2 maximum_bitcast_fusion
  100.5 0.2 copy.25
  100.7 0.8 all_gather_reshape.3
  101.5 17.4 %all_gather.9.lat_ref = bf16[4,240,512]{2,1,0:T(8,128)(2,1)S(1)} all-gather(bf16[1,240,512]{2,1,0:T(8,128)(2,1)} %all_gather_reshape.3), channel_id=1, replica_groups=mesh['ta'=8,'ha'=4,'wa'=8] {'ha'}, dimensions={0}, use_global_device_ids=true | all-gather | bytes 1228800 | tf_op jit(solution)/shard_map/all_gather | solution.py:213
  118.9 0.0 all-to-all-done.2.act_ref
  118.9 6.0 %shard_map.56.g_ref = bf16[8,4,16,128]{3,2,1,0:T(8,128)(2,1)S(1)} custom-call(bf16[4,240,512]{2,1,0:T(8,128)(2,1)S(1)} %all_gather.9.lat_ref, bf16[8,4,6,16,384]{4,3,2,1,0:T(8,128)(2,1)S(1)} %bitcast.43, bf16[8,4,6,16,384]{4,3,2,1,0:T(8,128)(2,1)} %collective-permute-done.3.other_ref, f32[1,128]{1,0:T(1,128)S(1)} %dynamic-slice_bitcast_fusion.bias_ref, ...), custom_call_target="tpu_custom_call" | custom-call | tf_op jit(solution)/shard_map/pallas_call | solution.py:237
  124.9 1.9 %collective-permute-start.4 = (bf16[8,4,8,128]{3,2,1,0:T(8,128)(2,1)S(1)}, bf16[8,4,8,128]{3,2,1,0:T(8,128)(2,1)S(1)}, u32[]{:S(2)}, u32[]{:S(2)}) collective-permute-start(bf16[8,4,8,128]{3,2,1,0:T(8,128)(2,1)S(1)} %slice.64), channel_id=1, source_target_pairs={{32,0},{64,32},{96,64},{128,96},{160,128},{192,160},{224,192},{33,... | collective-permute-start | bytes 196616 | tf_op jit(solution)/shard_map/ppermute | solution.py:172
  126.9 1.9 %collective-permute-done.4.later_ref = bf16[8,4,8,128]{3,2,1,0:T(8,128)(2,1)S(1)} collective-permute-done((bf16[8,4,8,128]{3,2,1,0:T(8,128)(2,1)S(1)}, bf16[8,4,8,128]{3,2,1,0:T(8,128)(2,1)S(1)}, u32[]{:S(2)}, u32[]{:S(2)}) %collective-permute-start.4) | collective-permute-done | bytes 65568 | tf_op jit(solution)/shard_map/ppermute | solution.py:172
  128.8 1.9 %collective-permute-start.6 = (bf16[4,24,128]{2,1,0:T(8,128)(2,1)S(1)}, bf16[4,24,128]{2,1,0:T(8,128)(2,1)S(1)}, u32[]{:S(2)}, u32[]{:S(2)}) collective-permute-start(bf16[4,24,128]{2,1,0:T(8,128)(2,1)S(1)} %pad_maximum_fusion.5), channel_id=1, source_target_pairs={{1,0},{2,1},{3,2},{4,3},{5,4},{6,5},{7,6},{9,8},{10,9},{11,10},{12... | collective-permute-start | bytes 73736 | tf_op jit(solution)/shard_map/ppermute | solution.py:172
  130.7 5.1 %collective-permute-start.5 = (bf16[4,24,128]{2,1,0:T(8,128)(2,1)S(1)}, bf16[4,24,128]{2,1,0:T(8,128)(2,1)S(1)}, u32[]{:S(2)}, u32[]{:S(2)}) collective-permute-start(bf16[4,24,128]{2,1,0:T(8,128)(2,1)S(1)} %pad_maximum_fusion.4), channel_id=1, source_target_pairs={{0,1},{1,2},{2,3},{3,4},{4,5},{5,6},{6,7},{8,9},{9,10},{10,11},{11... | collective-permute-start | bytes 73736 | tf_op jit(solution)/shard_map/ppermute | solution.py:172
  135.8 0.0 collective-permute-done.6.right_ref
  135.8 1.5 collective-permute-done.5.left_ref
  137.3 5.1 %shard_map.57 = bf16[4,8,16,512]{3,2,1,0:T(8,128)(2,1)S(1)} custom-call(bf16[8,4,16,128]{3,2,1,0:T(8,128)(2,1)S(1)} %shard_map.56.g_ref, bf16[8,4,8,128]{3,2,1,0:T(8,128)(2,1)S(1)} %collective-permute-done.4.later_ref, bf16[4,24,128]{2,1,0:T(8,128)(2,1)S(1)} %collective-permute-done.5.left_ref, bf16[4,24,128]{2,1,0:T(8,128)(2,1)S(1)} %collective-permute-done.6.right_ref, ...), custom_call_target="tpu_custom_call" | custom-call | tf_op jit(solution)/shard_map/pallas_call | solution.py:248
  142.4 12.6 %all_to_all.21 = bf16[4,8,16,512]{3,2,1,0:T(8,128)(2,1)S(1)} all-to-all(bf16[4,8,16,512]{3,2,1,0:T(8,128)(2,1)S(1)} %shard_map.57), channel_id=1, replica_groups=mesh['ta'=8,'ha'=4,'wa'=8] {'ha'}, dimensions={0} | all-to-all | bytes 1048576 | tf_op jit(solution)/shard_map/all_to_all | solution.py:254
  155.0 0.1 reduce_sum.12
  155.1 0.7 copy.35
  (29 shorter events, 0.2 us)
Async XLA Ops:
  6.5 76.8 %copy-start = (f32[512]{0:T(512)S(1)}, f32[512]{0:T(512)}, u32[]{:S(2)}) copy-start(f32[512]{0:T(512)} %param.7) | copy-start | bytes 6148
  6.5 1.9 %copy-start.4 = (bf16[3,3,16,512]{3,2,1,0:T(8,128)(2,1)S(1)}, bf16[3,3,16,512]{3,2,1,0:T(8,128)(2,1)}, u32[]{:S(2)}) copy-start(bf16[3,3,16,512]{3,2,1,0:T(8,128)(2,1)} %param.9) | copy-start | bytes 442372
  6.5 54.4 %all-gather.3.cloned.1.call-start = ((), (), s32[]{:S(2)}) async-start(), calls=%async_computation.4 | async-start | bytes 2654208 | tf_op jit(solution)/shard_map/all_gather | solution.py:189
  8.5 52.5 %copy-start.2 = (bf16[4,4,8,512]{3,2,1,0:T(8,128)(2,1)S(1)}, bf16[4,4,8,512]{3,2,1,0:T(8,128)(2,1)}, u32[]{:S(2)}) copy-start(bf16[4,4,8,512]{3,2,1,0:T(8,128)(2,1)} %param.5) | copy-start | bytes 393220
  8.5 54.9 %copy-start.3 = (bf16[4,8,16,512]{3,2,1,0:T(8,128)(2,1)S(1)}, bf16[4,8,16,512]{3,2,1,0:T(8,128)(2,1)}, u32[]{:S(2)}) copy-start(bf16[4,8,16,512]{3,2,1,0:T(8,128)(2,1)} %param.6) | copy-start | bytes 1572868
  61.0 30.8 %collective-permute-start.3 = (bf16[8,4,6,16,384]{4,3,2,1,0:T(8,128)(2,1)}, bf16[8,4,6,16,384]{4,3,2,1,0:T(8,128)(2,1)}, u32[]{:S(2)}, u32[]{:S(2)}) collective-permute-start(bf16[8,4,6,16,384]{4,3,2,1,0:T(8,128)(2,1)} %bitcast.41), channel_id=1, source_target_pairs={{0,32},{32,0},{64,96},{96,64},{128,160},{160,128},{192,224},{224,1... | collective-permute-start | bytes 7077896 | tf_op jit(solution)/shard_map/ppermute | solution.py:190
  61.0 5.6 %collective-permute-start = (bf16[2,4,8,512]{3,2,1,0:T(8,128)(2,1)S(1)}, bf16[2,4,8,512]{3,2,1,0:T(8,128)(2,1)S(1)}, u32[]{:S(2)}, u32[]{:S(2)}) collective-permute-start(bf16[2,4,8,512]{3,2,1,0:T(8,128)(2,1)S(1)} %slice.46), channel_id=1, source_target_pairs={{0,32},{32,64},{64,96},{96,128},{128,160},{160,192},{192,224},{1,3... | collective-permute-start | bytes 196616 | tf_op jit(solution)/shard_map/ppermute | solution.py:172
  66.9 6.1 %collective-permute-start.1 = (bf16[56,512]{1,0:T(8,128)(2,1)S(1)}, bf16[56,512]{1,0:T(8,128)(2,1)S(1)}, u32[]{:S(2)}, u32[]{:S(2)}) collective-permute-start(bf16[56,512]{1,0:T(8,128)(2,1)S(1)} %pad_maximum_fusion.1), channel_id=1, source_target_pairs={{0,1},{1,2},{2,3},{3,4},{4,5},{5,6},{6,7},{8,9},{9,10},{10,11},{11... | collective-permute-start | bytes 172040 | tf_op jit(solution)/shard_map/ppermute | solution.py:172
  69.9 7.3 %collective-permute-start.2 = (bf16[56,512]{1,0:T(8,128)(2,1)S(1)}, bf16[56,512]{1,0:T(8,128)(2,1)S(1)}, u32[]{:S(2)}, u32[]{:S(2)}) collective-permute-start(bf16[56,512]{1,0:T(8,128)(2,1)S(1)} %pad_maximum_fusion.2), channel_id=1, source_target_pairs={{1,0},{2,1},{3,2},{4,3},{5,4},{6,5},{7,6},{9,8},{10,9},{11,10},{12... | collective-permute-start | bytes 172040 | tf_op jit(solution)/shard_map/ppermute | solution.py:172
  78.0 13.8 %copy-start.1 = (bf16[32,6,16,384]{3,2,1,0:T(8,128)(2,1)S(1)}, bf16[32,6,16,384]{3,2,1,0:T(8,128)(2,1)}, u32[]{:S(2)}) copy-start(bf16[32,6,16,384]{3,2,1,0:T(8,128)(2,1)} %all-gather.3.cloned.1.call-done) | copy-start | bytes 7077892
  79.1 12.7 %all-to-all-start.1 = ((bf16[4,2,9,2,16,128]{5,4,3,2,1,0:T(8,128)(2,1)}), bf16[4,2,9,2,16,128]{5,4,3,2,1,0:T(8,128)(2,1)S(1)}, u32[]{:S(2)}, u32[]{:S(2)}) async-start(bf16[4,2,9,2,16,128]{5,4,3,2,1,0:T(8,128)(2,1)} %bitcast.12), calls=%async_computation.1 | async-start | bytes 1179648 | tf_op jit(solution)/shard_map/all_to_all | solution.py:217
  96.2 22.7 %all-to-all-start.2 = ((bf16[4,512,128]{2,1,0:T(8,128)(2,1)}), bf16[4,512,128]{2,1,0:T(8,128)(2,1)}, u32[]{:S(2)}, u32[]{:S(2)}) async-start(bf16[4,512,128]{2,1,0:T(8,128)(2,1)} %shard_map.55), calls=%async_computation.2 | async-start | bytes 1048576 | tf_op jit(solution)/shard_map/all_to_all | solution.py:234
  124.9 3.8 %collective-permute-start.4 = (bf16[8,4,8,128]{3,2,1,0:T(8,128)(2,1)S(1)}, bf16[8,4,8,128]{3,2,1,0:T(8,128)(2,1)S(1)}, u32[]{:S(2)}, u32[]{:S(2)}) collective-permute-start(bf16[8,4,8,128]{3,2,1,0:T(8,128)(2,1)S(1)} %slice.64), channel_id=1, source_target_pairs={{32,0},{64,32},{96,64},{128,96},{160,128},{192,160},{224,192},{33,... | collective-permute-start | bytes 196616 | tf_op jit(solution)/shard_map/ppermute | solution.py:172
  128.8 7.1 %collective-permute-start.6 = (bf16[4,24,128]{2,1,0:T(8,128)(2,1)S(1)}, bf16[4,24,128]{2,1,0:T(8,128)(2,1)S(1)}, u32[]{:S(2)}, u32[]{:S(2)}) collective-permute-start(bf16[4,24,128]{2,1,0:T(8,128)(2,1)S(1)} %pad_maximum_fusion.5), channel_id=1, source_target_pairs={{1,0},{2,1},{3,2},{4,3},{5,4},{6,5},{7,6},{9,8},{10,9},{11,10},{12... | collective-permute-start | bytes 73736 | tf_op jit(solution)/shard_map/ppermute | solution.py:172
  130.7 6.6 %collective-permute-start.5 = (bf16[4,24,128]{2,1,0:T(8,128)(2,1)S(1)}, bf16[4,24,128]{2,1,0:T(8,128)(2,1)S(1)}, u32[]{:S(2)}, u32[]{:S(2)}) collective-permute-start(bf16[4,24,128]{2,1,0:T(8,128)(2,1)S(1)} %pad_maximum_fusion.4), channel_id=1, source_target_pairs={{0,1},{1,2},{2,3},{3,4},{4,5},{5,6},{6,7},{8,9},{9,10},{10,11},{11... | collective-permute-start | bytes 73736 | tf_op jit(solution)/shard_map/ppermute | solution.py:172
Sparse Core Ops, SparseCore 0:
  20.3 40.6 all-gather.2

commit v2 on v1

--- a/solution.py
+++ b/solution.py
@@ -89,7 +89,7 @@
         out_ref[x] = total[:, x * LANES : (x + 1) * LANES].astype(BF16)
 
 
-def fwd_kernel(lat_ref, own_ref, other_ref, bias_ref, act_ref, out_ref, w_ref, win_ref, sem):
+def fwd_kernel(lat_ref, own_ref, other_ref, bias_ref, out_ref, w_ref, win_ref, sem):
     start, wait = weight_copies(own_ref, other_ref, 9, 0, w_ref, sem)
     start()
     n_ha = lat_ref.shape[0]
@@ -114,12 +114,15 @@
         + from_below(total[..., 2 * LANES :])
         + bias_ref[...].reshape(1, 1, 1, LANES)
     )
+    sig = 1.0 / (1.0 + jnp.exp(-pre))
+    out_ref[...] = sig * (1.0 + pre * (1.0 - sig))
+
+
+def gate_kernel(slope_ref, act_ref, out_ref):
     grad = act_ref[0].astype(F32)
-    for x in range(1, n_ha):
+    for x in range(1, act_ref.shape[0]):
         grad = grad + act_ref[x].astype(F32)
-    grad = grad.reshape(pre.shape)
-    sig = 1.0 / (1.0 + jnp.exp(-pre))
-    out_ref[...] = (grad * sig * (1.0 + pre * (1.0 - sig))).astype(BF16)
+    out_ref[...] = (grad.reshape(slope_ref.shape) * slope_ref[...]).astype(BF16)
 
 
 def bwd_kernel(g_ref, later_ref, left_ref, right_ref, own_ref, other_ref, out_ref, w_ref, win_ref, sem):
@@ -156,13 +159,14 @@
         out_ref[x] = total[:, x]
 
 
-def call(kernel, out_shape, specs, scratch):
+def call(kernel, out_shape, specs, scratch, cost=None):
     return pl.pallas_call(
         kernel,
         out_shape=out_shape,
         in_specs=specs,
         out_specs=pl.BlockSpec(memory_space=pltpu.VMEM),
         scratch_shapes=scratch,
+        cost_estimate=cost,
         compiler_params=pltpu.CompilerParams(vmem_limit_bytes=VMEM_LIMIT),
     )
 
@@ -187,7 +191,6 @@
     groups = lax.dynamic_slice_in_dim(groups, 6 * core, 6, axis=1)
     groups = lax.all_to_all(groups, "ha", 0, 0)
     w_own = lax.all_gather(groups, "wa", axis=0)
-    w_other = lax.ppermute(w_own, "ta", [(i, i ^ 1) for i in range(n_ta)])
 
     past = shifted(latent[frames - 2 :], "ta", 1)
     past = jnp.where(ta == 0, jnp.broadcast_to(latent[:1], past.shape), past)
@@ -215,6 +218,9 @@
     cot = cot.reshape(frames, rows, 2, cols + 1, 2, n_ha, LANES).transpose(5, 4, 3, 2, 0, 1, 6)
     cot = cot.reshape(n_ha, 2, cols + 1, 2, frames * rows, LANES)
     cot = lax.all_to_all(cot, "ha", 0, 0)
+
+    w_own, lat, cot = lax.optimization_barrier((w_own, lat, cot))
+    w_other = lax.ppermute(w_own, "ta", [(i, i ^ 1) for i in range(n_ta)])
 
     vmem, anywhere = pl.BlockSpec(memory_space=pltpu.VMEM), pl.BlockSpec(memory_space=pl.ANY)
     points = cols * n_ha * frames * rows
@@ -234,12 +240,16 @@
     act = lax.all_to_all(act, "ha", 0, 0)
 
     bias = lax.dynamic_slice_in_dim(conv_bias, ha * LANES, LANES).reshape(1, LANES)
+    slope = call(
+        fwd_kernel,
+        jax.ShapeDtypeStruct((cols, n_ha, frames * rows, LANES), F32),
+        [vmem, anywhere, anywhere, vmem],
+        [w_conv, pltpu.VMEM((3, cols + 2, n_ha, frames * rows, chans), BF16), sem],
+        pl.CostEstimate(flops=3 * 9 * 2 * points * LANES * chans, bytes_accessed=5 << 20, transcendentals=0),
+    )(lat, w_own, w_other, bias)
     grad = call(
-        fwd_kernel,
-        jax.ShapeDtypeStruct((cols, n_ha, frames * rows, LANES), BF16),
-        [vmem, anywhere, anywhere, vmem, vmem],
-        [w_conv, pltpu.VMEM((3, cols + 2, n_ha, frames * rows, chans), BF16), sem],
-    )(lat, w_own, w_other, bias, act)
+        gate_kernel, jax.ShapeDtypeStruct((cols, n_ha, frames * rows, LANES), BF16), [vmem, vmem], []
+    )(slope, act)
 
     later = shifted(grad[:, :, : 2 * rows], "ta", -1)
     g_left = shifted(jnp.concatenate([grad[cols - 1], later[cols - 1]], axis=1), "wa", 1)

time: 164 us -> 132 us (0.80)
  waiting for transfers between devices: 59.8 us -> 20.5 us
  local copies, waits for them, and re-layouts: 5.66 us -> 13.4 us
  blocking collectives: 41.2 us -> 43 us
  Pallas kernels: 15.5 us -> 13.8 us
    all_gather x1, waiting for transfers between devices: 40.8 us -> 0.27 us  [on_device(): w_own = lax.all_gather(groups, 'wa', axis=0)]
    all_to_all x1, waiting for transfers between devices: 8.3 us -> 0.01 us  [on_device(): cot = lax.all_to_all(cot, 'ha', 0, 0)]
    unnamed x12 -> x20, local copies, waits for them, and re-layouts: 0.04 us -> 7.63 us
    ppermute x1, waiting for transfers between devices: 0.01 us -> 4.74 us  [on_device(): w_other = lax.ppermute(w_own, 'ta', [(i, i ^ 1) for i in range(n_ta)])]
    ppermute x6, waiting for transfers between devices: 10.7 us -> 13.3 us  [shifted(): lax.ppermute(x, axis, [(i, i + step) for i in range(n) if 0 <= i + step <...]
    all_to_all x1, waiting for transfers between devices: 0.01 us -> 2.23 us  [on_device(): act = lax.all_to_all(act, 'ha', 0, 0)]
    all_gather x1, blocking collectives: 17.4 us -> 19.5 us  [on_device(): lat = lax.all_gather(lat, 'ha', axis=0)]
  transfers between devices with their start and end apart: 10 -> 10, of which waited for: 7 -> 8; matrix products, arithmetic and copies ran while one was open for 2% -> 2% of each run, Pallas kernels for 0% -> 3%
where the time goes in v2:
time: 132 us; the launch traced here: 131 us
  blocking collectives  43 us (33%)
  starting transfers between devices  25.7 us (19%)
  waiting for transfers between devices  20.5 us (16%)
  Pallas kernels  13.8 us (10%)
  between operations  13.7 us (10%)
  local copies, waits for them, and re-layouts  13.4 us (10%)
    all_gather x1, blocking collectives, on_device(): lat = lax.all_gather(lat, 'ha', axis=0)  19.5 us
    ppermute x6, starting transfers between devices, shifted(): lax.ppermute(x, axis, [(i, i + step) for i in range(n) if 0 <= i + step <...  18.3 us
    ppermute x6, waiting for transfers between devices, shifted(): lax.ppermute(x, axis, [(i, i + step) for i in range(n) if 0 <= i + step <...  13.3 us
    all_to_all x1, blocking collectives, on_device(): out = lax.all_to_all(out, 'ha', 0, 0)  12.3 us
    all_to_all x1, blocking collectives, on_device(): groups = lax.all_to_all(groups, 'ha', 0, 0)  11.2 us
    unnamed x20, local copies, waits for them, and re-layouts  7.63 us
    pallas_call x1, Pallas kernels, on_device(): call(bwd_kernel, jax.ShapeDtypeStruct((n_ha, cols, frames * rows, chans),...  5.06 us
    ppermute x1, waiting for transfers between devices, on_device(): w_other = lax.ppermute(w_own, 'ta', [(i, i ^ 1) for i in range(n_ta)])  4.74 us
  transfers between devices with their start and end apart: 10, of which 8 were waited for; matrix products, arithmetic and copies ran while one was open for 2% of the time, Pallas kernels for 3%

profile of v2, /device:TPU:104, one launch (start us, length us, event | category | flops | bytes accessed | tf_op | source)
XLA Modules:
  0.0 131.4 jit_solution(3767996818125563110)
XLA Ops:
  6.5 1.0 reshape.37
  7.5 0.1 copy.45
  7.6 0.1 reshape.38
  7.8 1.1 reshape.35
  8.9 0.4 copy.44
  9.3 0.4 reshape.36
  9.7 0.1 fusion
  9.8 11.2 %all_to_all.20 = bf16[4,6,16,384]{3,2,1,0:T(8,128)(2,1)} all-to-all(bf16[4,6,16,384]{3,2,1,0:T(8,128)(2,1)S(1)} %fusion), channel_id=1, replica_groups=mesh['ta'=8,'ha'=4,'wa'=8] {'ha'}, dimensions={0} | all-to-all | bytes 589824 | tf_op jit(solution)/shard_map/all_to_all | solution.py:192
  21.1 1.9 %collective-permute-start = (bf16[2,4,8,512]{3,2,1,0:T(8,128)(2,1)S(1)}, bf16[2,4,8,512]{3,2,1,0:T(8,128)(2,1)S(1)}, u32[]{:S(2)}, u32[]{:S(2)}) collective-permute-start(bf16[2,4,8,512]{3,2,1,0:T(8,128)(2,1)S(1)} %slice.46), channel_id=1, source_target_pairs={{0,32},{32,64},{64,96},{96,128},{128,160},{160,192},{192,224},{1,3... | collective-permute-start | bytes 196616 | tf_op jit(solution)/shard_map/ppermute | solution.py:176
  23.0 0.1 fusion.2
  23.2 3.5 %collective-permute-done = bf16[2,4,8,512]{3,2,1,0:T(8,128)(2,1)S(1)} collective-permute-done((bf16[2,4,8,512]{3,2,1,0:T(8,128)(2,1)S(1)}, bf16[2,4,8,512]{3,2,1,0:T(8,128)(2,1)S(1)}, u32[]{:S(2)}, u32[]{:S(2)}) %collective-permute-start) | collective-permute-done | bytes 65568 | tf_op jit(solution)/shard_map/ppermute | solution.py:176
  26.7 0.3 maximum_reduce_fusion
  27.0 2.0 %collective-permute-start.2 = (bf16[56,512]{1,0:T(8,128)(2,1)S(1)}, bf16[56,512]{1,0:T(8,128)(2,1)S(1)}, u32[]{:S(2)}, u32[]{:S(2)}) collective-permute-start(bf16[56,512]{1,0:T(8,128)(2,1)S(1)} %pad_maximum_fusion.2), channel_id=1, source_target_pairs={{1,0},{2,1},{3,2},{4,3},{5,4},{6,5},{7,6},{9,8},{10,9},{11,10},{12... | collective-permute-start | bytes 172040 | tf_op jit(solution)/shard_map/ppermute | solution.py:176
  29.0 5.0 %collective-permute-start.1 = (bf16[56,512]{1,0:T(8,128)(2,1)S(1)}, bf16[56,512]{1,0:T(8,128)(2,1)S(1)}, u32[]{:S(2)}, u32[]{:S(2)}) collective-permute-start(bf16[56,512]{1,0:T(8,128)(2,1)S(1)} %pad_maximum_fusion.1), channel_id=1, source_target_pairs={{0,1},{1,2},{2,3},{3,4},{4,5},{5,6},{6,7},{8,9},{9,10},{10,11},{11... | collective-permute-start | bytes 172040 | tf_op jit(solution)/shard_map/ppermute | solution.py:176
  34.1 0.2 collective-permute-done.2
  34.3 0.1 copy.29
  34.4 2.6 %collective-permute-done.1 = bf16[56,512]{1,0:T(8,128)(2,1)S(1)} collective-permute-done((bf16[56,512]{1,0:T(8,128)(2,1)S(1)}, bf16[56,512]{1,0:T(8,128)(2,1)S(1)}, u32[]{:S(2)}, u32[]{:S(2)}) %collective-permute-start.1) | collective-permute-done | bytes 57376 | tf_op jit(solution)/shard_map/ppermute | solution.py:176
  37.0 0.1 copy.28
  37.1 0.4 pad_maximum_fusion
  37.5 0.3 reshape.49
  37.8 1.1 copy.31
  38.8 3.5 %all-to-all-start.1 = ((bf16[4,2,9,2,16,128]{5,4,3,2,1,0:T(8,128)(2,1)}), bf16[4,2,9,2,16,128]{5,4,3,2,1,0:T(8,128)(2,1)S(1)}, u32[]{:S(2)}, u32[]{:S(2)}) async-start(bf16[4,2,9,2,16,128]{5,4,3,2,1,0:T(8,128)(2,1)} %bitcast.11), calls=%async_computation.1 | async-start | bytes 1179648 | tf_op jit(solution)/shard_map/all_to_all | solution.py:220
  42.3 0.2 maximum_bitcast_fusion
  42.5 0.2 copy.27
  42.7 0.1 all_gather_reshape.3
  42.8 19.5 %all_gather.11.lat_ref = bf16[4,240,512]{2,1,0:T(8,128)(2,1)} all-gather(bf16[1,240,512]{2,1,0:T(8,128)(2,1)S(1)} %all_gather_reshape.3), channel_id=1, replica_groups=mesh['ta'=8,'ha'=4,'wa'=8] {'ha'}, dimensions={0}, use_global_device_ids=true | all-gather | bytes 1228800 | tf_op jit(solution)/shard_map/all_gather | solution.py:216
  62.3 0.3 all-gather.3.cloned.1.call-done
  62.6 4.7 %collective-permute-done.3.other_ref = bf16[8,4,6,16,384]{4,3,2,1,0:T(8,128)(2,1)S(1)} collective-permute-done((bf16[8,4,6,16,384]{4,3,2,1,0:T(8,128)(2,1)}, bf16[8,4,6,16,384]{4,3,2,1,0:T(8,128)(2,1)S(1)}, u32[]{:S(2)}, u32[]{:S(2)}) %collective-permute-start.3) | collective-permute-done | bytes 2359328 | tf_op jit(solution)/shard_map/ppermute | solution.py:223
  67.4 1.7 %copy-done.1 = bf16[32,6,16,384]{3,2,1,0:T(8,128)(2,1)S(1)} copy-done((bf16[32,6,16,384]{3,2,1,0:T(8,128)(2,1)S(1)}, bf16[32,6,16,384]{3,2,1,0:T(8,128)(2,1)}, u32[]{:S(2)}) %copy-start.1) | copy-done | bytes 2359320
  69.0 4.1 %shard_map.56 = bf16[4,512,128]{2,1,0:T(8,128)(2,1)} custom-call(bf16[4,2,9,2,16,128]{5,4,3,2,1,0:T(8,128)(2,1)S(1)} %all-to-all-done.1.cot_ref, bf16[8,4,6,16,384]{4,3,2,1,0:T(8,128)(2,1)S(1)} %bitcast.42, bf16[8,4,6,16,384]{4,3,2,1,0:T(8,128)(2,1)S(1)} %collective-permute-done.3.other_ref), custom_call_target="tpu_custom_call" | custom-call | tf_op jit(solution)/shard_map/pallas_call | solution.py:230
  73.1 1.4 %copy-done.3 = bf16[8,4,6,16,384]{4,3,2,1,0:T(8,128)(2,1)} copy-done((bf16[8,4,6,16,384]{4,3,2,1,0:T(8,128)(2,1)}, bf16[8,4,6,16,384]{4,3,2,1,0:T(8,128)(2,1)S(1)}, u32[]{:S(2)}) %copy-start.3) | copy-done | bytes 2359320
  74.5 3.9 %all-to-all-start.2 = ((bf16[4,512,128]{2,1,0:T(8,128)(2,1)}), bf16[4,512,128]{2,1,0:T(8,128)(2,1)S(1)}, u32[]{:S(2)}, u32[]{:S(2)}) async-start(bf16[4,512,128]{2,1,0:T(8,128)(2,1)} %shard_map.56), calls=%async_computation.2 | async-start | bytes 1048576 | tf_op jit(solution)/shard_map/all_to_all | solution.py:240
  78.4 0.1 dynamic-slice_bitcast_fusion.bias_ref
  78.5 1.7 %copy-done.4 = bf16[8,4,6,16,384]{4,3,2,1,0:T(8,128)(2,1)S(1)} copy-done((bf16[8,4,6,16,384]{4,3,2,1,0:T(8,128)(2,1)S(1)}, bf16[8,4,6,16,384]{4,3,2,1,0:T(8,128)(2,1)}, u32[]{:S(2)}) %copy-start.4) | copy-done | bytes 2359320
  80.1 1.2 copy-done.6
  81.3 4.6 %shard_map.55.slope_ref = f32[8,4,16,128]{3,2,1,0:T(8,128)S(1)} custom-call(bf16[4,240,512]{2,1,0:T(8,128)(2,1)S(1)} %copy-done.6, bf16[8,4,6,16,384]{4,3,2,1,0:T(8,128)(2,1)S(1)} %bitcast.43, bf16[8,4,6,16,384]{4,3,2,1,0:T(8,128)(2,1)S(1)} %copy-done.4, f32[1,128]{1,0:T(1,128)S(1)} %dynamic-slice_bitcast_fusion.bias_ref), custom_call_target="tpu_custom_call" | custom-call | flops 1811939328 | bytes 5242880 | tf_op jit(solution)/shard_map/pallas_call | solution.py:243
  85.9 2.2 %all-to-all-done.2.act_ref = bf16[4,512,128]{2,1,0:T(8,128)(2,1)S(1)} async-done(((bf16[4,512,128]{2,1,0:T(8,128)(2,1)}), bf16[4,512,128]{2,1,0:T(8,128)(2,1)S(1)}, u32[]{:S(2)}, u32[]{:S(2)}) %all-to-all-start.2) | async-done | bytes 524320 | tf_op jit(solution)/shard_map/all_to_all | solution.py:240
  88.2 0.1 shard_map.57.g_ref
  88.3 1.9 %collective-permute-start.4 = (bf16[8,4,8,128]{3,2,1,0:T(8,128)(2,1)S(1)}, bf16[8,4,8,128]{3,2,1,0:T(8,128)(2,1)S(1)}, u32[]{:S(2)}, u32[]{:S(2)}) collective-permute-start(bf16[8,4,8,128]{3,2,1,0:T(8,128)(2,1)S(1)} %slice.64), channel_id=1, source_target_pairs={{32,0},{64,32},{96,64},{128,96},{160,128},{192,160},{224,192},{33,... | collective-permute-start | bytes 196616 | tf_op jit(solution)/shard_map/ppermute | solution.py:176
  90.2 1.9 %collective-permute-done.4.later_ref = bf16[8,4,8,128]{3,2,1,0:T(8,128)(2,1)S(1)} collective-permute-done((bf16[8,4,8,128]{3,2,1,0:T(8,128)(2,1)S(1)}, bf16[8,4,8,128]{3,2,1,0:T(8,128)(2,1)S(1)}, u32[]{:S(2)}, u32[]{:S(2)}) %collective-permute-start.4) | collective-permute-done | bytes 65568 | tf_op jit(solution)/shard_map/ppermute | solution.py:176
  92.1 5.5 %collective-permute-start.5 = (bf16[4,24,128]{2,1,0:T(8,128)(2,1)S(1)}, bf16[4,24,128]{2,1,0:T(8,128)(2,1)S(1)}, u32[]{:S(2)}, u32[]{:S(2)}) collective-permute-start(bf16[4,24,128]{2,1,0:T(8,128)(2,1)S(1)} %pad_maximum_fusion.4), channel_id=1, source_target_pairs={{0,1},{1,2},{2,3},{3,4},{4,5},{5,6},{6,7},{8,9},{9,10},{10,11},{11... | collective-permute-start | bytes 73736 | tf_op jit(solution)/shard_map/ppermute | solution.py:176
  97.6 1.9 %collective-permute-start.6 = (bf16[4,24,128]{2,1,0:T(8,128)(2,1)S(1)}, bf16[4,24,128]{2,1,0:T(8,128)(2,1)S(1)}, u32[]{:S(2)}, u32[]{:S(2)}) collective-permute-start(bf16[4,24,128]{2,1,0:T(8,128)(2,1)S(1)} %pad_maximum_fusion.5), channel_id=1, source_target_pairs={{1,0},{2,1},{3,2},{4,3},{5,4},{6,5},{7,6},{9,8},{10,9},{11,10},{12... | collective-permute-start | bytes 73736 | tf_op jit(solution)/shard_map/ppermute | solution.py:176
  99.6 5.1 %collective-permute-done.6.right_ref = bf16[4,24,128]{2,1,0:T(8,128)(2,1)S(1)} collective-permute-done((bf16[4,24,128]{2,1,0:T(8,128)(2,1)S(1)}, bf16[4,24,128]{2,1,0:T(8,128)(2,1)S(1)}, u32[]{:S(2)}, u32[]{:S(2)}) %collective-permute-start.6) | collective-permute-done | bytes 24608 | tf_op jit(solution)/shard_map/ppermute | solution.py:176
  104.7 1.7 %copy-done.5 = bf16[8,4,6,16,384]{4,3,2,1,0:T(8,128)(2,1)S(1)} copy-done((bf16[8,4,6,16,384]{4,3,2,1,0:T(8,128)(2,1)S(1)}, bf16[8,4,6,16,384]{4,3,2,1,0:T(8,128)(2,1)}, u32[]{:S(2)}) %copy-start.5) | copy-done | bytes 2359320
  106.4 5.1 %shard_map.58 = bf16[4,8,16,512]{3,2,1,0:T(8,128)(2,1)S(1)} custom-call(bf16[8,4,16,128]{3,2,1,0:T(8,128)(2,1)S(1)} %shard_map.57.g_ref, bf16[8,4,8,128]{3,2,1,0:T(8,128)(2,1)S(1)} %collective-permute-done.4.later_ref, bf16[4,24,128]{2,1,0:T(8,128)(2,1)S(1)} %collective-permute-done.5.left_ref, bf16[4,24,128]{2,1,0:T(8,128)(2,1)S(1)} %collective-permute-done.6.right_ref, ...), custom_call_target="tpu_custom_call" | custom-call | tf_op jit(solution)/shard_map/pallas_call | solution.py:258
  111.4 12.3 %all_to_all.21 = bf16[4,8,16,512]{3,2,1,0:T(8,128)(2,1)S(1)} all-to-all(bf16[4,8,16,512]{3,2,1,0:T(8,128)(2,1)S(1)} %shard_map.58), channel_id=1, replica_groups=mesh['ta'=8,'ha'=4,'wa'=8] {'ha'}, dimensions={0} | all-to-all | bytes 1048576 | tf_op jit(solution)/shard_map/all_to_all | solution.py:264
  123.7 0.1 reduce_sum.12
  123.8 0.7 copy.35
  (38 shorter events, 0.2 us)
Async XLA Ops:
  6.5 71.9 %copy-start = (f32[512]{0:T(512)S(1)}, f32[512]{0:T(512)}, u32[]{:S(2)}) copy-start(f32[512]{0:T(512)} %param.7) | copy-start | bytes 6148
  6.5 56.1 %all-gather.3.cloned.1.call-start = ((), (), s32[]{:S(2)}) async-start(), calls=%async_computation.4 | async-start | bytes 2654208 | tf_op jit(solution)/shard_map/all_gather | solution.py:193
  9.3 11.8 %copy-start.7 = (bf16[4,4,8,512]{3,2,1,0:T(8,128)(2,1)S(1)}, bf16[4,4,8,512]{3,2,1,0:T(8,128)(2,1)}, u32[]{:S(2)}) copy-start(bf16[4,4,8,512]{3,2,1,0:T(8,128)(2,1)} %param.5) | copy-start | bytes 393220
  9.3 13.7 %copy-start.8 = (bf16[4,8,16,512]{3,2,1,0:T(8,128)(2,1)S(1)}, bf16[4,8,16,512]{3,2,1,0:T(8,128)(2,1)}, u32[]{:S(2)}) copy-start(bf16[4,8,16,512]{3,2,1,0:T(8,128)(2,1)} %param.6) | copy-start | bytes 1572868
  21.1 5.6 %collective-permute-start = (bf16[2,4,8,512]{3,2,1,0:T(8,128)(2,1)S(1)}, bf16[2,4,8,512]{3,2,1,0:T(8,128)(2,1)S(1)}, u32[]{:S(2)}, u32[]{:S(2)}) collective-permute-start(bf16[2,4,8,512]{3,2,1,0:T(8,128)(2,1)S(1)} %slice.46), channel_id=1, source_target_pairs={{0,32},{32,64},{64,96},{96,128},{128,160},{160,192},{192,224},{1,3... | collective-permute-start | bytes 196616 | tf_op jit(solution)/shard_map/ppermute | solution.py:176
  27.0 7.3 %collective-permute-start.2 = (bf16[56,512]{1,0:T(8,128)(2,1)S(1)}, bf16[56,512]{1,0:T(8,128)(2,1)S(1)}, u32[]{:S(2)}, u32[]{:S(2)}) collective-permute-start(bf16[56,512]{1,0:T(8,128)(2,1)S(1)} %pad_maximum_fusion.2), channel_id=1, source_target_pairs={{1,0},{2,1},{3,2},{4,3},{5,4},{6,5},{7,6},{9,8},{10,9},{11,10},{12... | collective-permute-start | bytes 172040 | tf_op jit(solution)/shard_map/ppermute | solution.py:176
  29.0 7.9 %collective-permute-start.1 = (bf16[56,512]{1,0:T(8,128)(2,1)S(1)}, bf16[56,512]{1,0:T(8,128)(2,1)S(1)}, u32[]{:S(2)}, u32[]{:S(2)}) collective-permute-start(bf16[56,512]{1,0:T(8,128)(2,1)S(1)} %pad_maximum_fusion.1), channel_id=1, source_target_pairs={{0,1},{1,2},{2,3},{3,4},{4,5},{5,6},{6,7},{8,9},{9,10},{10,11},{11... | collective-permute-start | bytes 172040 | tf_op jit(solution)/shard_map/ppermute | solution.py:176
  38.8 23.5 %all-to-all-start.1 = ((bf16[4,2,9,2,16,128]{5,4,3,2,1,0:T(8,128)(2,1)}), bf16[4,2,9,2,16,128]{5,4,3,2,1,0:T(8,128)(2,1)S(1)}, u32[]{:S(2)}, u32[]{:S(2)}) async-start(bf16[4,2,9,2,16,128]{5,4,3,2,1,0:T(8,128)(2,1)} %bitcast.11), calls=%async_computation.1 | async-start | bytes 1179648 | tf_op jit(solution)/shard_map/all_to_all | solution.py:220
  62.6 4.7 %collective-permute-start.3 = (bf16[8,4,6,16,384]{4,3,2,1,0:T(8,128)(2,1)}, bf16[8,4,6,16,384]{4,3,2,1,0:T(8,128)(2,1)S(1)}, u32[]{:S(2)}, u32[]{:S(2)}) collective-permute-start(bf16[8,4,6,16,384]{4,3,2,1,0:T(8,128)(2,1)} %bitcast.41), channel_id=1, source_target_pairs={{0,32},{32,0},{64,96},{96,64},{128,160},{160,128},{192,224},{224,1... | collective-permute-start | bytes 7077896 | tf_op jit(solution)/shard_map/ppermute | solution.py:223
  67.4 1.7 %copy-start.1 = (bf16[32,6,16,384]{3,2,1,0:T(8,128)(2,1)S(1)}, bf16[32,6,16,384]{3,2,1,0:T(8,128)(2,1)}, u32[]{:S(2)}) copy-start(bf16[32,6,16,384]{3,2,1,0:T(8,128)(2,1)} %all-gather.3.cloned.1.call-done) | copy-start | bytes 7077892
  69.0 9.4 %copy-start.2 = (bf16[32,6,16,384]{3,2,1,0:T(8,128)(2,1)S(1)}, bf16[32,6,16,384]{3,2,1,0:T(8,128)(2,1)}, u32[]{:S(2)}) copy-start(bf16[32,6,16,384]{3,2,1,0:T(8,128)(2,1)} %all-gather.3.cloned.1.call-done) | copy-start | bytes 7077892
  73.1 1.4 %copy-start.3 = (bf16[8,4,6,16,384]{4,3,2,1,0:T(8,128)(2,1)}, bf16[8,4,6,16,384]{4,3,2,1,0:T(8,128)(2,1)S(1)}, u32[]{:S(2)}) copy-start(bf16[8,4,6,16,384]{4,3,2,1,0:T(8,128)(2,1)S(1)} %collective-permute-done.3.other_ref) | copy-start | bytes 7077892
  74.5 13.6 %all-to-all-start.2 = ((bf16[4,512,128]{2,1,0:T(8,128)(2,1)}), bf16[4,512,128]{2,1,0:T(8,128)(2,1)S(1)}, u32[]{:S(2)}, u32[]{:S(2)}) async-start(bf16[4,512,128]{2,1,0:T(8,128)(2,1)} %shard_map.56), calls=%async_computation.2 | async-start | bytes 1048576 | tf_op jit(solution)/shard_map/all_to_all | solution.py:240
  78.5 1.7 %copy-start.4 = (bf16[8,4,6,16,384]{4,3,2,1,0:T(8,128)(2,1)S(1)}, bf16[8,4,6,16,384]{4,3,2,1,0:T(8,128)(2,1)}, u32[]{:S(2)}) copy-start(bf16[8,4,6,16,384]{4,3,2,1,0:T(8,128)(2,1)} %copy-done.3) | copy-start | bytes 7077892
  80.1 1.2 copy-start.6
  88.3 3.8 %collective-permute-start.4 = (bf16[8,4,8,128]{3,2,1,0:T(8,128)(2,1)S(1)}, bf16[8,4,8,128]{3,2,1,0:T(8,128)(2,1)S(1)}, u32[]{:S(2)}, u32[]{:S(2)}) collective-permute-start(bf16[8,4,8,128]{3,2,1,0:T(8,128)(2,1)S(1)} %slice.64), channel_id=1, source_target_pairs={{32,0},{64,32},{96,64},{128,96},{160,128},{192,160},{224,192},{33,... | collective-permute-start | bytes 196616 | tf_op jit(solution)/shard_map/ppermute | solution.py:176
  92.1 7.5 %collective-permute-start.5 = (bf16[4,24,128]{2,1,0:T(8,128)(2,1)S(1)}, bf16[4,24,128]{2,1,0:T(8,128)(2,1)S(1)}, u32[]{:S(2)}, u32[]{:S(2)}) collective-permute-start(bf16[4,24,128]{2,1,0:T(8,128)(2,1)S(1)} %pad_maximum_fusion.4), channel_id=1, source_target_pairs={{0,1},{1,2},{2,3},{3,4},{4,5},{5,6},{6,7},{8,9},{9,10},{10,11},{11... | collective-permute-start | bytes 73736 | tf_op jit(solution)/shard_map/ppermute | solution.py:176
  97.6 7.1 %collective-permute-start.6 = (bf16[4,24,128]{2,1,0:T(8,128)(2,1)S(1)}, bf16[4,24,128]{2,1,0:T(8,128)(2,1)S(1)}, u32[]{:S(2)}, u32[]{:S(2)}) collective-permute-start(bf16[4,24,128]{2,1,0:T(8,128)(2,1)S(1)} %pad_maximum_fusion.5), channel_id=1, source_target_pairs={{1,0},{2,1},{3,2},{4,3},{5,4},{6,5},{7,6},{9,8},{10,9},{11,10},{12... | collective-permute-start | bytes 73736 | tf_op jit(solution)/shard_map/ppermute | solution.py:176
  104.7 1.7 %copy-start.5 = (bf16[8,4,6,16,384]{4,3,2,1,0:T(8,128)(2,1)S(1)}, bf16[8,4,6,16,384]{4,3,2,1,0:T(8,128)(2,1)}, u32[]{:S(2)}) copy-start(bf16[8,4,6,16,384]{4,3,2,1,0:T(8,128)(2,1)} %copy-done.3) | copy-start | bytes 7077892
Sparse Core Ops, SparseCore 0:
  21.2 41.3 all-gather.2

commit v3 on v2

v3 whole, which is shorter than its diff:
```python
import functools

import jax
import jax.numpy as jnp
from jax import lax
from jax.experimental import pallas as pl
from jax.experimental.pallas import tpu as pltpu
from jax.sharding import PartitionSpec as P

F32, BF16 = jnp.float32, jnp.bfloat16
LANES = 128
VMEM_LIMIT = 24 * 1024 * 1024


def roll_rows(x, shift):
    return pltpu.roll(x, shift, x.ndim - 2)


def row_in_block(shape):
    return lax.broadcasted_iota(jnp.int32, shape, len(shape) - 2) % 4


def from_above(x):
    prev = jnp.concatenate([jnp.zeros_like(x[:, :1]), x[:, :-1]], axis=1)
    n = x.shape[2]
    return jnp.where(row_in_block(x.shape) == 0, roll_rows(prev, n - 3), roll_rows(x, 1))


def from_below(x):
    later = jnp.concatenate([x[:, 1:], jnp.zeros_like(x[:, :1])], axis=1)
    n = x.shape[2]
    return jnp.where(row_in_block(x.shape) == 3, roll_rows(later, 3), roll_rows(x, n - 1))


def weight_copies(whole, refs, lo, first, groups, to, w_ref, sem, base=0):
    core = lax.rem(lax.axis_index("ta"), 2)
    wa = lax.axis_index("wa")
    way = 1 - 2 * core
    rounds = len(refs) // 2 + 1
    n_wa, (n_ha, _, shard, _) = 2 * rounds, whole[0].shape
    half = n_ha // 2
    copies = []

    def copy(ref, at, begin, ha, place):
        row = pl.multiple_of((ha * n_wa + place) * shard, shard)
        copies.append(
            pltpu.make_async_copy(
                ref.at[at, pl.ds(begin, groups)],
                w_ref.at[pl.ds(to, groups), pl.ds(row, shard)],
                sem.at[base + len(copies)],
            )
        )

    def behind(r):
        return lax.rem(wa + n_wa + way * r, n_wa)

    for at in range(n_ha):
        copy(whole[0], at, first, at, wa)
        copy(whole[1], at, first, at, behind(1))
        copy(whole[2], at, first, at, behind(-1))
        for r in range(2, rounds):
            copy(refs[r - 2], at, first - lo, at, behind(r))
            copy(refs[rounds - 1 + r - 2], at, first - lo, at, behind(-r))
    for at in range(half):
        copy(refs[rounds - 2], at, first - lo, core * half + at, behind(rounds))
        copy(refs[-1], at, first - lo, (1 - core) * half + at, behind(rounds))
    for one in copies:
        one.start()

    def wait():
        for one in copies:
            one.wait()

    return wait


def pack_kernel(conv_ref, up_ref, out_ref):
    for x in range(out_ref.shape[0]):
        lanes = slice(x * LANES, (x + 1) * LANES)
        for a in range(3):
            to = slice(a * LANES, (a + 1) * LANES)
            for b in range(3):
                for k in range(3):
                    out_ref[x, 3 * k + b, :, to] = conv_ref[k, a, b, :, lanes]
                out_ref[x, 9 + b, :, to] = up_ref[a, b, :, lanes]


def slab_kernel(lat_ref, past_ref, cot_ref, left_ref, right_ref, out_ref):
    n_ha, chans = out_ref.shape[0], out_ref.shape[2]
    rows, split = lat_ref.shape[1], lat_ref.shape[0] * lat_ref.shape[1]
    lat = lat_ref[...].astype(F32).reshape(split, lat_ref.shape[2], chans)
    lat = jnp.concatenate(
        [left_ref[:split].astype(F32)[None], jnp.swapaxes(lat, 0, 1), right_ref[:split].astype(F32)[None]], axis=0
    )
    first = jnp.concatenate([lat[:, :rows]] * 2, axis=1)
    past = jnp.where(lax.axis_index("ta") == 0, first, past_ref[...].astype(F32))
    lat = jnp.concatenate([past, lat], axis=1).reshape(-1, chans).astype(BF16)
    for x in range(n_ha):
        out_ref[x, : lat.shape[0]] = lat
    cot = cot_ref[...].astype(F32)
    frames, fine, cols, _ = cot.shape
    points = frames * fine // 2
    cot = cot.reshape(points, 2, cols, chans)
    for odd_row in range(2):
        part = jnp.swapaxes(cot[:, odd_row], 0, 1).astype(BF16)
        edge = slice(split + odd_row * points, split + (odd_row + 1) * points)
        columns = [left_ref[edge], *[part[w] for w in range(cols)], right_ref[edge]]
        for f, column in enumerate(columns):
            rows = pl.ds(lat.shape[0] + f // 2 * points, points)
            to = (f % 2 * 2 + odd_row) * LANES
            for x in range(n_ha):
                out_ref[x, rows, to : to + LANES] = column[:, x * LANES : (x + 1) * LANES]


def up_kernel(slab_ref, *refs):
    *blocks, out_ref, w_ref, rows_ref, sem = refs
    wait = weight_copies(blocks[:3], blocks[3:], 6, 9, 3, 0, w_ref, sem)
    n_ha = slab_ref.shape[0]
    for par in range(2):
        cot = jnp.stack([slab_ref[x, 240:384, :] for x in range(n_ha)], axis=0)
        cot = cot[:, :, 2 * par * LANES : 2 * (par + 1) * LANES].astype(F32)
        cot = jnp.stack([cot[x].reshape(9, 16, 2 * LANES) for x in range(n_ha)], axis=1)
        even, odd = cot[..., :LANES], cot[..., LANES:]
        rows_ref[par, :, :, :, 0:LANES] = odd + from_below(even)
        rows_ref[par, :, :, :, LANES : 2 * LANES] = even + odd
        rows_ref[par, :, :, :, 2 * LANES : 3 * LANES] = even + from_above(odd)
    wait()
    total = None
    for b in range(3):
        box = None
        for e in (1 - b, 2 - b):
            par, off = (e + 1) % 2, (e + 1) // 2
            part = rows_ref[par, off : off + 8]
            box = part if box is None else box + part
        box = box.reshape(-1, 3 * LANES)
        high = box.astype(BF16)
        low = (box - high.astype(F32)).astype(BF16)
        for piece in (high, low):
            term = lax.dot_general(
                piece, w_ref[b], (((1,), (1,)), ((), ())), preferred_element_type=F32
            )
            total = term if total is None else total + term
    for x in range(n_ha):
        out_ref[x] = total[:, x * LANES : (x + 1) * LANES].astype(BF16)


def fwd_kernel(slab_ref, bias_ref, *refs):
    *blocks, out_ref, w_hbm, win_ref, w_ref, sem, out_sem = refs
    whole, early, late = blocks[:3], blocks[3 : 3 + (len(blocks) - 3) // 2], blocks[3 + (len(blocks) - 3) // 2 :]
    early_wait = weight_copies(whole, early, 6, 6, 3, 6, w_ref, sem)
    late_wait = weight_copies(whole, late, 0, 0, 6, 0, w_ref, sem, sem.shape[0] // 2)
    n_ha = slab_ref.shape[0]
    for x in range(n_ha):
        for pair in range(5):
            two = slab_ref[x, pair * 48 : pair * 48 + 48, :].astype(F32)
            for one in range(2):
                for k in range(3):
                    lo = one * 24 + 4 * k
                    win_ref[k, 2 * pair + one, x] = two[lo : lo + 16].astype(BF16)
    early_wait()
    total = None
    for k in (2, 0, 1):
        if k == 0:
            late_wait()
            keep = pltpu.make_async_copy(w_ref, w_hbm, out_sem)
            keep.start()
        for b in range(3):
            window = win_ref[k, b : b + 8].reshape(-1, win_ref.shape[-1])
            term = jnp.dot(window, w_ref[3 * k + b], preferred_element_type=F32)
            total = term if total is None else total + term
    total = total.reshape(8, n_ha, 16, 3 * LANES)
    pre = (
        from_above(total[..., :LANES])
        + total[..., LANES : 2 * LANES]
        + from_below(total[..., 2 * LANES :])
        + bias_ref[...].reshape(1, 1, 1, LANES)
    )
    sig = 1.0 / (1.0 + jnp.exp(-pre))
    out_ref[...] = sig * (1.0 + pre * (1.0 - sig))
    keep.wait()


def gate_kernel(slope_ref, act_ref, out_ref, head_ref, first_ref, last_ref):
    grad = act_ref[0].astype(F32)
    for x in range(1, act_ref.shape[0]):
        grad = grad + act_ref[x].astype(F32)
    grad = (grad.reshape(slope_ref.shape) * slope_ref[...]).astype(BF16)
    out_ref[...] = grad
    first_ref[...] = grad[0]
    last_ref[...] = grad[-1]
    head_ref[...] = grad[:, :, : head_ref.shape[2]]


def bwd_kernel(g_ref, later_ref, left_ref, right_ref, w_hbm, out_ref, win_ref, w_ref, sem):
    fetch = [
        pltpu.make_async_copy(w_hbm.at[pl.ds(3 * k, 3)], w_ref.at[pl.ds(3 * k, 3)], sem.at[k]) for k in range(3)
    ]
    for copy in fetch:
        copy.start()
    n_ha = g_ref.shape[1]
    at_start = (lax.axis_index("ta") == 0).astype(F32)
    grad = jnp.concatenate([g_ref[...].astype(F32), later_ref[...].astype(F32)], axis=2)
    grad = jnp.concatenate(
        [left_ref[...].astype(F32)[None], grad, right_ref[...].astype(F32)[None]], axis=0
    )
    zero, one, two = grad[:, :, 0:4], grad[:, :, 4:8], grad[:, :, 8:12]
    windows = [
        grad[:, :, 0:16],
        jnp.concatenate([one + at_start * zero, grad[:, :, 8:20]], axis=2),
        jnp.concatenate([two + at_start * (zero + one), grad[:, :, 12:24]], axis=2),
    ]
    for shift in range(3):
        x = windows[shift]
        win_ref[shift, :, :, :, 0:LANES] = from_below(x).astype(BF16)
        win_ref[shift, :, :, :, LANES : 2 * LANES] = x.astype(BF16)
        win_ref[shift, :, :, :, 2 * LANES : 3 * LANES] = from_above(x).astype(BF16)
    total = None
    for k in range(3):
        fetch[k].wait()
        for b in range(3):
            window = win_ref[2 - k, 2 - b : 10 - b].reshape(-1, 3 * LANES)
            term = lax.dot_general(
                window, w_ref[3 * k + b], (((1,), (1,)), ((), ())), preferred_element_type=F32
            )
            total = term if total is None else total + term
    total = total.astype(BF16).reshape(8, n_ha, 16, -1)
    for x in range(n_ha):
        out_ref[x] = total[:, x]


def call(kernel, out_shape, specs, scratch, cost=None, outs=None):
    return pl.pallas_call(
        kernel,
        out_shape=out_shape,
        in_specs=specs,
        out_specs=outs or jax.tree.map(lambda _: pl.BlockSpec(memory_space=pltpu.VMEM), out_shape),
        scratch_shapes=scratch,
        cost_estimate=cost,
        compiler_params=pltpu.CompilerParams(vmem_limit_bytes=VMEM_LIMIT),
    )


def in_hbm(x):
    return pltpu.with_memory_space_constraint(x, pltpu.HBM)


def shifted(x, axis, step):
    n = lax.axis_size(axis)
    return lax.ppermute(x, axis, [(i, i + step) for i in range(n) if 0 <= i + step < n])


def on_device(latent, cotangent, conv_bias, conv_weight, up_weight):
    frames, rows, cols, chans = latent.shape
    n_ta, n_ha, n_wa = (lax.axis_size(a) for a in ("ta", "ha", "wa"))
    ta, ha = lax.axis_index("ta"), lax.axis_index("ha")
    shard = conv_weight.shape[3]
    core = lax.rem(ta, 2)

    vmem, anywhere = pl.BlockSpec(memory_space=pltpu.VMEM), pl.BlockSpec(memory_space=pl.ANY)
    groups = call(
        pack_kernel,
        jax.ShapeDtypeStruct((n_ha, 12, shard, 3 * LANES), BF16),
        [vmem, vmem],
        [],
    )(conv_weight, up_weight)
    def edge(col_l, col_c):
        fine = cotangent[:, :, col_c].reshape(frames * rows, 2, chans).transpose(1, 0, 2)
        return jnp.concatenate([latent[:, :, col_l].reshape(-1, chans), fine.reshape(-1, chans)], axis=0)

    left = shifted(edge(cols - 1, 2 * cols - 1), "wa", 1)
    right = shifted(edge(0, 0), "wa", -1)
    tail = slice((frames - 2) * rows, frames * rows)
    middle = latent[frames - 2 :].transpose(2, 0, 1, 3).reshape(cols, 2 * rows, chans)
    past = shifted(jnp.concatenate([left[None, tail], middle, right[None, tail]], axis=0), "ta", 1)
    groups, past = lax.optimization_barrier((lax.all_to_all(groups, "ha", 0, 0), past))
    length = (cols + 2) * (frames + 2) * rows + (cols + 1) * frames * rows
    slab = call(
        slab_kernel, jax.ShapeDtypeStruct((n_ha, length, chans), BF16), [vmem] * 5, []
    )(latent, past, cotangent, left, right)

    swap = [(i, i ^ 1) for i in range(n_ta)]
    around = [
        (t * n_wa + (w + 1 - 2 * (t % 2)) % n_wa, t * n_wa + w) for t in range(n_ta) for w in range(n_wa)
    ]
    spans = [(6, 12), (0, 6)]
    block, slab = lax.optimization_barrier((lax.ppermute(groups, ("ta", "wa"), around), slab))
    swapped = lax.ppermute(block, "ta", swap)
    mine, others = [], []
    for lo, hi in spans:
        mine.append([block[:, lo:hi]])
        others.append([])
    for r in range(2, n_wa // 2 + 1):
        for q in range(2):
            part = mine[q][-1]
            if r == n_wa // 2:
                part = lax.dynamic_slice_in_dim(part, core * (n_ha // 2), n_ha // 2, axis=0)
            mine[q].append(lax.ppermute(part, ("ta", "wa"), around))
            others[q].append(lax.ppermute(mine[q][-1], "ta", swap))
    whole = [groups, block, swapped]
    slab = lax.all_to_all(slab, "ha", 0, 0)
    early, late = mine[0][1:] + others[0], mine[1][1:] + others[1]

    points = cols * n_ha * frames * rows
    copies = (n_wa - 1) * n_ha + n_ha
    dma = pltpu.SemaphoreType.DMA
    act = call(
        up_kernel,
        jax.ShapeDtypeStruct((n_ha, points, LANES), BF16),
        [vmem] + [anywhere] * len(whole + early),
        [
            pltpu.VMEM((3, chans, 3 * LANES), BF16),
            pltpu.VMEM((2, cols + 1, n_ha, frames * rows, 3 * LANES), F32),
            dma((copies,)),
        ],
    )(slab, *[in_hbm(x) for x in whole + early])
    act = lax.all_to_all(act, "ha", 0, 0)

    bias = lax.dynamic_slice_in_dim(conv_bias, ha * LANES, LANES).reshape(1, LANES)
    hbm = pl.BlockSpec(memory_space=pltpu.HBM)
    w_conv = (9, chans, 3 * LANES)
    slope, w_conv = call(
        fwd_kernel,
        (jax.ShapeDtypeStruct((cols, n_ha, frames * rows, LANES), F32), pltpu.HBM(w_conv, BF16)),
        [vmem, vmem] + [anywhere] * len(whole + early + late),
        [
            pltpu.VMEM((3, cols + 2, n_ha, frames * rows, chans), BF16),
            pltpu.VMEM(w_conv, BF16),
            dma((2 * copies,)),
            dma,
        ],
        pl.CostEstimate(flops=3 * 9 * 2 * points * LANES * chans, bytes_accessed=5 << 20, transcendentals=0),
        (vmem, hbm),
    )(slab, bias, *[in_hbm(x) for x in whole + early + late])
    w_conv = in_hbm(w_conv)
    deep, high = frames * rows, 2 * rows
    shapes = [(cols, n_ha, deep), (cols, n_ha, high), (n_ha, deep), (n_ha, deep)]
    grad, head, first, last = call(
        gate_kernel, [jax.ShapeDtypeStruct((*sh, LANES), BF16) for sh in shapes], [vmem, vmem], []
    )(slope, act)

    later = shifted(head, "ta", -1)
    g_left = shifted(jnp.concatenate([last, later[cols - 1]], axis=1), "wa", 1)
    g_right = shifted(jnp.concatenate([first, later[0]], axis=1), "wa", -1)

    out = call(
        bwd_kernel,
        jax.ShapeDtypeStruct((n_ha, cols, frames * rows, chans), BF16),
        [vmem, vmem, vmem, vmem, hbm],
        [pltpu.VMEM((3, cols + 2, n_ha, frames * rows, 3 * LANES), BF16), pltpu.VMEM(w_conv.shape, BF16), dma((3,))],
    )(grad, later, g_left, g_right, w_conv)
    out = lax.all_to_all(out, "ha", 0, 0)
    out = out.astype(F32).sum(axis=0).reshape(cols, frames, rows, chans)
    return out.transpose(1, 2, 0, 3).astype(BF16)


def solution(mesh):
    in_specs = (
        P("ta", "ha", "wa", None),
        P("ta", "ha", "wa", None),
        P(),
        P(None, None, None, ("ha", "wa"), None),
        P(None, None, ("ha", "wa"), None),
    )
    return jax.shard_map(
        on_device, mesh=mesh, in_specs=in_specs, out_specs=P("ta", "ha", "wa", None), check_vma=False
    )
```

time: 132 us -> 116 us (0.88)
  blocking collectives: 43 us -> 13.3 us
  waiting for transfers between devices: 20.5 us -> 48 us
  between operations: 13.7 us -> 0.36 us
  local copies, waits for them, and re-layouts: 13.4 us -> 5.86 us
  starting transfers between devices: 25.7 us -> 31.9 us
  Pallas kernels: 13.8 us -> 15.4 us
    ppermute x1 -> x14, waiting for transfers between devices: 4.74 us -> 33.1 us  [the longest x6 22 us: on_device(): mine[q].append(lax.ppermute(part, ('ta', 'wa'), around))]
    all_gather x1 -> x0, blocking collectives: 19.5 us -> none  [on_device(): lat = lax.all_gather(lat, 'ha', axis=0)]
    all_to_all x1 -> x0, blocking collectives: 11.2 us -> none  [on_device(): groups = lax.all_to_all(groups, 'ha', 0, 0)]
    all_to_all x1 -> x2, starting transfers between devices: 3.48 us -> 9.09 us  [the longest x1 4.8 us: on_device(): slab = lax.all_to_all(slab, 'ha', 0, 0)]
    unnamed x20 -> x30, local copies, waits for them, and re-layouts: 7.63 us -> 3.44 us
    reshape x13 -> x1, local copies, waits for them, and re-layouts: 3.52 us -> 0.02 us  [on_device(): latent[frames - 2:].transpose(2, 0, 1, 3).reshape(cols, 2 * rows, chans)]
    pallas_call x3 -> x5, Pallas kernels: 8.76 us -> 11.3 us  [the longest x1 4.57 us: on_device(): call(fwd_kernel, (jax.ShapeDtypeStruct((cols, n_ha, frames * rows, LANES)...]
    ppermute x6, starting transfers between devices: 18.3 us -> 16.7 us  [shifted(): lax.ppermute(x, axis, [(i, i + step) for i in range(n) if 0 <= i + step <...]
  transfers between devices with their start and end apart: 10 -> 23, of which waited for: 8 -> 12; matrix products, arithmetic and copies ran while one was open for 2% -> 1% of each run, Pallas kernels for 3% -> 9%
where the time goes in v3:
time: 116 us; the launch traced here: 115 us
  waiting for transfers between devices  48 us (41%)
  starting transfers between devices  31.9 us (28%)
  Pallas kernels  15.4 us (13%)
  blocking collectives  13.3 us (11%)
  local copies, waits for them, and re-layouts  5.86 us (5%)
    ppermute x6, waiting for transfers between devices, on_device(): mine[q].append(lax.ppermute(part, ('ta', 'wa'), around))  22 us
    ppermute x6, starting transfers between devices, shifted(): lax.ppermute(x, axis, [(i, i + step) for i in range(n) if 0 <= i + step <...  16.7 us
    all_to_all x1, blocking collectives, on_device(): out = lax.all_to_all(out, 'ha', 0, 0)  13.3 us
    ppermute x6, waiting for transfers between devices, shifted(): lax.ppermute(x, axis, [(i, i + step) for i in range(n) if 0 <= i + step <...  11.7 us
    ppermute x1, waiting for transfers between devices, on_device(): lax.ppermute(groups, ('ta', 'wa'), around)  9.84 us
    all_to_all x1, starting transfers between devices, on_device(): act = lax.all_to_all(act, 'ha', 0, 0)  4.81 us
    all_to_all x1, starting transfers between devices, on_device(): slab = lax.all_to_all(slab, 'ha', 0, 0)  4.8 us
    pallas_call x1, Pallas kernels, on_device(): call(fwd_kernel, (jax.ShapeDtypeStruct((cols, n_ha, frames * rows, LANES)...  4.57 us
  transfers between devices with their start and end apart: 23, of which 12 were waited for; matrix products, arithmetic and copies ran while one was open for 1% of the time, Pallas kernels for 9%

profile of v3, /device:TPU:104, one launch (start us, length us, event | category | flops | bytes accessed | tf_op | source)
XLA Modules:
  0.0 115.0 jit_solution(7865956829633883572)
XLA Ops:
  0.0 1.1 copy-done.3
  1.1 0.9 copy-done.4
  2.0 0.9 shard_map.55
  2.9 4.3 %all-to-all-start = ((bf16[4,12,16,384]{3,2,1,0:T(8,128)(2,1)}), bf16[4,12,16,384]{3,2,1,0:T(8,128)(2,1)S(1)}, u32[]{:S(2)}, u32[]{:S(2)}) async-start(bf16[4,12,16,384]{3,2,1,0:T(8,128)(2,1)} %shard_map.55), calls=%async_computation | async-start | bytes 1179648 | tf_op jit(solution)/shard_map/all_to_all | solution.py:275
  7.2 0.3 slice_reduce_fusion.1
  7.6 0.2 slice_reduce_fusion.3
  7.8 2.0 %collective-permute-start.1 = (bf16[48,512]{1,0:T(8,128)(2,1)S(1)}, bf16[48,512]{1,0:T(8,128)(2,1)S(1)}, u32[]{:S(2)}, u32[]{:S(2)}) collective-permute-start(bf16[48,512]{1,0:T(8,128)(2,1)S(1)} %pad_maximum_fusion.2), channel_id=1, source_target_pairs={{1,0},{2,1},{3,2},{4,3},{5,4},{6,5},{7,6},{9,8},{10,9},{11,10},{12... | collective-permute-start | bytes 147464 | tf_op jit(solution)/shard_map/ppermute | solution.py:249
  9.9 5.0 %collective-permute-start = (bf16[48,512]{1,0:T(8,128)(2,1)S(1)}, bf16[48,512]{1,0:T(8,128)(2,1)S(1)}, u32[]{:S(2)}, u32[]{:S(2)}) collective-permute-start(bf16[48,512]{1,0:T(8,128)(2,1)S(1)} %pad_maximum_fusion.1), channel_id=1, source_target_pairs={{0,1},{1,2},{2,3},{3,4},{4,5},{5,6},{6,7},{8,9},{9,10},{10,11},{11... | collective-permute-start | bytes 147464 | tf_op jit(solution)/shard_map/ppermute | solution.py:249
  14.9 0.0 collective-permute-done.1.right_ref
  15.0 1.7 %collective-permute-done.left_ref = bf16[48,512]{1,0:T(8,128)(2,1)S(1)} collective-permute-done((bf16[48,512]{1,0:T(8,128)(2,1)S(1)}, bf16[48,512]{1,0:T(8,128)(2,1)S(1)}, u32[]{:S(2)}, u32[]{:S(2)}) %collective-permute-start) | collective-permute-done | bytes 49184 | tf_op jit(solution)/shard_map/ppermute | solution.py:249
  16.6 1.9 %collective-permute-start.2 = (bf16[10,8,512]{2,1,0:T(8,128)(2,1)S(1)}, bf16[10,8,512]{2,1,0:T(8,128)(2,1)S(1)}, u32[]{:S(2)}, u32[]{:S(2)}) collective-permute-start(bf16[10,8,512]{2,1,0:T(8,128)(2,1)S(1)} %pad_maximum_fusion), channel_id=1, source_target_pairs={{0,32},{32,64},{64,96},{96,128},{128,160},{160,192},{192,224},{1,3... | collective-permute-start | bytes 245768 | tf_op jit(solution)/shard_map/ppermute | solution.py:249
  18.6 3.8 %collective-permute-done.2.past_ref = bf16[10,8,512]{2,1,0:T(8,128)(2,1)S(1)} collective-permute-done((bf16[10,8,512]{2,1,0:T(8,128)(2,1)S(1)}, bf16[10,8,512]{2,1,0:T(8,128)(2,1)S(1)}, u32[]{:S(2)}, u32[]{:S(2)}) %collective-permute-start.2) | collective-permute-done | bytes 81952 | tf_op jit(solution)/shard_map/ppermute | solution.py:249
  22.4 1.6 %shard_map.56 = bf16[4,384,512]{2,1,0:T(8,128)(2,1)} custom-call(bf16[4,4,8,512]{3,2,1,0:T(8,128)(2,1)S(1)} %copy-done.2, bf16[10,8,512]{2,1,0:T(8,128)(2,1)S(1)} %collective-permute-done.2.past_ref, bf16[4,8,16,512]{3,2,1,0:T(8,128)(2,1)S(1)} %copy-done.1, bf16[48,512]{1,0:T(8,128)(2,1)S(1)} %collective-permute-done.left_ref, ...), custom_call_target="tpu_custom_call" | custom-call | tf_op jit(solution)/shard_map/pallas_call | solution.py:277
  24.0 9.8 %collective-permute-done.3.refs_1_ = bf16[4,12,16,384]{3,2,1,0:T(8,128)(2,1)S(1)} collective-permute-done((bf16[4,12,16,384]{3,2,1,0:T(8,128)(2,1)S(1)}, bf16[4,12,16,384]{3,2,1,0:T(8,128)(2,1)S(1)}, u32[]{:S(2)}, u32[]{:S(2)}) %collective-permute-start.3) | collective-permute-done | bytes 589856 | tf_op jit(solution)/shard_map/ppermute | solution.py:286
  33.8 4.8 %all-to-all-start.1 = ((bf16[4,384,512]{2,1,0:T(8,128)(2,1)}), bf16[4,384,512]{2,1,0:T(8,128)(2,1)S(1)}, u32[]{:S(2)}, u32[]{:S(2)}) async-start(bf16[4,384,512]{2,1,0:T(8,128)(2,1)} %shard_map.56), calls=%async_computation.1 | async-start | bytes 3145728 | tf_op jit(solution)/shard_map/all_to_all | solution.py:300
  38.6 0.1 fusion
  38.7 0.1 collective-permute-start.5
  38.8 0.1 collective-permute-start.11
  38.9 7.9 %collective-permute-done.5.refs_3_ = bf16[4,6,16,384]{3,2,1,0:T(8,128)(2,1)} collective-permute-done((bf16[4,6,16,384]{3,2,1,0:T(8,128)(2,1)S(1)}, bf16[4,6,16,384]{3,2,1,0:T(8,128)(2,1)}, u32[]{:S(2)}, u32[]{:S(2)}) %collective-permute-start.5) | collective-permute-done | bytes 294944 | tf_op jit(solution)/shard_map/ppermute | solution.py:297
  46.8 3.1 %collective-permute-done.11.refs_9_ = bf16[4,6,16,384]{3,2,1,0:T(8,128)(2,1)} collective-permute-done((bf16[4,6,16,384]{3,2,1,0:T(8,128)(2,1)S(1)}, bf16[4,6,16,384]{3,2,1,0:T(8,128)(2,1)}, u32[]{:S(2)}, u32[]{:S(2)}) %collective-permute-start.11) | collective-permute-done | bytes 294944 | tf_op jit(solution)/shard_map/ppermute | solution.py:297
  50.0 0.3 collective-permute-start.8
  50.3 4.7 %collective-permute-done.6.refs_4_ = bf16[4,6,16,384]{3,2,1,0:T(8,128)(2,1)S(1)} collective-permute-done((bf16[4,6,16,384]{3,2,1,0:T(8,128)(2,1)}, bf16[4,6,16,384]{3,2,1,0:T(8,128)(2,1)S(1)}, u32[]{:S(2)}, u32[]{:S(2)}) %collective-permute-start.6) | collective-permute-done | bytes 294944 | tf_op jit(solution)/shard_map/ppermute | solution.py:297
  55.0 0.1 collective-permute-start.7
  55.1 0.1 collective-permute-start.9
  55.2 3.1 %collective-permute-done.12.refs_10_ = bf16[4,6,16,384]{3,2,1,0:T(8,128)(2,1)} collective-permute-done((bf16[4,6,16,384]{3,2,1,0:T(8,128)(2,1)}, bf16[4,6,16,384]{3,2,1,0:T(8,128)(2,1)}, u32[]{:S(2)}, u32[]{:S(2)}) %collective-permute-start.12) | collective-permute-done | bytes 294944 | tf_op jit(solution)/shard_map/ppermute | solution.py:297
  58.2 3.2 %collective-permute-done.7.refs_5_ = bf16[2,6,16,384]{3,2,1,0:T(8,128)(2,1)S(1)} collective-permute-done((bf16[2,6,16,384]{3,2,1,0:T(8,128)(2,1)S(1)}, bf16[2,6,16,384]{3,2,1,0:T(8,128)(2,1)S(1)}, u32[]{:S(2)}, u32[]{:S(2)}) %collective-permute-start.7) | collective-permute-done | bytes 147488 | tf_op jit(solution)/shard_map/ppermute | solution.py:297
  61.4 1.0 constant_dynamic-slice_fusion
  62.4 0.5 collective-permute-start.15
  63.0 0.0 collective-permute-start.13
  63.0 0.8 copy-done.10
  63.8 4.2 %shard_map.58 = bf16[4,512,128]{2,1,0:T(8,128)(2,1)} custom-call(bf16[4,384,512]{2,1,0:T(8,128)(2,1)S(1)} %all-to-all-done.1.slab_ref, bf16[4,12,16,384]{3,2,1,0:T(8,128)(2,1)} %copy-done.5, bf16[4,12,16,384]{3,2,1,0:T(8,128)(2,1)} %copy-done.6, bf16[4,12,16,384]{3,2,1,0:T(8,128)(2,1)} %copy-done.8, bf16[4,6,16,384]{3,2,1,0:T(8,128)(2,1)} %collective-permute-done.5.refs_3_, ...), custom_call_target="tpu_custom_call" | custom-call | tf_op jit(solution)/shard_map/pallas_call | solution.py:306
  67.9 4.8 %all-to-all-start.2 = ((bf16[4,512,128]{2,1,0:T(8,128)(2,1)}), bf16[4,512,128]{2,1,0:T(8,128)(2,1)S(1)}, u32[]{:S(2)}, u32[]{:S(2)}) async-start(bf16[4,512,128]{2,1,0:T(8,128)(2,1)} %shard_map.58), calls=%async_computation.2 | async-start | bytes 1048576 | tf_op jit(solution)/shard_map/all_to_all | solution.py:316
  72.8 0.1 collective-permute-start.16
  72.9 0.1 dynamic-slice_bitcast_fusion.bias_ref
  73.0 1.3 %collective-permute-done.16.refs_14_ = bf16[2,6,16,384]{3,2,1,0:T(8,128)(2,1)S(1)} collective-permute-done((bf16[2,6,16,384]{3,2,1,0:T(8,128)(2,1)S(1)}, bf16[2,6,16,384]{3,2,1,0:T(8,128)(2,1)S(1)}, u32[]{:S(2)}, u32[]{:S(2)}) %collective-permute-start.16) | collective-permute-done | bytes 147488 | tf_op jit(solution)/shard_map/ppermute | solution.py:298
  74.2 0.7 copy-done.14
  74.9 4.6 %shard_map.57 = (f32[8,4,16,128]{3,2,1,0:T(8,128)S(1)}, bf16[9,512,384]{2,1,0:T(8,128)(2,1)}) custom-call(bf16[4,384,512]{2,1,0:T(8,128)(2,1)S(1)} %all-to-all-done.1.slab_ref, f32[1,128]{1,0:T(1,128)S(1)} %dynamic-slice_bitcast_fusion.bias_ref, bf16[4,12,16,384]{3,2,1,0:T(8,128)(2,1)} %copy-done.5, bf16[4,12,16,384]{3,2,1,0:T(8,128)(2,1)} %copy-done.6, ...), custom_call_target="tpu_custom_call" | custom-call | flops 1811939328 | bytes 5242880 | tf_op jit(solution)/shard_map/pallas_call | solution.py:321
  79.5 3.2 %all-to-all-done.2.act_ref = bf16[4,512,128]{2,1,0:T(8,128)(2,1)S(1)} async-done(((bf16[4,512,128]{2,1,0:T(8,128)(2,1)}), bf16[4,512,128]{2,1,0:T(8,128)(2,1)S(1)}, u32[]{:S(2)}, u32[]{:S(2)}) %all-to-all-start.2) | async-done | bytes 524320 | tf_op jit(solution)/shard_map/all_to_all | solution.py:316
  82.7 0.1 shard_map.59
  82.7 1.9 %collective-permute-start.17 = (bf16[8,4,8,128]{3,2,1,0:T(8,128)(2,1)S(1)}, bf16[8,4,8,128]{3,2,1,0:T(8,128)(2,1)S(1)}, u32[]{:S(2)}, u32[]{:S(2)}) collective-permute-start(bf16[8,4,8,128]{3,2,1,0:T(8,128)(2,1)S(1)} %get-tuple-element.21), channel_id=1, source_target_pairs={{32,0},{64,32},{96,64},{128,96},{160,128},{192,160},{224,192},{33,... | collective-permute-start | bytes 196616 | tf_op jit(solution)/shard_map/ppermute | solution.py:249
  84.7 1.9 %collective-permute-done.17.later_ref = bf16[8,4,8,128]{3,2,1,0:T(8,128)(2,1)S(1)} collective-permute-done((bf16[8,4,8,128]{3,2,1,0:T(8,128)(2,1)S(1)}, bf16[8,4,8,128]{3,2,1,0:T(8,128)(2,1)S(1)}, u32[]{:S(2)}, u32[]{:S(2)}) %collective-permute-start.17) | collective-permute-done | bytes 65568 | tf_op jit(solution)/shard_map/ppermute | solution.py:249
  86.6 3.3 %collective-permute-start.18 = (bf16[4,24,128]{2,1,0:T(8,128)(2,1)S(1)}, bf16[4,24,128]{2,1,0:T(8,128)(2,1)S(1)}, u32[]{:S(2)}, u32[]{:S(2)}) collective-permute-start(bf16[4,24,128]{2,1,0:T(8,128)(2,1)S(1)} %pad_maximum_fusion.3), channel_id=1, source_target_pairs={{0,1},{1,2},{2,3},{3,4},{4,5},{5,6},{6,7},{8,9},{9,10},{10,11},{11... | collective-permute-start | bytes 73736 | tf_op jit(solution)/shard_map/ppermute | solution.py:249
  89.8 2.6 %collective-permute-start.19 = (bf16[4,24,128]{2,1,0:T(8,128)(2,1)S(1)}, bf16[4,24,128]{2,1,0:T(8,128)(2,1)S(1)}, u32[]{:S(2)}, u32[]{:S(2)}) collective-permute-start(bf16[4,24,128]{2,1,0:T(8,128)(2,1)S(1)} %pad_maximum_fusion.4), channel_id=1, source_target_pairs={{1,0},{2,1},{3,2},{4,3},{5,4},{6,5},{7,6},{9,8},{10,9},{11,10},{12... | collective-permute-start | bytes 73736 | tf_op jit(solution)/shard_map/ppermute | solution.py:249
  92.4 4.4 %collective-permute-done.19.right_ref = bf16[4,24,128]{2,1,0:T(8,128)(2,1)S(1)} collective-permute-done((bf16[4,24,128]{2,1,0:T(8,128)(2,1)S(1)}, bf16[4,24,128]{2,1,0:T(8,128)(2,1)S(1)}, u32[]{:S(2)}, u32[]{:S(2)}) %collective-permute-start.19) | collective-permute-done | bytes 24608 | tf_op jit(solution)/shard_map/ppermute | solution.py:249
  96.8 4.1 %shard_map.60 = bf16[4,8,16,512]{3,2,1,0:T(8,128)(2,1)S(1)} custom-call(bf16[8,4,16,128]{3,2,1,0:T(8,128)(2,1)S(1)} %get-tuple-element.20.g_ref, bf16[8,4,8,128]{3,2,1,0:T(8,128)(2,1)S(1)} %collective-permute-done.17.later_ref, bf16[4,24,128]{2,1,0:T(8,128)(2,1)S(1)} %collective-permute-done.18.left_ref, ...), custom_call_target="tpu_custom_call" | custom-call | tf_op jit(solution)/shard_map/pallas_call | solution.py:345
  100.9 13.3 %all_to_all.20 = bf16[4,8,16,512]{3,2,1,0:T(8,128)(2,1)S(1)} all-to-all(bf16[4,8,16,512]{3,2,1,0:T(8,128)(2,1)S(1)} %shard_map.60), channel_id=1, replica_groups=mesh['ta'=8,'ha'=4,'wa'=8] {'ha'}, dimensions={0} | all-to-all | bytes 1048576 | tf_op jit(solution)/shard_map/all_to_all | solution.py:351
  114.2 0.1 reduce_sum.12
  114.2 0.7 copy.17
  (60 shorter events, 0.3 us)
Async XLA Ops:
  0.0 72.9 %copy-start = (f32[512]{0:T(512)S(1)}, f32[512]{0:T(512)}, u32[]{:S(2)}) copy-start(f32[512]{0:T(512)} %param.7) | copy-start | bytes 6148
  0.0 7.2 %copy-start.1 = (bf16[4,8,16,512]{3,2,1,0:T(8,128)(2,1)S(1)}, bf16[4,8,16,512]{3,2,1,0:T(8,128)(2,1)}, u32[]{:S(2)}) copy-start(bf16[4,8,16,512]{3,2,1,0:T(8,128)(2,1)} %cot_ref.1) | copy-start | bytes 1572868
  0.0 7.6 %copy-start.2 = (bf16[4,4,8,512]{3,2,1,0:T(8,128)(2,1)S(1)}, bf16[4,4,8,512]{3,2,1,0:T(8,128)(2,1)}, u32[]{:S(2)}) copy-start(bf16[4,4,8,512]{3,2,1,0:T(8,128)(2,1)} %lat_ref.1) | copy-start | bytes 393220
  0.0 14.9 %slice-start = ((bf16[4,4,8,512]{3,2,1,0:T(8,128)(2,1)}), bf16[2,4,8,512]{3,2,1,0:T(8,128)(2,1)S(1)}, s32[]{:S(2)}) async-start(bf16[4,4,8,512]{3,2,1,0:T(8,128)(2,1)} %lat_ref.1), calls=%async_computation.4 | async-start | bytes 131072 | tf_op jit(solution)/shard_map/slice | solution.py:273
  0.0 1.1 copy-start.3
  1.1 0.9 copy-start.4
  2.9 19.5 %all-to-all-start = ((bf16[4,12,16,384]{3,2,1,0:T(8,128)(2,1)}), bf16[4,12,16,384]{3,2,1,0:T(8,128)(2,1)S(1)}, u32[]{:S(2)}, u32[]{:S(2)}) async-start(bf16[4,12,16,384]{3,2,1,0:T(8,128)(2,1)} %shard_map.55), calls=%async_computation | async-start | bytes 1179648 | tf_op jit(solution)/shard_map/all_to_all | solution.py:275
  7.8 7.2 %collective-permute-start.1 = (bf16[48,512]{1,0:T(8,128)(2,1)S(1)}, bf16[48,512]{1,0:T(8,128)(2,1)S(1)}, u32[]{:S(2)}, u32[]{:S(2)}) collective-permute-start(bf16[48,512]{1,0:T(8,128)(2,1)S(1)} %pad_maximum_fusion.2), channel_id=1, source_target_pairs={{1,0},{2,1},{3,2},{4,3},{5,4},{6,5},{7,6},{9,8},{10,9},{11,10},{12... | collective-permute-start | bytes 147464 | tf_op jit(solution)/shard_map/ppermute | solution.py:249
  9.9 6.8 %collective-permute-start = (bf16[48,512]{1,0:T(8,128)(2,1)S(1)}, bf16[48,512]{1,0:T(8,128)(2,1)S(1)}, u32[]{:S(2)}, u32[]{:S(2)}) collective-permute-start(bf16[48,512]{1,0:T(8,128)(2,1)S(1)} %pad_maximum_fusion.1), channel_id=1, source_target_pairs={{0,1},{1,2},{2,3},{3,4},{4,5},{5,6},{6,7},{8,9},{9,10},{10,11},{11... | collective-permute-start | bytes 147464 | tf_op jit(solution)/shard_map/ppermute | solution.py:249
  16.6 5.8 %collective-permute-start.2 = (bf16[10,8,512]{2,1,0:T(8,128)(2,1)S(1)}, bf16[10,8,512]{2,1,0:T(8,128)(2,1)S(1)}, u32[]{:S(2)}, u32[]{:S(2)}) collective-permute-start(bf16[10,8,512]{2,1,0:T(8,128)(2,1)S(1)} %pad_maximum_fusion), channel_id=1, source_target_pairs={{0,32},{32,64},{64,96},{96,128},{128,160},{160,192},{192,224},{1,3... | collective-permute-start | bytes 245768 | tf_op jit(solution)/shard_map/ppermute | solution.py:249
  22.4 11.4 %copy-start.5 = (bf16[4,12,16,384]{3,2,1,0:T(8,128)(2,1)}, bf16[4,12,16,384]{3,2,1,0:T(8,128)(2,1)S(1)}, u32[]{:S(2)}) copy-start(bf16[4,12,16,384]{3,2,1,0:T(8,128)(2,1)S(1)} %all-to-all-done.refs_0_) | copy-start | bytes 1769476
  22.4 11.4 %collective-permute-start.3 = (bf16[4,12,16,384]{3,2,1,0:T(8,128)(2,1)S(1)}, bf16[4,12,16,384]{3,2,1,0:T(8,128)(2,1)S(1)}, u32[]{:S(2)}, u32[]{:S(2)}) collective-permute-start(bf16[4,12,16,384]{3,2,1,0:T(8,128)(2,1)S(1)} %all-to-all-done.refs_0_), channel_id=1, source_target_pairs={{1,0},{2,1},{3,2},{4,3},{5,4},{6,5},{7,6},{0,7},{39,32},{32,33},{3... | collective-permute-start | bytes 1769480 | tf_op jit(solution)/shard_map/ppermute | solution.py:286
  33.8 13.0 %copy-start.6 = (bf16[4,12,16,384]{3,2,1,0:T(8,128)(2,1)}, bf16[4,12,16,384]{3,2,1,0:T(8,128)(2,1)S(1)}, u32[]{:S(2)}) copy-start(bf16[4,12,16,384]{3,2,1,0:T(8,128)(2,1)S(1)} %collective-permute-done.3.refs_1_) | copy-start | bytes 1769476
  33.8 29.9 %all-to-all-start.1 = ((bf16[4,384,512]{2,1,0:T(8,128)(2,1)}), bf16[4,384,512]{2,1,0:T(8,128)(2,1)S(1)}, u32[]{:S(2)}, u32[]{:S(2)}) async-start(bf16[4,384,512]{2,1,0:T(8,128)(2,1)} %shard_map.56), calls=%async_computation.1 | async-start | bytes 3145728 | tf_op jit(solution)/shard_map/all_to_all | solution.py:300
  38.7 8.1 %collective-permute-start.5 = (bf16[4,6,16,384]{3,2,1,0:T(8,128)(2,1)S(1)}, bf16[4,6,16,384]{3,2,1,0:T(8,128)(2,1)}, u32[]{:S(2)}, u32[]{:S(2)}) collective-permute-start(bf16[4,6,16,384]{3,2,1,0:T(8,128)(2,1)S(1)} %get-tuple-element.30), channel_id=1, source_target_pairs={{1,0},{2,1},{3,2},{4,3},{5,4},{6,5},{7,6},{0,7},{39,32},{32,33},{3... | collective-permute-start | bytes 884744 | tf_op jit(solution)/shard_map/ppermute | solution.py:297
  38.8 11.2 %collective-permute-start.11 = (bf16[4,6,16,384]{3,2,1,0:T(8,128)(2,1)S(1)}, bf16[4,6,16,384]{3,2,1,0:T(8,128)(2,1)}, u32[]{:S(2)}, u32[]{:S(2)}) collective-permute-start(bf16[4,6,16,384]{3,2,1,0:T(8,128)(2,1)S(1)} %get-tuple-element.29), channel_id=1, source_target_pairs={{1,0},{2,1},{3,2},{4,3},{5,4},{6,5},{7,6},{0,7},{39,32},{32,33},{3... | collective-permute-start | bytes 884744 | tf_op jit(solution)/shard_map/ppermute | solution.py:297
  46.8 8.1 %collective-permute-start.6 = (bf16[4,6,16,384]{3,2,1,0:T(8,128)(2,1)}, bf16[4,6,16,384]{3,2,1,0:T(8,128)(2,1)S(1)}, u32[]{:S(2)}, u32[]{:S(2)}) collective-permute-start(bf16[4,6,16,384]{3,2,1,0:T(8,128)(2,1)} %collective-permute-done.5.refs_3_), channel_id=1, source_target_pairs={{1,0},{2,1},{3,2},{4,3},{5,4},{6,5},{7,6},{0,7},{39,32},{32,33},{3... | collective-permute-start | bytes 884744 | tf_op jit(solution)/shard_map/ppermute | solution.py:297
  46.8 15.6 %collective-permute-start.4 = (bf16[4,12,16,384]{3,2,1,0:T(8,128)(2,1)S(1)}, bf16[4,12,16,384]{3,2,1,0:T(8,128)(2,1)S(1)}, u32[]{:S(2)}, u32[]{:S(2)}) collective-permute-start(bf16[4,12,16,384]{3,2,1,0:T(8,128)(2,1)S(1)} %collective-permute-done.3.refs_1_), channel_id=1, source_target_pairs={{0,32},{32,0},{64,96},{96,64},{128,160},{160,128},{192,224},{224,1... | collective-permute-start | bytes 1769480 | tf_op jit(solution)/shard_map/ppermute | solution.py:287
  50.0 8.2 %collective-permute-start.12 = (bf16[4,6,16,384]{3,2,1,0:T(8,128)(2,1)}, bf16[4,6,16,384]{3,2,1,0:T(8,128)(2,1)}, u32[]{:S(2)}, u32[]{:S(2)}) collective-permute-start(bf16[4,6,16,384]{3,2,1,0:T(8,128)(2,1)} %collective-permute-done.11.refs_9_), channel_id=1, source_target_pairs={{1,0},{2,1},{3,2},{4,3},{5,4},{6,5},{7,6},{0,7},{39,32},{32,33},{3... | collective-permute-start | bytes 884744 | tf_op jit(solution)/shard_map/ppermute | solution.py:297
  50.0 13.0 %collective-permute-start.8 = (bf16[4,6,16,384]{3,2,1,0:T(8,128)(2,1)}, bf16[4,6,16,384]{3,2,1,0:T(8,128)(2,1)S(1)}, u32[]{:S(2)}, u32[]{:S(2)}) collective-permute-start(bf16[4,6,16,384]{3,2,1,0:T(8,128)(2,1)} %collective-permute-done.5.refs_3_), channel_id=1, source_target_pairs={{0,32},{32,0},{64,96},{96,64},{128,160},{160,128},{192,224},{224,1... | collective-permute-start | bytes 884744 | tf_op jit(solution)/shard_map/ppermute | solution.py:298
  55.0 8.8 %copy-start.7 = (bf16[4,6,16,384]{3,2,1,0:T(8,128)(2,1)}, bf16[4,6,16,384]{3,2,1,0:T(8,128)(2,1)S(1)}, u32[]{:S(2)}) copy-start(bf16[4,6,16,384]{3,2,1,0:T(8,128)(2,1)S(1)} %collective-permute-done.6.refs_4_) | copy-start | bytes 884740
  55.0 6.4 %collective-permute-start.7 = (bf16[2,6,16,384]{3,2,1,0:T(8,128)(2,1)S(1)}, bf16[2,6,16,384]{3,2,1,0:T(8,128)(2,1)S(1)}, u32[]{:S(2)}, u32[]{:S(2)}) collective-permute-start(bf16[2,6,16,384]{3,2,1,0:T(8,128)(2,1)S(1)} %constant_dynamic-slice_fusion.1), channel_id=1, source_target_pairs={{1,0},{2,1},{3,2},{4,3},{5,4},{6,5},{7,6},{0,7},{39,32},{32,33},{3... | collective-permute-start | bytes 442376 | tf_op jit(solution)/shard_map/ppermute | solution.py:297
  55.1 7.9 %collective-permute-start.9 = (bf16[4,6,16,384]{3,2,1,0:T(8,128)(2,1)S(1)}, bf16[4,6,16,384]{3,2,1,0:T(8,128)(2,1)S(1)}, u32[]{:S(2)}, u32[]{:S(2)}) collective-permute-start(bf16[4,6,16,384]{3,2,1,0:T(8,128)(2,1)S(1)} %collective-permute-done.6.refs_4_), channel_id=1, source_target_pairs={{0,32},{32,0},{64,96},{96,64},{128,160},{160,128},{192,224},{224,1... | collective-permute-start | bytes 884744 | tf_op jit(solution)/shard_map/ppermute | solution.py:298
  58.2 14.7 %collective-permute-start.14 = (bf16[4,6,16,384]{3,2,1,0:T(8,128)(2,1)}, bf16[4,6,16,384]{3,2,1,0:T(8,128)(2,1)}, u32[]{:S(2)}, u32[]{:S(2)}) collective-permute-start(bf16[4,6,16,384]{3,2,1,0:T(8,128)(2,1)} %collective-permute-done.11.refs_9_), channel_id=1, source_target_pairs={{0,32},{32,0},{64,96},{96,64},{128,160},{160,128},{192,224},{224,1... | collective-permute-start | bytes 884744 | tf_op jit(solution)/shard_map/ppermute | solution.py:298
  61.4 1.6 %copy-start.11 = (bf16[2,6,16,384]{3,2,1,0:T(8,128)(2,1)}, bf16[2,6,16,384]{3,2,1,0:T(8,128)(2,1)S(1)}, u32[]{:S(2)}) copy-start(bf16[2,6,16,384]{3,2,1,0:T(8,128)(2,1)S(1)} %collective-permute-done.7.refs_5_) | copy-start | bytes 442372
  61.4 2.3 %collective-permute-start.10 = (bf16[2,6,16,384]{3,2,1,0:T(8,128)(2,1)S(1)}, bf16[2,6,16,384]{3,2,1,0:T(8,128)(2,1)}, u32[]{:S(2)}, u32[]{:S(2)}) collective-permute-start(bf16[2,6,16,384]{3,2,1,0:T(8,128)(2,1)S(1)} %collective-permute-done.7.refs_5_), channel_id=1, source_target_pairs={{0,32},{32,0},{64,96},{96,64},{128,160},{160,128},{192,224},{224,1... | collective-permute-start | bytes 442376 | tf_op jit(solution)/shard_map/ppermute | solution.py:298
  62.4 1.4 %copy-start.8 = (bf16[4,12,16,384]{3,2,1,0:T(8,128)(2,1)}, bf16[4,12,16,384]{3,2,1,0:T(8,128)(2,1)S(1)}, u32[]{:S(2)}) copy-start(bf16[4,12,16,384]{3,2,1,0:T(8,128)(2,1)S(1)} %collective-permute-done.4.refs_2_) | copy-start | bytes 1769476
  62.4 10.5 %collective-permute-start.15 = (bf16[4,6,16,384]{3,2,1,0:T(8,128)(2,1)}, bf16[4,6,16,384]{3,2,1,0:T(8,128)(2,1)S(1)}, u32[]{:S(2)}, u32[]{:S(2)}) collective-permute-start(bf16[4,6,16,384]{3,2,1,0:T(8,128)(2,1)} %collective-permute-done.12.refs_10_), channel_id=1, source_target_pairs={{0,32},{32,0},{64,96},{96,64},{128,160},{160,128},{192,224},{224,1... | collective-permute-start | bytes 884744 | tf_op jit(solution)/shard_map/ppermute | solution.py:298
  63.0 0.8 copy-start.9
  63.0 9.8 %collective-permute-start.13 = (bf16[2,6,16,384]{3,2,1,0:T(8,128)(2,1)S(1)}, bf16[2,6,16,384]{3,2,1,0:T(8,128)(2,1)S(1)}, u32[]{:S(2)}, u32[]{:S(2)}) collective-permute-start(bf16[2,6,16,384]{3,2,1,0:T(8,128)(2,1)S(1)} %constant_dynamic-slice_fusion), channel_id=1, source_target_pairs={{1,0},{2,1},{3,2},{4,3},{5,4},{6,5},{7,6},{0,7},{39,32},{32,33},{3... | collective-permute-start | bytes 442376 | tf_op jit(solution)/shard_map/ppermute | solution.py:297
  63.0 0.8 copy-start.10
  67.9 14.7 %all-to-all-start.2 = ((bf16[4,512,128]{2,1,0:T(8,128)(2,1)}), bf16[4,512,128]{2,1,0:T(8,128)(2,1)S(1)}, u32[]{:S(2)}, u32[]{:S(2)}) async-start(bf16[4,512,128]{2,1,0:T(8,128)(2,1)} %shard_map.58), calls=%async_computation.2 | async-start | bytes 1048576 | tf_op jit(solution)/shard_map/all_to_all | solution.py:316
  72.8 1.5 %copy-start.13 = (bf16[2,6,16,384]{3,2,1,0:T(8,128)(2,1)}, bf16[2,6,16,384]{3,2,1,0:T(8,128)(2,1)S(1)}, u32[]{:S(2)}) copy-start(bf16[2,6,16,384]{3,2,1,0:T(8,128)(2,1)S(1)} %collective-permute-done.13.refs_11_) | copy-start | bytes 442372
  72.8 1.5 %collective-permute-start.16 = (bf16[2,6,16,384]{3,2,1,0:T(8,128)(2,1)S(1)}, bf16[2,6,16,384]{3,2,1,0:T(8,128)(2,1)S(1)}, u32[]{:S(2)}, u32[]{:S(2)}) collective-permute-start(bf16[2,6,16,384]{3,2,1,0:T(8,128)(2,1)S(1)} %collective-permute-done.13.refs_11_), channel_id=1, source_target_pairs={{0,32},{32,0},{64,96},{96,64},{128,160},{160,128},{192,224},{224,1... | collective-permute-start | bytes 442376 | tf_op jit(solution)/shard_map/ppermute | solution.py:298
  73.0 1.3 %copy-start.12 = (bf16[4,6,16,384]{3,2,1,0:T(8,128)(2,1)}, bf16[4,6,16,384]{3,2,1,0:T(8,128)(2,1)S(1)}, u32[]{:S(2)}) copy-start(bf16[4,6,16,384]{3,2,1,0:T(8,128)(2,1)S(1)} %collective-permute-done.15.refs_13_) | copy-start | bytes 884740
  74.2 0.7 copy-start.14
  82.7 3.8 %collective-permute-start.17 = (bf16[8,4,8,128]{3,2,1,0:T(8,128)(2,1)S(1)}, bf16[8,4,8,128]{3,2,1,0:T(8,128)(2,1)S(1)}, u32[]{:S(2)}, u32[]{:S(2)}) collective-permute-start(bf16[8,4,8,128]{3,2,1,0:T(8,128)(2,1)S(1)} %get-tuple-element.21), channel_id=1, source_target_pairs={{32,0},{64,32},{96,64},{128,96},{160,128},{192,160},{224,192},{33,... | collective-permute-start | bytes 196616 | tf_op jit(solution)/shard_map/ppermute | solution.py:249
  86.6 5.9 %collective-permute-start.18 = (bf16[4,24,128]{2,1,0:T(8,128)(2,1)S(1)}, bf16[4,24,128]{2,1,0:T(8,128)(2,1)S(1)}, u32[]{:S(2)}, u32[]{:S(2)}) collective-permute-start(bf16[4,24,128]{2,1,0:T(8,128)(2,1)S(1)} %pad_maximum_fusion.3), channel_id=1, source_target_pairs={{0,1},{1,2},{2,3},{3,4},{4,5},{5,6},{6,7},{8,9},{9,10},{10,11},{11... | collective-permute-start | bytes 73736 | tf_op jit(solution)/shard_map/ppermute | solution.py:249
  89.8 6.9 %collective-permute-start.19 = (bf16[4,24,128]{2,1,0:T(8,128)(2,1)S(1)}, bf16[4,24,128]{2,1,0:T(8,128)(2,1)S(1)}, u32[]{:S(2)}, u32[]{:S(2)}) collective-permute-start(bf16[4,24,128]{2,1,0:T(8,128)(2,1)S(1)} %pad_maximum_fusion.4), channel_id=1, source_target_pairs={{1,0},{2,1},{3,2},{4,3},{5,4},{6,5},{7,6},{9,8},{10,9},{11,10},{12... | collective-permute-start | bytes 73736 | tf_op jit(solution)/shard_map/ppermute | solution.py:249

commit v4 on v3

--- a/solution.py
+++ b/solution.py
@@ -135,11 +135,13 @@
         box = box.reshape(-1, 3 * LANES)
         high = box.astype(BF16)
         low = (box - high.astype(F32)).astype(BF16)
-        for piece in (high, low):
-            term = lax.dot_general(
-                piece, w_ref[b], (((1,), (1,)), ((), ())), preferred_element_type=F32
-            )
-            total = term if total is None else total + term
+        term = lax.dot_general(
+            jnp.concatenate([high, low], axis=1),
+            jnp.concatenate([w_ref[b], w_ref[b]], axis=1),
+            (((1,), (1,)), ((), ())),
+            preferred_element_type=F32,
+        )
+        total = term if total is None else total + term
     for x in range(n_ha):
         out_ref[x] = total[:, x * LANES : (x + 1) * LANES].astype(BF16)
 
@@ -215,14 +217,18 @@
         win_ref[shift, :, :, :, LANES : 2 * LANES] = x.astype(BF16)
         win_ref[shift, :, :, :, 2 * LANES : 3 * LANES] = from_above(x).astype(BF16)
     total = None
-    for k in range(3):
-        fetch[k].wait()
-        for b in range(3):
-            window = win_ref[2 - k, 2 - b : 10 - b].reshape(-1, 3 * LANES)
-            term = lax.dot_general(
-                window, w_ref[3 * k + b], (((1,), (1,)), ((), ())), preferred_element_type=F32
-            )
-            total = term if total is None else total + term
+    taps = [(k, b) for k in range(3) for b in range(3)]
+    for few in (taps[0:2], taps[2:4], taps[4:6], taps[6:8], taps[8:9]):
+        for k, b in few:
+            if b == 0:
+                fetch[k].wait()
+        term = lax.dot_general(
+            jnp.concatenate([win_ref[2 - k, 2 - b : 10 - b].reshape(-1, 3 * LANES) for k, b in few], axis=1),
+            jnp.concatenate([w_ref[3 * k + b] for k, b in few], axis=1),
+            (((1,), (1,)), ((), ())),
+            preferred_element_type=F32,
+        )
+        total = term if total is None else total + term
     total = total.astype(BF16).reshape(8, n_ha, 16, -1)
     for x in range(n_ha):
         out_ref[x] = total[:, x]
@@ -272,7 +278,7 @@
     tail = slice((frames - 2) * rows, frames * rows)
     middle = latent[frames - 2 :].transpose(2, 0, 1, 3).reshape(cols, 2 * rows, chans)
     past = shifted(jnp.concatenate([left[None, tail], middle, right[None, tail]], axis=0), "ta", 1)
-    groups, past = lax.optimization_barrier((lax.all_to_all(groups, "ha", 0, 0), past))
+    groups = lax.all_to_all(groups, "ha", 0, 0)
     length = (cols + 2) * (frames + 2) * rows + (cols + 1) * frames * rows
     slab = call(
         slab_kernel, jax.ShapeDtypeStruct((n_ha, length, chans), BF16), [vmem] * 5, []
@@ -283,7 +289,7 @@
         (t * n_wa + (w + 1 - 2 * (t % 2)) % n_wa, t * n_wa + w) for t in range(n_ta) for w in range(n_wa)
     ]
     spans = [(6, 12), (0, 6)]
-    block, slab = lax.optimization_barrier((lax.ppermute(groups, ("ta", "wa"), around), slab))
+    block = lax.ppermute(groups, ("ta", "wa"), around)
     swapped = lax.ppermute(block, "ta", swap)
     mine, others = [], []
     for lo, hi in spans:

time: 116 us -> 106 us (0.914)
  waiting for transfers between devices: 48 us -> 36.1 us
  starting transfers between devices: 31.9 us -> 34.2 us
    ppermute x1, waiting for transfers between devices: 9.84 us -> 0.01 us  [on_device(): block = lax.ppermute(groups, ('ta', 'wa'), around)]
    ppermute x6, waiting for transfers between devices: 11.7 us -> 8.23 us  [shifted(): lax.ppermute(x, axis, [(i, i + step) for i in range(n) if 0 <= i + step <...]
    all_to_all x1, waiting for transfers between devices: 0.01 us -> 2.47 us  [on_device(): groups = lax.all_to_all(groups, 'ha', 0, 0)]
    ppermute x6, starting transfers between devices: 16.7 us -> 18.1 us  [shifted(): lax.ppermute(x, axis, [(i, i + step) for i in range(n) if 0 <= i + step <...]
    unnamed x30 -> x22, local copies, waits for them, and re-layouts: 3.44 us -> 3.23 us
  transfers between devices with their start and end apart: 23 -> 23, of which waited for: 12 -> 12; matrix products, arithmetic and copies ran while one was open for 1% -> 2% of each run, Pallas kernels for 9% -> 9%
where the time goes in v4:
time: 106 us; the launch traced here: 105 us
  waiting for transfers between devices  36.1 us (34%)
  starting transfers between devices  34.2 us (32%)
  Pallas kernels  14.7 us (14%)
  blocking collectives  13.5 us (13%)
  local copies, waits for them, and re-layouts  5.6 us (5%)
    ppermute x6, waiting for transfers between devices, on_device(): mine[q].append(lax.ppermute(part, ('ta', 'wa'), around))  20.8 us
    ppermute x6, starting transfers between devices, shifted(): lax.ppermute(x, axis, [(i, i + step) for i in range(n) if 0 <= i + step <...  18.1 us
    all_to_all x1, blocking collectives, on_device(): out = lax.all_to_all(out, 'ha', 0, 0)  13.5 us
    ppermute x6, waiting for transfers between devices, shifted(): lax.ppermute(x, axis, [(i, i + step) for i in range(n) if 0 <= i + step <...  8.23 us
    all_to_all x1, starting transfers between devices, on_device(): act = lax.all_to_all(act, 'ha', 0, 0)  4.81 us
    pallas_call x1, Pallas kernels, on_device(): call(fwd_kernel, (jax.ShapeDtypeStruct((cols, n_ha, frames * rows, LANES)...  4.57 us
    all_to_all x1, starting transfers between devices, on_device(): groups = lax.all_to_all(groups, 'ha', 0, 0)  4.29 us
    all_to_all x1, starting transfers between devices, on_device(): slab = lax.all_to_all(slab, 'ha', 0, 0)  3.93 us
  transfers between devices with their start and end apart: 23, of which 12 were waited for; matrix products, arithmetic and copies ran while one was open for 2% of the time, Pallas kernels for 9%

profile of v4, /device:TPU:104, one launch (start us, length us, event | category | flops | bytes accessed | tf_op | source)
XLA Modules:
  0.0 104.6 jit_solution(13567055298677751572)
XLA Ops:
  0.0 1.1 %copy-done.3 = bf16[3,3,3,16,512]{4,3,2,1,0:T(8,128)(2,1)S(1)} copy-done((bf16[3,3,3,16,512]{4,3,2,1,0:T(8,128)(2,1)S(1)}, bf16[3,3,3,16,512]{4,3,2,1,0:T(8,128)(2,1)}, u32[]{:S(2)}) %copy-start.3) | copy-done | bytes 442392
  1.1 0.9 copy-done.4
  2.0 0.9 shard_map.56
  2.9 4.3 %all-to-all-start.1 = ((bf16[4,12,16,384]{3,2,1,0:T(8,128)(2,1)}), bf16[4,12,16,384]{3,2,1,0:T(8,128)(2,1)S(1)}, u32[]{:S(2)}, u32[]{:S(2)}) async-start(bf16[4,12,16,384]{3,2,1,0:T(8,128)(2,1)} %shard_map.56), calls=%async_computation.1 | async-start | bytes 1179648 | tf_op jit(solution)/shard_map/all_to_all | solution.py:281
  7.2 0.3 slice_reduce_fusion.1
  7.6 0.2 slice_reduce_fusion.3
  7.8 2.0 %collective-permute-start.1 = (bf16[48,512]{1,0:T(8,128)(2,1)S(1)}, bf16[48,512]{1,0:T(8,128)(2,1)S(1)}, u32[]{:S(2)}, u32[]{:S(2)}) collective-permute-start(bf16[48,512]{1,0:T(8,128)(2,1)S(1)} %pad_maximum_fusion.2), channel_id=1, source_target_pairs={{1,0},{2,1},{3,2},{4,3},{5,4},{6,5},{7,6},{9,8},{10,9},{11,10},{12... | collective-permute-start | bytes 147464 | tf_op jit(solution)/shard_map/ppermute | solution.py:255
  9.9 5.0 %collective-permute-start = (bf16[48,512]{1,0:T(8,128)(2,1)S(1)}, bf16[48,512]{1,0:T(8,128)(2,1)S(1)}, u32[]{:S(2)}, u32[]{:S(2)}) collective-permute-start(bf16[48,512]{1,0:T(8,128)(2,1)S(1)} %pad_maximum_fusion.1), channel_id=1, source_target_pairs={{0,1},{1,2},{2,3},{3,4},{4,5},{5,6},{6,7},{8,9},{9,10},{10,11},{11... | collective-permute-start | bytes 147464 | tf_op jit(solution)/shard_map/ppermute | solution.py:255
  14.9 2.5 %all-to-all-done.1.refs_0_ = bf16[4,12,16,384]{3,2,1,0:T(8,128)(2,1)S(1)} async-done(((bf16[4,12,16,384]{3,2,1,0:T(8,128)(2,1)}), bf16[4,12,16,384]{3,2,1,0:T(8,128)(2,1)S(1)}, u32[]{:S(2)}, u32[]{:S(2)}) %all-to-all-start.1) | async-done | bytes 589856 | tf_op jit(solution)/shard_map/all_to_all | solution.py:281
  17.4 0.1 collective-permute-start.3
  17.6 3.3 %collective-permute-start.2 = (bf16[10,8,512]{2,1,0:T(8,128)(2,1)S(1)}, bf16[10,8,512]{2,1,0:T(8,128)(2,1)S(1)}, u32[]{:S(2)}, u32[]{:S(2)}) collective-permute-start(bf16[10,8,512]{2,1,0:T(8,128)(2,1)S(1)} %pad_maximum_fusion), channel_id=1, source_target_pairs={{0,32},{32,64},{64,96},{96,128},{128,160},{160,192},{192,224},{1,3... | collective-permute-start | bytes 245768 | tf_op jit(solution)/shard_map/ppermute | solution.py:255
  20.9 2.5 %collective-permute-done.2.past_ref = bf16[10,8,512]{2,1,0:T(8,128)(2,1)S(1)} collective-permute-done((bf16[10,8,512]{2,1,0:T(8,128)(2,1)S(1)}, bf16[10,8,512]{2,1,0:T(8,128)(2,1)S(1)}, u32[]{:S(2)}, u32[]{:S(2)}) %collective-permute-start.2) | collective-permute-done | bytes 81952 | tf_op jit(solution)/shard_map/ppermute | solution.py:255
  23.3 1.6 %shard_map.55 = bf16[4,384,512]{2,1,0:T(8,128)(2,1)} custom-call(bf16[4,4,8,512]{3,2,1,0:T(8,128)(2,1)S(1)} %copy-done.2, bf16[10,8,512]{2,1,0:T(8,128)(2,1)S(1)} %collective-permute-done.2.past_ref, bf16[4,8,16,512]{3,2,1,0:T(8,128)(2,1)S(1)} %copy-done.1, bf16[48,512]{1,0:T(8,128)(2,1)S(1)} %collective-permute-done.left_ref, ...), custom_call_target="tpu_custom_call" | custom-call | tf_op jit(solution)/shard_map/pallas_call | solution.py:283
  24.9 3.9 %all-to-all-start = ((bf16[4,384,512]{2,1,0:T(8,128)(2,1)}), bf16[4,384,512]{2,1,0:T(8,128)(2,1)S(1)}, u32[]{:S(2)}, u32[]{:S(2)}) async-start(bf16[4,384,512]{2,1,0:T(8,128)(2,1)} %shard_map.55), calls=%async_computation | async-start | bytes 3145728 | tf_op jit(solution)/shard_map/all_to_all | solution.py:306
  28.9 0.1 fusion
  28.9 0.1 collective-permute-start.5
  29.0 0.1 collective-permute-start.11
  29.1 8.4 %collective-permute-done.5.refs_3_ = bf16[4,6,16,384]{3,2,1,0:T(8,128)(2,1)} collective-permute-done((bf16[4,6,16,384]{3,2,1,0:T(8,128)(2,1)S(1)}, bf16[4,6,16,384]{3,2,1,0:T(8,128)(2,1)}, u32[]{:S(2)}, u32[]{:S(2)}) %collective-permute-start.5) | collective-permute-done | bytes 294944 | tf_op jit(solution)/shard_map/ppermute | solution.py:303
  37.5 1.0 collective-permute-start.4
  38.5 2.1 %collective-permute-done.11.refs_9_ = bf16[4,6,16,384]{3,2,1,0:T(8,128)(2,1)} collective-permute-done((bf16[4,6,16,384]{3,2,1,0:T(8,128)(2,1)S(1)}, bf16[4,6,16,384]{3,2,1,0:T(8,128)(2,1)}, u32[]{:S(2)}, u32[]{:S(2)}) %collective-permute-start.11) | collective-permute-done | bytes 294944 | tf_op jit(solution)/shard_map/ppermute | solution.py:303
  40.7 1.0 collective-permute-start.8
  41.7 4.0 %collective-permute-done.6.refs_4_ = bf16[4,6,16,384]{3,2,1,0:T(8,128)(2,1)S(1)} collective-permute-done((bf16[4,6,16,384]{3,2,1,0:T(8,128)(2,1)}, bf16[4,6,16,384]{3,2,1,0:T(8,128)(2,1)S(1)}, u32[]{:S(2)}, u32[]{:S(2)}) %collective-permute-start.6) | collective-permute-done | bytes 294944 | tf_op jit(solution)/shard_map/ppermute | solution.py:303
  45.7 0.1 collective-permute-start.7
  45.8 0.1 collective-permute-start.9
  45.9 3.1 %collective-permute-done.12.refs_10_ = bf16[4,6,16,384]{3,2,1,0:T(8,128)(2,1)} collective-permute-done((bf16[4,6,16,384]{3,2,1,0:T(8,128)(2,1)}, bf16[4,6,16,384]{3,2,1,0:T(8,128)(2,1)}, u32[]{:S(2)}, u32[]{:S(2)}) %collective-permute-start.12) | collective-permute-done | bytes 294944 | tf_op jit(solution)/shard_map/ppermute | solution.py:303
  48.9 3.3 %collective-permute-done.7.refs_5_ = bf16[2,6,16,384]{3,2,1,0:T(8,128)(2,1)} collective-permute-done((bf16[2,6,16,384]{3,2,1,0:T(8,128)(2,1)S(1)}, bf16[2,6,16,384]{3,2,1,0:T(8,128)(2,1)}, u32[]{:S(2)}, u32[]{:S(2)}) %collective-permute-start.7) | collective-permute-done | bytes 147488 | tf_op jit(solution)/shard_map/ppermute | solution.py:303
  52.2 0.9 constant_dynamic-slice_fusion
  53.2 0.6 collective-permute-start.15
  53.8 0.1 collective-permute-done.10.refs_8_
  53.9 0.1 copy-done.8
  54.0 0.5 copy-done.9
  54.5 3.7 %shard_map.58 = bf16[4,512,128]{2,1,0:T(8,128)(2,1)} custom-call(bf16[4,384,512]{2,1,0:T(8,128)(2,1)S(1)} %all-to-all-done.slab_ref, bf16[4,12,16,384]{3,2,1,0:T(8,128)(2,1)} %copy-done.5, bf16[4,12,16,384]{3,2,1,0:T(8,128)(2,1)} %copy-done.6, bf16[4,12,16,384]{3,2,1,0:T(8,128)(2,1)} %copy-done.8, bf16[4,6,16,384]{3,2,1,0:T(8,128)(2,1)} %collective-permute-done.5.refs_3_, ...), custom_call_target="tpu_custom_call" | custom-call | tf_op jit(solution)/shard_map/pallas_call | solution.py:312
  58.2 4.8 %all-to-all-start.2 = ((bf16[4,512,128]{2,1,0:T(8,128)(2,1)}), bf16[4,512,128]{2,1,0:T(8,128)(2,1)S(1)}, u32[]{:S(2)}, u32[]{:S(2)}) async-start(bf16[4,512,128]{2,1,0:T(8,128)(2,1)} %shard_map.58), calls=%async_computation.2 | async-start | bytes 1048576 | tf_op jit(solution)/shard_map/all_to_all | solution.py:322
  63.1 0.1 dynamic-slice_bitcast_fusion.bias_ref
  63.1 1.5 %collective-permute-done.16.refs_14_ = bf16[2,6,16,384]{3,2,1,0:T(8,128)(2,1)S(1)} collective-permute-done((bf16[2,6,16,384]{3,2,1,0:T(8,128)(2,1)}, bf16[2,6,16,384]{3,2,1,0:T(8,128)(2,1)S(1)}, u32[]{:S(2)}, u32[]{:S(2)}) %collective-permute-start.16) | collective-permute-done | bytes 147488 | tf_op jit(solution)/shard_map/ppermute | solution.py:304
  64.6 0.7 copy-done.10
  65.3 4.6 %shard_map.57 = (f32[8,4,16,128]{3,2,1,0:T(8,128)S(1)}, bf16[9,512,384]{2,1,0:T(8,128)(2,1)}) custom-call(bf16[4,384,512]{2,1,0:T(8,128)(2,1)S(1)} %all-to-all-done.slab_ref, f32[1,128]{1,0:T(1,128)S(1)} %dynamic-slice_bitcast_fusion.bias_ref, bf16[4,12,16,384]{3,2,1,0:T(8,128)(2,1)} %copy-done.5, bf16[4,12,16,384]{3,2,1,0:T(8,128)(2,1)} %copy-done.6, ...), custom_call_target="tpu_custom_call" | custom-call | flops 1811939328 | bytes 5242880 | tf_op jit(solution)/shard_map/pallas_call | solution.py:327
  69.9 2.9 %all-to-all-done.2.act_ref = bf16[4,512,128]{2,1,0:T(8,128)(2,1)S(1)} async-done(((bf16[4,512,128]{2,1,0:T(8,128)(2,1)}), bf16[4,512,128]{2,1,0:T(8,128)(2,1)S(1)}, u32[]{:S(2)}, u32[]{:S(2)}) %all-to-all-start.2) | async-done | bytes 524320 | tf_op jit(solution)/shard_map/all_to_all | solution.py:322
  72.8 0.1 shard_map.59
  72.9 1.9 %collective-permute-start.17 = (bf16[8,4,8,128]{3,2,1,0:T(8,128)(2,1)S(1)}, bf16[8,4,8,128]{3,2,1,0:T(8,128)(2,1)S(1)}, u32[]{:S(2)}, u32[]{:S(2)}) collective-permute-start(bf16[8,4,8,128]{3,2,1,0:T(8,128)(2,1)S(1)} %get-tuple-element.13), channel_id=1, source_target_pairs={{32,0},{64,32},{96,64},{128,96},{160,128},{192,160},{224,192},{33,... | collective-permute-start | bytes 196616 | tf_op jit(solution)/shard_map/ppermute | solution.py:255
  74.8 1.9 %collective-permute-done.17.later_ref = bf16[8,4,8,128]{3,2,1,0:T(8,128)(2,1)S(1)} collective-permute-done((bf16[8,4,8,128]{3,2,1,0:T(8,128)(2,1)S(1)}, bf16[8,4,8,128]{3,2,1,0:T(8,128)(2,1)S(1)}, u32[]{:S(2)}, u32[]{:S(2)}) %collective-permute-start.17) | collective-permute-done | bytes 65568 | tf_op jit(solution)/shard_map/ppermute | solution.py:255
  76.7 2.8 %collective-permute-start.18 = (bf16[4,24,128]{2,1,0:T(8,128)(2,1)S(1)}, bf16[4,24,128]{2,1,0:T(8,128)(2,1)S(1)}, u32[]{:S(2)}, u32[]{:S(2)}) collective-permute-start(bf16[4,24,128]{2,1,0:T(8,128)(2,1)S(1)} %pad_maximum_fusion.3), channel_id=1, source_target_pairs={{0,1},{1,2},{2,3},{3,4},{4,5},{5,6},{6,7},{8,9},{9,10},{10,11},{11... | collective-permute-start | bytes 73736 | tf_op jit(solution)/shard_map/ppermute | solution.py:255
  79.5 3.0 %collective-permute-start.19 = (bf16[4,24,128]{2,1,0:T(8,128)(2,1)S(1)}, bf16[4,24,128]{2,1,0:T(8,128)(2,1)S(1)}, u32[]{:S(2)}, u32[]{:S(2)}) collective-permute-start(bf16[4,24,128]{2,1,0:T(8,128)(2,1)S(1)} %pad_maximum_fusion.4), channel_id=1, source_target_pairs={{1,0},{2,1},{3,2},{4,3},{5,4},{6,5},{7,6},{9,8},{10,9},{11,10},{12... | collective-permute-start | bytes 73736 | tf_op jit(solution)/shard_map/ppermute | solution.py:255
  82.6 3.9 %collective-permute-done.19.right_ref = bf16[4,24,128]{2,1,0:T(8,128)(2,1)S(1)} collective-permute-done((bf16[4,24,128]{2,1,0:T(8,128)(2,1)S(1)}, bf16[4,24,128]{2,1,0:T(8,128)(2,1)S(1)}, u32[]{:S(2)}, u32[]{:S(2)}) %collective-permute-start.19) | collective-permute-done | bytes 24608 | tf_op jit(solution)/shard_map/ppermute | solution.py:255
  86.5 3.8 %shard_map.60 = bf16[4,8,16,512]{3,2,1,0:T(8,128)(2,1)S(1)} custom-call(bf16[8,4,16,128]{3,2,1,0:T(8,128)(2,1)S(1)} %get-tuple-element.12.g_ref, bf16[8,4,8,128]{3,2,1,0:T(8,128)(2,1)S(1)} %collective-permute-done.17.later_ref, bf16[4,24,128]{2,1,0:T(8,128)(2,1)S(1)} %collective-permute-done.18.left_ref, ...), custom_call_target="tpu_custom_call" | custom-call | tf_op jit(solution)/shard_map/pallas_call | solution.py:351
  90.3 13.5 %all_to_all.20 = bf16[4,8,16,512]{3,2,1,0:T(8,128)(2,1)S(1)} all-to-all(bf16[4,8,16,512]{3,2,1,0:T(8,128)(2,1)S(1)} %shard_map.60), channel_id=1, replica_groups=mesh['ta'=8,'ha'=4,'wa'=8] {'ha'}, dimensions={0} | all-to-all | bytes 1048576 | tf_op jit(solution)/shard_map/all_to_all | solution.py:357
  103.8 0.1 reduce_sum.12
  103.9 0.7 copy.17
  (52 shorter events, 0.2 us)
Async XLA Ops:
  0.0 63.1 %copy-start = (f32[512]{0:T(512)S(1)}, f32[512]{0:T(512)}, u32[]{:S(2)}) copy-start(f32[512]{0:T(512)} %param.7) | copy-start | bytes 6148
  0.0 7.2 %copy-start.1 = (bf16[4,8,16,512]{3,2,1,0:T(8,128)(2,1)S(1)}, bf16[4,8,16,512]{3,2,1,0:T(8,128)(2,1)}, u32[]{:S(2)}) copy-start(bf16[4,8,16,512]{3,2,1,0:T(8,128)(2,1)} %cot_ref.1) | copy-start | bytes 1572868
  0.0 7.6 %copy-start.2 = (bf16[4,4,8,512]{3,2,1,0:T(8,128)(2,1)S(1)}, bf16[4,4,8,512]{3,2,1,0:T(8,128)(2,1)}, u32[]{:S(2)}) copy-start(bf16[4,4,8,512]{3,2,1,0:T(8,128)(2,1)} %lat_ref.1) | copy-start | bytes 393220
  0.0 14.9 %slice-start = ((bf16[4,4,8,512]{3,2,1,0:T(8,128)(2,1)}), bf16[2,4,8,512]{3,2,1,0:T(8,128)(2,1)S(1)}, s32[]{:S(2)}) async-start(bf16[4,4,8,512]{3,2,1,0:T(8,128)(2,1)} %lat_ref.1), calls=%async_computation.4 | async-start | bytes 131072 | tf_op jit(solution)/shard_map/slice | solution.py:279
  0.0 1.1 %copy-start.3 = (bf16[3,3,3,16,512]{4,3,2,1,0:T(8,128)(2,1)S(1)}, bf16[3,3,3,16,512]{4,3,2,1,0:T(8,128)(2,1)}, u32[]{:S(2)}) copy-start(bf16[3,3,3,16,512]{4,3,2,1,0:T(8,128)(2,1)} %conv_ref.1) | copy-start | bytes 1327108
  1.1 0.9 copy-start.4
  2.9 14.5 %all-to-all-start.1 = ((bf16[4,12,16,384]{3,2,1,0:T(8,128)(2,1)}), bf16[4,12,16,384]{3,2,1,0:T(8,128)(2,1)S(1)}, u32[]{:S(2)}, u32[]{:S(2)}) async-start(bf16[4,12,16,384]{3,2,1,0:T(8,128)(2,1)} %shard_map.56), calls=%async_computation.1 | async-start | bytes 1179648 | tf_op jit(solution)/shard_map/all_to_all | solution.py:281
  7.8 9.8 %collective-permute-start.1 = (bf16[48,512]{1,0:T(8,128)(2,1)S(1)}, bf16[48,512]{1,0:T(8,128)(2,1)S(1)}, u32[]{:S(2)}, u32[]{:S(2)}) collective-permute-start(bf16[48,512]{1,0:T(8,128)(2,1)S(1)} %pad_maximum_fusion.2), channel_id=1, source_target_pairs={{1,0},{2,1},{3,2},{4,3},{5,4},{6,5},{7,6},{9,8},{10,9},{11,10},{12... | collective-permute-start | bytes 147464 | tf_op jit(solution)/shard_map/ppermute | solution.py:255
  9.9 7.7 %collective-permute-start = (bf16[48,512]{1,0:T(8,128)(2,1)S(1)}, bf16[48,512]{1,0:T(8,128)(2,1)S(1)}, u32[]{:S(2)}, u32[]{:S(2)}) collective-permute-start(bf16[48,512]{1,0:T(8,128)(2,1)S(1)} %pad_maximum_fusion.1), channel_id=1, source_target_pairs={{0,1},{1,2},{2,3},{3,4},{4,5},{5,6},{6,7},{8,9},{9,10},{10,11},{11... | collective-permute-start | bytes 147464 | tf_op jit(solution)/shard_map/ppermute | solution.py:255
  17.4 7.5 %copy-start.5 = (bf16[4,12,16,384]{3,2,1,0:T(8,128)(2,1)}, bf16[4,12,16,384]{3,2,1,0:T(8,128)(2,1)S(1)}, u32[]{:S(2)}) copy-start(bf16[4,12,16,384]{3,2,1,0:T(8,128)(2,1)S(1)} %all-to-all-done.1.refs_0_) | copy-start | bytes 1769476
  17.4 11.4 %collective-permute-start.3 = (bf16[4,12,16,384]{3,2,1,0:T(8,128)(2,1)S(1)}, bf16[4,12,16,384]{3,2,1,0:T(8,128)(2,1)S(1)}, u32[]{:S(2)}, u32[]{:S(2)}) collective-permute-start(bf16[4,12,16,384]{3,2,1,0:T(8,128)(2,1)S(1)} %all-to-all-done.1.refs_0_), channel_id=1, source_target_pairs={{1,0},{2,1},{3,2},{4,3},{5,4},{6,5},{7,6},{0,7},{39,32},{32,33},{3... | collective-permute-start | bytes 1769480 | tf_op jit(solution)/shard_map/ppermute | solution.py:292
  17.6 5.8 %collective-permute-start.2 = (bf16[10,8,512]{2,1,0:T(8,128)(2,1)S(1)}, bf16[10,8,512]{2,1,0:T(8,128)(2,1)S(1)}, u32[]{:S(2)}, u32[]{:S(2)}) collective-permute-start(bf16[10,8,512]{2,1,0:T(8,128)(2,1)S(1)} %pad_maximum_fusion), channel_id=1, source_target_pairs={{0,32},{32,64},{64,96},{96,128},{128,160},{160,192},{192,224},{1,3... | collective-permute-start | bytes 245768 | tf_op jit(solution)/shard_map/ppermute | solution.py:255
  24.9 28.8 %all-to-all-start = ((bf16[4,384,512]{2,1,0:T(8,128)(2,1)}), bf16[4,384,512]{2,1,0:T(8,128)(2,1)S(1)}, u32[]{:S(2)}, u32[]{:S(2)}) async-start(bf16[4,384,512]{2,1,0:T(8,128)(2,1)} %shard_map.55), calls=%async_computation | async-start | bytes 3145728 | tf_op jit(solution)/shard_map/all_to_all | solution.py:306
  28.9 25.1 %copy-start.6 = (bf16[4,12,16,384]{3,2,1,0:T(8,128)(2,1)}, bf16[4,12,16,384]{3,2,1,0:T(8,128)(2,1)S(1)}, u32[]{:S(2)}) copy-start(bf16[4,12,16,384]{3,2,1,0:T(8,128)(2,1)S(1)} %collective-permute-done.3.refs_1_) | copy-start | bytes 1769476
  28.9 8.6 %collective-permute-start.5 = (bf16[4,6,16,384]{3,2,1,0:T(8,128)(2,1)S(1)}, bf16[4,6,16,384]{3,2,1,0:T(8,128)(2,1)}, u32[]{:S(2)}, u32[]{:S(2)}) collective-permute-start(bf16[4,6,16,384]{3,2,1,0:T(8,128)(2,1)S(1)} %get-tuple-element.22), channel_id=1, source_target_pairs={{1,0},{2,1},{3,2},{4,3},{5,4},{6,5},{7,6},{0,7},{39,32},{32,33},{3... | collective-permute-start | bytes 884744 | tf_op jit(solution)/shard_map/ppermute | solution.py:303
  29.0 11.6 %collective-permute-start.11 = (bf16[4,6,16,384]{3,2,1,0:T(8,128)(2,1)S(1)}, bf16[4,6,16,384]{3,2,1,0:T(8,128)(2,1)}, u32[]{:S(2)}, u32[]{:S(2)}) collective-permute-start(bf16[4,6,16,384]{3,2,1,0:T(8,128)(2,1)S(1)} %get-tuple-element.21), channel_id=1, source_target_pairs={{1,0},{2,1},{3,2},{4,3},{5,4},{6,5},{7,6},{0,7},{39,32},{32,33},{3... | collective-permute-start | bytes 884744 | tf_op jit(solution)/shard_map/ppermute | solution.py:303
  37.5 8.1 %collective-permute-start.6 = (bf16[4,6,16,384]{3,2,1,0:T(8,128)(2,1)}, bf16[4,6,16,384]{3,2,1,0:T(8,128)(2,1)S(1)}, u32[]{:S(2)}, u32[]{:S(2)}) collective-permute-start(bf16[4,6,16,384]{3,2,1,0:T(8,128)(2,1)} %collective-permute-done.5.refs_3_), channel_id=1, source_target_pairs={{1,0},{2,1},{3,2},{4,3},{5,4},{6,5},{7,6},{0,7},{39,32},{32,33},{3... | collective-permute-start | bytes 884744 | tf_op jit(solution)/shard_map/ppermute | solution.py:303
  37.5 15.6 %collective-permute-start.4 = (bf16[4,12,16,384]{3,2,1,0:T(8,128)(2,1)S(1)}, bf16[4,12,16,384]{3,2,1,0:T(8,128)(2,1)S(1)}, u32[]{:S(2)}, u32[]{:S(2)}) collective-permute-start(bf16[4,12,16,384]{3,2,1,0:T(8,128)(2,1)S(1)} %collective-permute-done.3.refs_1_), channel_id=1, source_target_pairs={{0,32},{32,0},{64,96},{96,64},{128,160},{160,128},{192,224},{224,1... | collective-permute-start | bytes 1769480 | tf_op jit(solution)/shard_map/ppermute | solution.py:293
  40.7 8.2 %collective-permute-start.12 = (bf16[4,6,16,384]{3,2,1,0:T(8,128)(2,1)}, bf16[4,6,16,384]{3,2,1,0:T(8,128)(2,1)}, u32[]{:S(2)}, u32[]{:S(2)}) collective-permute-start(bf16[4,6,16,384]{3,2,1,0:T(8,128)(2,1)} %collective-permute-done.11.refs_9_), channel_id=1, source_target_pairs={{1,0},{2,1},{3,2},{4,3},{5,4},{6,5},{7,6},{0,7},{39,32},{32,33},{3... | collective-permute-start | bytes 884744 | tf_op jit(solution)/shard_map/ppermute | solution.py:303
  40.7 13.1 %collective-permute-start.8 = (bf16[4,6,16,384]{3,2,1,0:T(8,128)(2,1)}, bf16[4,6,16,384]{3,2,1,0:T(8,128)(2,1)S(1)}, u32[]{:S(2)}, u32[]{:S(2)}) collective-permute-start(bf16[4,6,16,384]{3,2,1,0:T(8,128)(2,1)} %collective-permute-done.5.refs_3_), channel_id=1, source_target_pairs={{0,32},{32,0},{64,96},{96,64},{128,160},{160,128},{192,224},{224,1... | collective-permute-start | bytes 884744 | tf_op jit(solution)/shard_map/ppermute | solution.py:304
  45.6 8.3 %copy-start.7 = (bf16[4,6,16,384]{3,2,1,0:T(8,128)(2,1)}, bf16[4,6,16,384]{3,2,1,0:T(8,128)(2,1)S(1)}, u32[]{:S(2)}) copy-start(bf16[4,6,16,384]{3,2,1,0:T(8,128)(2,1)S(1)} %collective-permute-done.6.refs_4_) | copy-start | bytes 884740
  45.7 6.5 %collective-permute-start.7 = (bf16[2,6,16,384]{3,2,1,0:T(8,128)(2,1)S(1)}, bf16[2,6,16,384]{3,2,1,0:T(8,128)(2,1)}, u32[]{:S(2)}, u32[]{:S(2)}) collective-permute-start(bf16[2,6,16,384]{3,2,1,0:T(8,128)(2,1)S(1)} %constant_dynamic-slice_fusion.1), channel_id=1, source_target_pairs={{1,0},{2,1},{3,2},{4,3},{5,4},{6,5},{7,6},{0,7},{39,32},{32,33},{3... | collective-permute-start | bytes 442376 | tf_op jit(solution)/shard_map/ppermute | solution.py:303
  45.8 8.0 %collective-permute-start.9 = (bf16[4,6,16,384]{3,2,1,0:T(8,128)(2,1)S(1)}, bf16[4,6,16,384]{3,2,1,0:T(8,128)(2,1)}, u32[]{:S(2)}, u32[]{:S(2)}) collective-permute-start(bf16[4,6,16,384]{3,2,1,0:T(8,128)(2,1)S(1)} %collective-permute-done.6.refs_4_), channel_id=1, source_target_pairs={{0,32},{32,0},{64,96},{96,64},{128,160},{160,128},{192,224},{224,1... | collective-permute-start | bytes 884744 | tf_op jit(solution)/shard_map/ppermute | solution.py:304
  48.9 14.2 %collective-permute-start.14 = (bf16[4,6,16,384]{3,2,1,0:T(8,128)(2,1)}, bf16[4,6,16,384]{3,2,1,0:T(8,128)(2,1)}, u32[]{:S(2)}, u32[]{:S(2)}) collective-permute-start(bf16[4,6,16,384]{3,2,1,0:T(8,128)(2,1)} %collective-permute-done.11.refs_9_), channel_id=1, source_target_pairs={{0,32},{32,0},{64,96},{96,64},{128,160},{160,128},{192,224},{224,1... | collective-permute-start | bytes 884744 | tf_op jit(solution)/shard_map/ppermute | solution.py:304
  52.2 1.7 %collective-permute-start.10 = (bf16[2,6,16,384]{3,2,1,0:T(8,128)(2,1)}, bf16[2,6,16,384]{3,2,1,0:T(8,128)(2,1)}, u32[]{:S(2)}, u32[]{:S(2)}) collective-permute-start(bf16[2,6,16,384]{3,2,1,0:T(8,128)(2,1)} %collective-permute-done.7.refs_5_), channel_id=1, source_target_pairs={{0,32},{32,0},{64,96},{96,64},{128,160},{160,128},{192,224},{224,1... | collective-permute-start | bytes 442376 | tf_op jit(solution)/shard_map/ppermute | solution.py:304
  53.1 0.8 copy-start.8
  53.2 10.0 %collective-permute-start.15 = (bf16[4,6,16,384]{3,2,1,0:T(8,128)(2,1)}, bf16[4,6,16,384]{3,2,1,0:T(8,128)(2,1)}, u32[]{:S(2)}, u32[]{:S(2)}) collective-permute-start(bf16[4,6,16,384]{3,2,1,0:T(8,128)(2,1)} %collective-permute-done.12.refs_10_), channel_id=1, source_target_pairs={{0,32},{32,0},{64,96},{96,64},{128,160},{160,128},{192,224},{224,1... | collective-permute-start | bytes 884744 | tf_op jit(solution)/shard_map/ppermute | solution.py:304
  53.8 0.7 copy-start.9
  53.8 9.3 %collective-permute-start.13 = (bf16[2,6,16,384]{3,2,1,0:T(8,128)(2,1)S(1)}, bf16[2,6,16,384]{3,2,1,0:T(8,128)(2,1)}, u32[]{:S(2)}, u32[]{:S(2)}) collective-permute-start(bf16[2,6,16,384]{3,2,1,0:T(8,128)(2,1)S(1)} %constant_dynamic-slice_fusion), channel_id=1, source_target_pairs={{1,0},{2,1},{3,2},{4,3},{5,4},{6,5},{7,6},{0,7},{39,32},{32,33},{3... | collective-permute-start | bytes 442376 | tf_op jit(solution)/shard_map/ppermute | solution.py:303
  58.2 14.6 %all-to-all-start.2 = ((bf16[4,512,128]{2,1,0:T(8,128)(2,1)}), bf16[4,512,128]{2,1,0:T(8,128)(2,1)S(1)}, u32[]{:S(2)}, u32[]{:S(2)}) async-start(bf16[4,512,128]{2,1,0:T(8,128)(2,1)} %shard_map.58), calls=%async_computation.2 | async-start | bytes 1048576 | tf_op jit(solution)/shard_map/all_to_all | solution.py:322
  63.0 1.6 %collective-permute-start.16 = (bf16[2,6,16,384]{3,2,1,0:T(8,128)(2,1)}, bf16[2,6,16,384]{3,2,1,0:T(8,128)(2,1)S(1)}, u32[]{:S(2)}, u32[]{:S(2)}) collective-permute-start(bf16[2,6,16,384]{3,2,1,0:T(8,128)(2,1)} %collective-permute-done.13.refs_11_), channel_id=1, source_target_pairs={{0,32},{32,0},{64,96},{96,64},{128,160},{160,128},{192,224},{224,1... | collective-permute-start | bytes 442376 | tf_op jit(solution)/shard_map/ppermute | solution.py:304
  64.6 0.7 copy-start.10
  72.9 3.8 %collective-permute-start.17 = (bf16[8,4,8,128]{3,2,1,0:T(8,128)(2,1)S(1)}, bf16[8,4,8,128]{3,2,1,0:T(8,128)(2,1)S(1)}, u32[]{:S(2)}, u32[]{:S(2)}) collective-permute-start(bf16[8,4,8,128]{3,2,1,0:T(8,128)(2,1)S(1)} %get-tuple-element.13), channel_id=1, source_target_pairs={{32,0},{64,32},{96,64},{128,96},{160,128},{192,160},{224,192},{33,... | collective-permute-start | bytes 196616 | tf_op jit(solution)/shard_map/ppermute | solution.py:255
  76.7 5.9 %collective-permute-start.18 = (bf16[4,24,128]{2,1,0:T(8,128)(2,1)S(1)}, bf16[4,24,128]{2,1,0:T(8,128)(2,1)S(1)}, u32[]{:S(2)}, u32[]{:S(2)}) collective-permute-start(bf16[4,24,128]{2,1,0:T(8,128)(2,1)S(1)} %pad_maximum_fusion.3), channel_id=1, source_target_pairs={{0,1},{1,2},{2,3},{3,4},{4,5},{5,6},{6,7},{8,9},{9,10},{10,11},{11... | collective-permute-start | bytes 73736 | tf_op jit(solution)/shard_map/ppermute | solution.py:255
  79.5 6.9 %collective-permute-start.19 = (bf16[4,24,128]{2,1,0:T(8,128)(2,1)S(1)}, bf16[4,24,128]{2,1,0:T(8,128)(2,1)S(1)}, u32[]{:S(2)}, u32[]{:S(2)}) collective-permute-start(bf16[4,24,128]{2,1,0:T(8,128)(2,1)S(1)} %pad_maximum_fusion.4), channel_id=1, source_target_pairs={{1,0},{2,1},{3,2},{4,3},{5,4},{6,5},{7,6},{9,8},{10,9},{11,10},{12... | collective-permute-start | bytes 73736 | tf_op jit(solution)/shard_map/ppermute | solution.py:255

commit v5 on v4

--- a/solution.py
+++ b/solution.py
@@ -250,6 +250,10 @@
     return pltpu.with_memory_space_constraint(x, pltpu.HBM)
 
 
+def settled(blocks):
+    return [x if x.shape[0] == 2 else in_hbm(x) for x in blocks]
+
+
 def shifted(x, axis, step):
     n = lax.axis_size(axis)
     return lax.ppermute(x, axis, [(i, i + step) for i in range(n) if 0 <= i + step < n])
@@ -268,7 +272,7 @@
         jax.ShapeDtypeStruct((n_ha, 12, shard, 3 * LANES), BF16),
         [vmem, vmem],
         [],
-    )(conv_weight, up_weight)
+    )(in_hbm(conv_weight), in_hbm(up_weight))
     def edge(col_l, col_c):
         fine = cotangent[:, :, col_c].reshape(frames * rows, 2, chans).transpose(1, 0, 2)
         return jnp.concatenate([latent[:, :, col_l].reshape(-1, chans), fine.reshape(-1, chans)], axis=0)
@@ -318,7 +322,7 @@
             pltpu.VMEM((2, cols + 1, n_ha, frames * rows, 3 * LANES), F32),
             dma((copies,)),
         ],
-    )(slab, *[in_hbm(x) for x in whole + early])
+    )(slab, *settled(whole + early))
     act = lax.all_to_all(act, "ha", 0, 0)
 
     bias = lax.dynamic_slice_in_dim(conv_bias, ha * LANES, LANES).reshape(1, LANES)
@@ -336,7 +340,7 @@
         ],
         pl.CostEstimate(flops=3 * 9 * 2 * points * LANES * chans, bytes_accessed=5 << 20, transcendentals=0),
         (vmem, hbm),
-    )(slab, bias, *[in_hbm(x) for x in whole + early + late])
+    )(slab, bias, *settled(whole + early), *settled(late))
     w_conv = in_hbm(w_conv)
     deep, high = frames * rows, 2 * rows
     shapes = [(cols, n_ha, deep), (cols, n_ha, high), (n_ha, deep), (n_ha, deep)]

time: 106 us -> 104 us (0.981)
  local copies, waits for them, and re-layouts: 5.6 us -> 3.1 us
  Pallas kernels: 14.7 us -> 15.8 us
    unnamed x22 -> x16, local copies, waits for them, and re-layouts: 3.23 us -> 0.74 us
    ppermute x6, waiting for transfers between devices: 20.8 us -> 19.5 us  [on_device(): mine[q].append(lax.ppermute(part, ('ta', 'wa'), around))]
    pallas_call x1, Pallas kernels: 0.93 us -> 2.06 us  [on_device(): call(pack_kernel, jax.ShapeDtypeStruct((n_ha, 12, shard, 3 * LANES), BF16...]
    all_to_all x1, waiting for transfers between devices: 2.92 us -> 4.03 us  [on_device(): act = lax.all_to_all(act, 'ha', 0, 0)]
  transfers between devices with their start and end apart: 23 -> 23, of which waited for: 12 -> 11; matrix products, arithmetic and copies ran while one was open for 2% -> 2% of each run, Pallas kernels for 9% -> 10%
where the time goes in v5:
time: 104 us; the launch traced here: 102 us
  waiting for transfers between devices  36 us (35%)
  starting transfers between devices  34.5 us (33%)
  Pallas kernels  15.8 us (15%)
  blocking collectives  12.6 us (12%)
  local copies, waits for them, and re-layouts  3.1 us (3%)
    ppermute x6, waiting for transfers between devices, on_device(): mine[q].append(lax.ppermute(part, ('ta', 'wa'), around))  19.5 us
    ppermute x6, starting transfers between devices, shifted(): lax.ppermute(x, axis, [(i, i + step) for i in range(n) if 0 <= i + step <...  18.1 us
    all_to_all x1, blocking collectives, on_device(): out = lax.all_to_all(out, 'ha', 0, 0)  12.6 us
    ppermute x6, waiting for transfers between devices, shifted(): lax.ppermute(x, axis, [(i, i + step) for i in range(n) if 0 <= i + step <...  8.69 us
    all_to_all x1, starting transfers between devices, on_device(): act = lax.all_to_all(act, 'ha', 0, 0)  4.81 us
    pallas_call x1, Pallas kernels, on_device(): call(fwd_kernel, (jax.ShapeDtypeStruct((cols, n_ha, frames * rows, LANES)...  4.52 us
    all_to_all x1, starting transfers between devices, on_device(): groups = lax.all_to_all(groups, 'ha', 0, 0)  4.29 us
    all_to_all x1, waiting for transfers between devices, on_device(): act = lax.all_to_all(act, 'ha', 0, 0)  4.03 us
  transfers between devices with their start and end apart: 23, of which 11 were waited for; matrix products, arithmetic and copies ran while one was open for 2% of the time, Pallas kernels for 10%

profile of v5, /device:TPU:104, one launch (start us, length us, event | category | flops | bytes accessed | tf_op | source)
XLA Modules:
  0.0 102.4 jit_solution(3383986714768991291)
XLA Ops:
  0.0 2.1 %shard_map.56 = bf16[4,12,16,384]{3,2,1,0:T(8,128)(2,1)} custom-call(bf16[3,3,3,16,512]{4,3,2,1,0:T(8,128)(2,1)} %conv_ref.1, bf16[3,3,16,512]{3,2,1,0:T(8,128)(2,1)} %up_ref.1), custom_call_target="tpu_custom_call" | custom-call | tf_op jit(solution)/shard_map/pallas_call | solution.py:270
  2.1 4.3 %all-to-all-start.1 = ((bf16[4,12,16,384]{3,2,1,0:T(8,128)(2,1)}), bf16[4,12,16,384]{3,2,1,0:T(8,128)(2,1)S(1)}, u32[]{:S(2)}, u32[]{:S(2)}) async-start(bf16[4,12,16,384]{3,2,1,0:T(8,128)(2,1)} %shard_map.56), calls=%async_computation.1 | async-start | bytes 1179648 | tf_op jit(solution)/shard_map/all_to_all | solution.py:285
  6.4 0.3 slice_reduce_fusion.1
  6.7 0.2 slice_reduce_fusion.3
  6.9 2.0 %collective-permute-start.1 = (bf16[48,512]{1,0:T(8,128)(2,1)S(1)}, bf16[48,512]{1,0:T(8,128)(2,1)S(1)}, u32[]{:S(2)}, u32[]{:S(2)}) collective-permute-start(bf16[48,512]{1,0:T(8,128)(2,1)S(1)} %pad_maximum_fusion.2), channel_id=1, source_target_pairs={{1,0},{2,1},{3,2},{4,3},{5,4},{6,5},{7,6},{9,8},{10,9},{11,10},{12... | collective-permute-start | bytes 147464 | tf_op jit(solution)/shard_map/ppermute | solution.py:259
  9.0 5.0 %collective-permute-start = (bf16[48,512]{1,0:T(8,128)(2,1)S(1)}, bf16[48,512]{1,0:T(8,128)(2,1)S(1)}, u32[]{:S(2)}, u32[]{:S(2)}) collective-permute-start(bf16[48,512]{1,0:T(8,128)(2,1)S(1)} %pad_maximum_fusion.1), channel_id=1, source_target_pairs={{0,1},{1,2},{2,3},{3,4},{4,5},{5,6},{6,7},{8,9},{9,10},{10,11},{11... | collective-permute-start | bytes 147464 | tf_op jit(solution)/shard_map/ppermute | solution.py:259
  14.1 2.5 %all-to-all-done.1.refs_0_ = bf16[4,12,16,384]{3,2,1,0:T(8,128)(2,1)S(1)} async-done(((bf16[4,12,16,384]{3,2,1,0:T(8,128)(2,1)}), bf16[4,12,16,384]{3,2,1,0:T(8,128)(2,1)S(1)}, u32[]{:S(2)}, u32[]{:S(2)}) %all-to-all-start.1) | async-done | bytes 589856 | tf_op jit(solution)/shard_map/all_to_all | solution.py:285
  16.6 0.1 collective-permute-start.3
  16.7 0.0 collective-permute-done.1.right_ref
  16.7 3.3 %collective-permute-start.2 = (bf16[10,8,512]{2,1,0:T(8,128)(2,1)S(1)}, bf16[10,8,512]{2,1,0:T(8,128)(2,1)S(1)}, u32[]{:S(2)}, u32[]{:S(2)}) collective-permute-start(bf16[10,8,512]{2,1,0:T(8,128)(2,1)S(1)} %pad_maximum_fusion), channel_id=1, source_target_pairs={{0,32},{32,64},{64,96},{96,128},{128,160},{160,192},{192,224},{1,3... | collective-permute-start | bytes 245768 | tf_op jit(solution)/shard_map/ppermute | solution.py:259
  20.0 2.5 %collective-permute-done.2.past_ref = bf16[10,8,512]{2,1,0:T(8,128)(2,1)S(1)} collective-permute-done((bf16[10,8,512]{2,1,0:T(8,128)(2,1)S(1)}, bf16[10,8,512]{2,1,0:T(8,128)(2,1)S(1)}, u32[]{:S(2)}, u32[]{:S(2)}) %collective-permute-start.2) | collective-permute-done | bytes 81952 | tf_op jit(solution)/shard_map/ppermute | solution.py:259
  22.5 1.6 %shard_map.55 = bf16[4,384,512]{2,1,0:T(8,128)(2,1)} custom-call(bf16[4,4,8,512]{3,2,1,0:T(8,128)(2,1)S(1)} %copy-done.2, bf16[10,8,512]{2,1,0:T(8,128)(2,1)S(1)} %collective-permute-done.2.past_ref, bf16[4,8,16,512]{3,2,1,0:T(8,128)(2,1)S(1)} %copy-done.1, bf16[48,512]{1,0:T(8,128)(2,1)S(1)} %collective-permute-done.left_ref, ...), custom_call_target="tpu_custom_call" | custom-call | tf_op jit(solution)/shard_map/pallas_call | solution.py:287
  24.0 3.9 %all-to-all-start = ((bf16[4,384,512]{2,1,0:T(8,128)(2,1)}), bf16[4,384,512]{2,1,0:T(8,128)(2,1)S(1)}, u32[]{:S(2)}, u32[]{:S(2)}) async-start(bf16[4,384,512]{2,1,0:T(8,128)(2,1)} %shard_map.55), calls=%async_computation | async-start | bytes 3145728 | tf_op jit(solution)/shard_map/all_to_all | solution.py:310
  28.0 0.1 fusion
  28.0 0.1 collective-permute-start.5
  28.1 0.1 collective-permute-start.11
  28.2 8.3 %collective-permute-done.5.refs_3_ = bf16[4,6,16,384]{3,2,1,0:T(8,128)(2,1)S(1)} collective-permute-done((bf16[4,6,16,384]{3,2,1,0:T(8,128)(2,1)S(1)}, bf16[4,6,16,384]{3,2,1,0:T(8,128)(2,1)S(1)}, u32[]{:S(2)}, u32[]{:S(2)}) %collective-permute-start.5) | collective-permute-done | bytes 294944 | tf_op jit(solution)/shard_map/ppermute | solution.py:307
  36.5 0.0 collective-permute-start.6
  36.5 1.1 %collective-permute-start.4 = (bf16[4,12,16,384]{3,2,1,0:T(8,128)(2,1)S(1)}, bf16[4,12,16,384]{3,2,1,0:T(8,128)(2,1)}, u32[]{:S(2)}, u32[]{:S(2)}) collective-permute-start(bf16[4,12,16,384]{3,2,1,0:T(8,128)(2,1)S(1)} %collective-permute-done.3.refs_1_), channel_id=1, source_target_pairs={{0,32},{32,0},{64,96},{96,64},{128,160},{160,128},{192,224},{224,1... | collective-permute-start | bytes 1769480 | tf_op jit(solution)/shard_map/ppermute | solution.py:297
  37.6 2.1 %collective-permute-done.11.refs_9_ = bf16[4,6,16,384]{3,2,1,0:T(8,128)(2,1)} collective-permute-done((bf16[4,6,16,384]{3,2,1,0:T(8,128)(2,1)S(1)}, bf16[4,6,16,384]{3,2,1,0:T(8,128)(2,1)}, u32[]{:S(2)}, u32[]{:S(2)}) %collective-permute-start.11) | collective-permute-done | bytes 294944 | tf_op jit(solution)/shard_map/ppermute | solution.py:307
  39.8 0.0 collective-permute-start.12
  39.8 1.0 collective-permute-start.8
  40.8 3.6 %collective-permute-done.6.refs_4_ = bf16[4,6,16,384]{3,2,1,0:T(8,128)(2,1)S(1)} collective-permute-done((bf16[4,6,16,384]{3,2,1,0:T(8,128)(2,1)S(1)}, bf16[4,6,16,384]{3,2,1,0:T(8,128)(2,1)S(1)}, u32[]{:S(2)}, u32[]{:S(2)}) %collective-permute-start.6) | collective-permute-done | bytes 294944 | tf_op jit(solution)/shard_map/ppermute | solution.py:307
  44.5 0.1 collective-permute-start.7
  44.6 0.2 collective-permute-start.9
  44.8 3.1 %collective-permute-done.12.refs_10_ = bf16[4,6,16,384]{3,2,1,0:T(8,128)(2,1)S(1)} collective-permute-done((bf16[4,6,16,384]{3,2,1,0:T(8,128)(2,1)}, bf16[4,6,16,384]{3,2,1,0:T(8,128)(2,1)S(1)}, u32[]{:S(2)}, u32[]{:S(2)}) %collective-permute-start.12) | collective-permute-done | bytes 294944 | tf_op jit(solution)/shard_map/ppermute | solution.py:307
  47.9 0.7 copy-done.7
  48.6 2.3 %collective-permute-done.7.refs_5_ = bf16[2,6,16,384]{3,2,1,0:T(8,128)(2,1)S(1)} collective-permute-done((bf16[2,6,16,384]{3,2,1,0:T(8,128)(2,1)S(1)}, bf16[2,6,16,384]{3,2,1,0:T(8,128)(2,1)S(1)}, u32[]{:S(2)}, u32[]{:S(2)}) %collective-permute-start.7) | collective-permute-done | bytes 147488 | tf_op jit(solution)/shard_map/ppermute | solution.py:307
  50.9 0.9 constant_dynamic-slice_fusion
  51.8 0.6 collective-permute-start.15
  52.4 0.0 collective-permute-start.13
  52.5 3.8 %shard_map.58 = bf16[4,512,128]{2,1,0:T(8,128)(2,1)} custom-call(bf16[4,384,512]{2,1,0:T(8,128)(2,1)S(1)} %all-to-all-done.slab_ref, bf16[4,12,16,384]{3,2,1,0:T(8,128)(2,1)} %copy-done.3, bf16[4,12,16,384]{3,2,1,0:T(8,128)(2,1)} %copy-done.4, bf16[4,12,16,384]{3,2,1,0:T(8,128)(2,1)} %collective-permute-done.4.refs_2_, bf16[4,6,16,384]{3,2,1,0:T(8,128)(2,1)} %copy-done.6, ...), custom_call_target="tpu_custom_call" | custom-call | tf_op jit(solution)/shard_map/pallas_call | solution.py:316
  56.3 4.8 %all-to-all-start.2 = ((bf16[4,512,128]{2,1,0:T(8,128)(2,1)}), bf16[4,512,128]{2,1,0:T(8,128)(2,1)S(1)}, u32[]{:S(2)}, u32[]{:S(2)}) async-start(bf16[4,512,128]{2,1,0:T(8,128)(2,1)} %shard_map.58), calls=%async_computation.2 | async-start | bytes 1048576 | tf_op jit(solution)/shard_map/all_to_all | solution.py:326
  61.1 0.0 collective-permute-start.16
  61.1 0.1 dynamic-slice_bitcast_fusion.bias_ref
  61.2 1.3 %collective-permute-done.16.refs_14_ = bf16[2,6,16,384]{3,2,1,0:T(8,128)(2,1)S(1)} collective-permute-done((bf16[2,6,16,384]{3,2,1,0:T(8,128)(2,1)S(1)}, bf16[2,6,16,384]{3,2,1,0:T(8,128)(2,1)S(1)}, u32[]{:S(2)}, u32[]{:S(2)}) %collective-permute-start.16) | collective-permute-done | bytes 147488 | tf_op jit(solution)/shard_map/ppermute | solution.py:308
  62.5 4.5 %shard_map.57 = (f32[8,4,16,128]{3,2,1,0:T(8,128)S(1)}, bf16[9,512,384]{2,1,0:T(8,128)(2,1)}) custom-call(bf16[4,384,512]{2,1,0:T(8,128)(2,1)S(1)} %all-to-all-done.slab_ref, f32[1,128]{1,0:T(1,128)S(1)} %dynamic-slice_bitcast_fusion.bias_ref, bf16[4,12,16,384]{3,2,1,0:T(8,128)(2,1)} %copy-done.3, bf16[4,12,16,384]{3,2,1,0:T(8,128)(2,1)} %copy-done.4, ...), custom_call_target="tpu_custom_call" | custom-call | flops 1811939328 | bytes 5242880 | tf_op jit(solution)/shard_map/pallas_call | solution.py:331
  67.0 4.0 %all-to-all-done.2.act_ref = bf16[4,512,128]{2,1,0:T(8,128)(2,1)S(1)} async-done(((bf16[4,512,128]{2,1,0:T(8,128)(2,1)}), bf16[4,512,128]{2,1,0:T(8,128)(2,1)S(1)}, u32[]{:S(2)}, u32[]{:S(2)}) %all-to-all-start.2) | async-done | bytes 524320 | tf_op jit(solution)/shard_map/all_to_all | solution.py:326
  71.0 0.1 shard_map.59
  71.1 1.9 %collective-permute-start.17 = (bf16[8,4,8,128]{3,2,1,0:T(8,128)(2,1)S(1)}, bf16[8,4,8,128]{3,2,1,0:T(8,128)(2,1)S(1)}, u32[]{:S(2)}, u32[]{:S(2)}) collective-permute-start(bf16[8,4,8,128]{3,2,1,0:T(8,128)(2,1)S(1)} %get-tuple-element.13), channel_id=1, source_target_pairs={{32,0},{64,32},{96,64},{128,96},{160,128},{192,160},{224,192},{33,... | collective-permute-start | bytes 196616 | tf_op jit(solution)/shard_map/ppermute | solution.py:259
  73.0 1.9 %collective-permute-done.17.later_ref = bf16[8,4,8,128]{3,2,1,0:T(8,128)(2,1)S(1)} collective-permute-done((bf16[8,4,8,128]{3,2,1,0:T(8,128)(2,1)S(1)}, bf16[8,4,8,128]{3,2,1,0:T(8,128)(2,1)S(1)}, u32[]{:S(2)}, u32[]{:S(2)}) %collective-permute-start.17) | collective-permute-done | bytes 65568 | tf_op jit(solution)/shard_map/ppermute | solution.py:259
  74.9 3.3 %collective-permute-start.18 = (bf16[4,24,128]{2,1,0:T(8,128)(2,1)S(1)}, bf16[4,24,128]{2,1,0:T(8,128)(2,1)S(1)}, u32[]{:S(2)}, u32[]{:S(2)}) collective-permute-start(bf16[4,24,128]{2,1,0:T(8,128)(2,1)S(1)} %pad_maximum_fusion.3), channel_id=1, source_target_pairs={{0,1},{1,2},{2,3},{3,4},{4,5},{5,6},{6,7},{8,9},{9,10},{10,11},{11... | collective-permute-start | bytes 73736 | tf_op jit(solution)/shard_map/ppermute | solution.py:259
  78.2 2.6 %collective-permute-start.19 = (bf16[4,24,128]{2,1,0:T(8,128)(2,1)S(1)}, bf16[4,24,128]{2,1,0:T(8,128)(2,1)S(1)}, u32[]{:S(2)}, u32[]{:S(2)}) collective-permute-start(bf16[4,24,128]{2,1,0:T(8,128)(2,1)S(1)} %pad_maximum_fusion.4), channel_id=1, source_target_pairs={{1,0},{2,1},{3,2},{4,3},{5,4},{6,5},{7,6},{9,8},{10,9},{11,10},{12... | collective-permute-start | bytes 73736 | tf_op jit(solution)/shard_map/ppermute | solution.py:259
  80.8 4.3 %collective-permute-done.19.right_ref = bf16[4,24,128]{2,1,0:T(8,128)(2,1)S(1)} collective-permute-done((bf16[4,24,128]{2,1,0:T(8,128)(2,1)S(1)}, bf16[4,24,128]{2,1,0:T(8,128)(2,1)S(1)}, u32[]{:S(2)}, u32[]{:S(2)}) %collective-permute-start.19) | collective-permute-done | bytes 24608 | tf_op jit(solution)/shard_map/ppermute | solution.py:259
  85.2 3.8 %shard_map.60 = bf16[4,8,16,512]{3,2,1,0:T(8,128)(2,1)S(1)} custom-call(bf16[8,4,16,128]{3,2,1,0:T(8,128)(2,1)S(1)} %get-tuple-element.12.g_ref, bf16[8,4,8,128]{3,2,1,0:T(8,128)(2,1)S(1)} %collective-permute-done.17.later_ref, bf16[4,24,128]{2,1,0:T(8,128)(2,1)S(1)} %collective-permute-done.18.left_ref, ...), custom_call_target="tpu_custom_call" | custom-call | tf_op jit(solution)/shard_map/pallas_call | solution.py:355
  89.0 12.6 %all_to_all.20 = bf16[4,8,16,512]{3,2,1,0:T(8,128)(2,1)S(1)} all-to-all(bf16[4,8,16,512]{3,2,1,0:T(8,128)(2,1)S(1)} %shard_map.60), channel_id=1, replica_groups=mesh['ta'=8,'ha'=4,'wa'=8] {'ha'}, dimensions={0} | all-to-all | bytes 1048576 | tf_op jit(solution)/shard_map/all_to_all | solution.py:361
  101.6 0.1 reduce_sum.12
  101.7 0.7 copy.17
  (46 shorter events, 0.2 us)
Async XLA Ops:
  0.0 61.1 %copy-start = (f32[512]{0:T(512)S(1)}, f32[512]{0:T(512)}, u32[]{:S(2)}) copy-start(f32[512]{0:T(512)} %param.7) | copy-start | bytes 6148
  0.0 6.4 %copy-start.1 = (bf16[4,8,16,512]{3,2,1,0:T(8,128)(2,1)S(1)}, bf16[4,8,16,512]{3,2,1,0:T(8,128)(2,1)}, u32[]{:S(2)}) copy-start(bf16[4,8,16,512]{3,2,1,0:T(8,128)(2,1)} %cot_ref.1) | copy-start | bytes 1572868
  0.0 6.7 %copy-start.2 = (bf16[4,4,8,512]{3,2,1,0:T(8,128)(2,1)S(1)}, bf16[4,4,8,512]{3,2,1,0:T(8,128)(2,1)}, u32[]{:S(2)}) copy-start(bf16[4,4,8,512]{3,2,1,0:T(8,128)(2,1)} %lat_ref.1) | copy-start | bytes 393220
  0.0 14.0 %slice-start = ((bf16[4,4,8,512]{3,2,1,0:T(8,128)(2,1)}), bf16[2,4,8,512]{3,2,1,0:T(8,128)(2,1)S(1)}, s32[]{:S(2)}) async-start(bf16[4,4,8,512]{3,2,1,0:T(8,128)(2,1)} %lat_ref.1), calls=%async_computation.4 | async-start | bytes 131072 | tf_op jit(solution)/shard_map/slice | solution.py:283
  2.1 14.5 %all-to-all-start.1 = ((bf16[4,12,16,384]{3,2,1,0:T(8,128)(2,1)}), bf16[4,12,16,384]{3,2,1,0:T(8,128)(2,1)S(1)}, u32[]{:S(2)}, u32[]{:S(2)}) async-start(bf16[4,12,16,384]{3,2,1,0:T(8,128)(2,1)} %shard_map.56), calls=%async_computation.1 | async-start | bytes 1179648 | tf_op jit(solution)/shard_map/all_to_all | solution.py:285
  6.9 9.8 %collective-permute-start.1 = (bf16[48,512]{1,0:T(8,128)(2,1)S(1)}, bf16[48,512]{1,0:T(8,128)(2,1)S(1)}, u32[]{:S(2)}, u32[]{:S(2)}) collective-permute-start(bf16[48,512]{1,0:T(8,128)(2,1)S(1)} %pad_maximum_fusion.2), channel_id=1, source_target_pairs={{1,0},{2,1},{3,2},{4,3},{5,4},{6,5},{7,6},{9,8},{10,9},{11,10},{12... | collective-permute-start | bytes 147464 | tf_op jit(solution)/shard_map/ppermute | solution.py:259
  9.0 7.7 %collective-permute-start = (bf16[48,512]{1,0:T(8,128)(2,1)S(1)}, bf16[48,512]{1,0:T(8,128)(2,1)S(1)}, u32[]{:S(2)}, u32[]{:S(2)}) collective-permute-start(bf16[48,512]{1,0:T(8,128)(2,1)S(1)} %pad_maximum_fusion.1), channel_id=1, source_target_pairs={{0,1},{1,2},{2,3},{3,4},{4,5},{5,6},{6,7},{8,9},{9,10},{10,11},{11... | collective-permute-start | bytes 147464 | tf_op jit(solution)/shard_map/ppermute | solution.py:259
  16.6 7.5 %copy-start.3 = (bf16[4,12,16,384]{3,2,1,0:T(8,128)(2,1)}, bf16[4,12,16,384]{3,2,1,0:T(8,128)(2,1)S(1)}, u32[]{:S(2)}) copy-start(bf16[4,12,16,384]{3,2,1,0:T(8,128)(2,1)S(1)} %all-to-all-done.1.refs_0_) | copy-start | bytes 1769476
  16.6 11.4 %collective-permute-start.3 = (bf16[4,12,16,384]{3,2,1,0:T(8,128)(2,1)S(1)}, bf16[4,12,16,384]{3,2,1,0:T(8,128)(2,1)S(1)}, u32[]{:S(2)}, u32[]{:S(2)}) collective-permute-start(bf16[4,12,16,384]{3,2,1,0:T(8,128)(2,1)S(1)} %all-to-all-done.1.refs_0_), channel_id=1, source_target_pairs={{1,0},{2,1},{3,2},{4,3},{5,4},{6,5},{7,6},{0,7},{39,32},{32,33},{3... | collective-permute-start | bytes 1769480 | tf_op jit(solution)/shard_map/ppermute | solution.py:296
  16.7 5.8 %collective-permute-start.2 = (bf16[10,8,512]{2,1,0:T(8,128)(2,1)S(1)}, bf16[10,8,512]{2,1,0:T(8,128)(2,1)S(1)}, u32[]{:S(2)}, u32[]{:S(2)}) collective-permute-start(bf16[10,8,512]{2,1,0:T(8,128)(2,1)S(1)} %pad_maximum_fusion), channel_id=1, source_target_pairs={{0,32},{32,64},{64,96},{96,128},{128,160},{160,192},{192,224},{1,3... | collective-permute-start | bytes 245768 | tf_op jit(solution)/shard_map/ppermute | solution.py:259
  24.0 28.4 %all-to-all-start = ((bf16[4,384,512]{2,1,0:T(8,128)(2,1)}), bf16[4,384,512]{2,1,0:T(8,128)(2,1)S(1)}, u32[]{:S(2)}, u32[]{:S(2)}) async-start(bf16[4,384,512]{2,1,0:T(8,128)(2,1)} %shard_map.55), calls=%async_computation | async-start | bytes 3145728 | tf_op jit(solution)/shard_map/all_to_all | solution.py:310
  28.0 24.5 %copy-start.4 = (bf16[4,12,16,384]{3,2,1,0:T(8,128)(2,1)}, bf16[4,12,16,384]{3,2,1,0:T(8,128)(2,1)S(1)}, u32[]{:S(2)}) copy-start(bf16[4,12,16,384]{3,2,1,0:T(8,128)(2,1)S(1)} %collective-permute-done.3.refs_1_) | copy-start | bytes 1769476
  28.0 8.5 %collective-permute-start.5 = (bf16[4,6,16,384]{3,2,1,0:T(8,128)(2,1)S(1)}, bf16[4,6,16,384]{3,2,1,0:T(8,128)(2,1)S(1)}, u32[]{:S(2)}, u32[]{:S(2)}) collective-permute-start(bf16[4,6,16,384]{3,2,1,0:T(8,128)(2,1)S(1)} %get-tuple-element.22), channel_id=1, source_target_pairs={{1,0},{2,1},{3,2},{4,3},{5,4},{6,5},{7,6},{0,7},{39,32},{32,33},{3... | collective-permute-start | bytes 884744 | tf_op jit(solution)/shard_map/ppermute | solution.py:307
  28.1 11.6 %collective-permute-start.11 = (bf16[4,6,16,384]{3,2,1,0:T(8,128)(2,1)S(1)}, bf16[4,6,16,384]{3,2,1,0:T(8,128)(2,1)}, u32[]{:S(2)}, u32[]{:S(2)}) collective-permute-start(bf16[4,6,16,384]{3,2,1,0:T(8,128)(2,1)S(1)} %get-tuple-element.21), channel_id=1, source_target_pairs={{1,0},{2,1},{3,2},{4,3},{5,4},{6,5},{7,6},{0,7},{39,32},{32,33},{3... | collective-permute-start | bytes 884744 | tf_op jit(solution)/shard_map/ppermute | solution.py:307
  36.5 16.0 %copy-start.6 = (bf16[4,6,16,384]{3,2,1,0:T(8,128)(2,1)}, bf16[4,6,16,384]{3,2,1,0:T(8,128)(2,1)S(1)}, u32[]{:S(2)}) copy-start(bf16[4,6,16,384]{3,2,1,0:T(8,128)(2,1)S(1)} %collective-permute-done.5.refs_3_) | copy-start | bytes 884740
  36.5 7.9 %collective-permute-start.6 = (bf16[4,6,16,384]{3,2,1,0:T(8,128)(2,1)S(1)}, bf16[4,6,16,384]{3,2,1,0:T(8,128)(2,1)S(1)}, u32[]{:S(2)}, u32[]{:S(2)}) collective-permute-start(bf16[4,6,16,384]{3,2,1,0:T(8,128)(2,1)S(1)} %collective-permute-done.5.refs_3_), channel_id=1, source_target_pairs={{1,0},{2,1},{3,2},{4,3},{5,4},{6,5},{7,6},{0,7},{39,32},{32,33},{3... | collective-permute-start | bytes 884744 | tf_op jit(solution)/shard_map/ppermute | solution.py:307
  36.5 15.3 %collective-permute-start.4 = (bf16[4,12,16,384]{3,2,1,0:T(8,128)(2,1)S(1)}, bf16[4,12,16,384]{3,2,1,0:T(8,128)(2,1)}, u32[]{:S(2)}, u32[]{:S(2)}) collective-permute-start(bf16[4,12,16,384]{3,2,1,0:T(8,128)(2,1)S(1)} %collective-permute-done.3.refs_1_), channel_id=1, source_target_pairs={{0,32},{32,0},{64,96},{96,64},{128,160},{160,128},{192,224},{224,1... | collective-permute-start | bytes 1769480 | tf_op jit(solution)/shard_map/ppermute | solution.py:297
  39.8 8.1 %collective-permute-start.12 = (bf16[4,6,16,384]{3,2,1,0:T(8,128)(2,1)}, bf16[4,6,16,384]{3,2,1,0:T(8,128)(2,1)S(1)}, u32[]{:S(2)}, u32[]{:S(2)}) collective-permute-start(bf16[4,6,16,384]{3,2,1,0:T(8,128)(2,1)} %collective-permute-done.11.refs_9_), channel_id=1, source_target_pairs={{1,0},{2,1},{3,2},{4,3},{5,4},{6,5},{7,6},{0,7},{39,32},{32,33},{3... | collective-permute-start | bytes 884744 | tf_op jit(solution)/shard_map/ppermute | solution.py:307
  39.8 12.7 %collective-permute-start.8 = (bf16[4,6,16,384]{3,2,1,0:T(8,128)(2,1)S(1)}, bf16[4,6,16,384]{3,2,1,0:T(8,128)(2,1)}, u32[]{:S(2)}, u32[]{:S(2)}) collective-permute-start(bf16[4,6,16,384]{3,2,1,0:T(8,128)(2,1)S(1)} %collective-permute-done.5.refs_3_), channel_id=1, source_target_pairs={{0,32},{32,0},{64,96},{96,64},{128,160},{160,128},{192,224},{224,1... | collective-permute-start | bytes 884744 | tf_op jit(solution)/shard_map/ppermute | solution.py:308
  44.5 8.0 %copy-start.5 = (bf16[4,6,16,384]{3,2,1,0:T(8,128)(2,1)}, bf16[4,6,16,384]{3,2,1,0:T(8,128)(2,1)S(1)}, u32[]{:S(2)}) copy-start(bf16[4,6,16,384]{3,2,1,0:T(8,128)(2,1)S(1)} %collective-permute-done.6.refs_4_) | copy-start | bytes 884740
  44.5 6.4 %collective-permute-start.7 = (bf16[2,6,16,384]{3,2,1,0:T(8,128)(2,1)S(1)}, bf16[2,6,16,384]{3,2,1,0:T(8,128)(2,1)S(1)}, u32[]{:S(2)}, u32[]{:S(2)}) collective-permute-start(bf16[2,6,16,384]{3,2,1,0:T(8,128)(2,1)S(1)} %constant_dynamic-slice_fusion.1), channel_id=1, source_target_pairs={{1,0},{2,1},{3,2},{4,3},{5,4},{6,5},{7,6},{0,7},{39,32},{32,33},{3... | collective-permute-start | bytes 442376 | tf_op jit(solution)/shard_map/ppermute | solution.py:307
  44.6 7.9 %collective-permute-start.9 = (bf16[4,6,16,384]{3,2,1,0:T(8,128)(2,1)S(1)}, bf16[4,6,16,384]{3,2,1,0:T(8,128)(2,1)}, u32[]{:S(2)}, u32[]{:S(2)}) collective-permute-start(bf16[4,6,16,384]{3,2,1,0:T(8,128)(2,1)S(1)} %collective-permute-done.6.refs_4_), channel_id=1, source_target_pairs={{0,32},{32,0},{64,96},{96,64},{128,160},{160,128},{192,224},{224,1... | collective-permute-start | bytes 884744 | tf_op jit(solution)/shard_map/ppermute | solution.py:308
  47.9 0.7 copy-start.7
  47.9 13.3 %collective-permute-start.14 = (bf16[4,6,16,384]{3,2,1,0:T(8,128)(2,1)}, bf16[4,6,16,384]{3,2,1,0:T(8,128)(2,1)}, u32[]{:S(2)}, u32[]{:S(2)}) collective-permute-start(bf16[4,6,16,384]{3,2,1,0:T(8,128)(2,1)} %collective-permute-done.11.refs_9_), channel_id=1, source_target_pairs={{0,32},{32,0},{64,96},{96,64},{128,160},{160,128},{192,224},{224,1... | collective-permute-start | bytes 884744 | tf_op jit(solution)/shard_map/ppermute | solution.py:308
  50.9 1.6 %collective-permute-start.10 = (bf16[2,6,16,384]{3,2,1,0:T(8,128)(2,1)S(1)}, bf16[2,6,16,384]{3,2,1,0:T(8,128)(2,1)S(1)}, u32[]{:S(2)}, u32[]{:S(2)}) collective-permute-start(bf16[2,6,16,384]{3,2,1,0:T(8,128)(2,1)S(1)} %collective-permute-done.7.refs_5_), channel_id=1, source_target_pairs={{0,32},{32,0},{64,96},{96,64},{128,160},{160,128},{192,224},{224,1... | collective-permute-start | bytes 442376 | tf_op jit(solution)/shard_map/ppermute | solution.py:308
  51.8 9.4 %collective-permute-start.15 = (bf16[4,6,16,384]{3,2,1,0:T(8,128)(2,1)}, bf16[4,6,16,384]{3,2,1,0:T(8,128)(2,1)}, u32[]{:S(2)}, u32[]{:S(2)}) collective-permute-start(bf16[4,6,16,384]{3,2,1,0:T(8,128)(2,1)} %copy-done.7), channel_id=1, source_target_pairs={{0,32},{32,0},{64,96},{96,64},{128,160},{160,128},{192,224},{224,1... | collective-permute-start | bytes 884744 | tf_op jit(solution)/shard_map/ppermute | solution.py:308
  52.4 8.7 %collective-permute-start.13 = (bf16[2,6,16,384]{3,2,1,0:T(8,128)(2,1)S(1)}, bf16[2,6,16,384]{3,2,1,0:T(8,128)(2,1)S(1)}, u32[]{:S(2)}, u32[]{:S(2)}) collective-permute-start(bf16[2,6,16,384]{3,2,1,0:T(8,128)(2,1)S(1)} %constant_dynamic-slice_fusion), channel_id=1, source_target_pairs={{1,0},{2,1},{3,2},{4,3},{5,4},{6,5},{7,6},{0,7},{39,32},{32,33},{3... | collective-permute-start | bytes 442376 | tf_op jit(solution)/shard_map/ppermute | solution.py:307
  56.3 14.7 %all-to-all-start.2 = ((bf16[4,512,128]{2,1,0:T(8,128)(2,1)}), bf16[4,512,128]{2,1,0:T(8,128)(2,1)S(1)}, u32[]{:S(2)}, u32[]{:S(2)}) async-start(bf16[4,512,128]{2,1,0:T(8,128)(2,1)} %shard_map.58), calls=%async_computation.2 | async-start | bytes 1048576 | tf_op jit(solution)/shard_map/all_to_all | solution.py:326
  61.1 1.4 %collective-permute-start.16 = (bf16[2,6,16,384]{3,2,1,0:T(8,128)(2,1)S(1)}, bf16[2,6,16,384]{3,2,1,0:T(8,128)(2,1)S(1)}, u32[]{:S(2)}, u32[]{:S(2)}) collective-permute-start(bf16[2,6,16,384]{3,2,1,0:T(8,128)(2,1)S(1)} %collective-permute-done.13.refs_11_), channel_id=1, source_target_pairs={{0,32},{32,0},{64,96},{96,64},{128,160},{160,128},{192,224},{224,1... | collective-permute-start | bytes 442376 | tf_op jit(solution)/shard_map/ppermute | solution.py:308
  71.1 3.8 %collective-permute-start.17 = (bf16[8,4,8,128]{3,2,1,0:T(8,128)(2,1)S(1)}, bf16[8,4,8,128]{3,2,1,0:T(8,128)(2,1)S(1)}, u32[]{:S(2)}, u32[]{:S(2)}) collective-permute-start(bf16[8,4,8,128]{3,2,1,0:T(8,128)(2,1)S(1)} %get-tuple-element.13), channel_id=1, source_target_pairs={{32,0},{64,32},{96,64},{128,96},{160,128},{192,160},{224,192},{33,... | collective-permute-start | bytes 196616 | tf_op jit(solution)/shard_map/ppermute | solution.py:259
  74.9 5.9 %collective-permute-start.18 = (bf16[4,24,128]{2,1,0:T(8,128)(2,1)S(1)}, bf16[4,24,128]{2,1,0:T(8,128)(2,1)S(1)}, u32[]{:S(2)}, u32[]{:S(2)}) collective-permute-start(bf16[4,24,128]{2,1,0:T(8,128)(2,1)S(1)} %pad_maximum_fusion.3), channel_id=1, source_target_pairs={{0,1},{1,2},{2,3},{3,4},{4,5},{5,6},{6,7},{8,9},{9,10},{10,11},{11... | collective-permute-start | bytes 73736 | tf_op jit(solution)/shard_map/ppermute | solution.py:259
  78.2 6.9 %collective-permute-start.19 = (bf16[4,24,128]{2,1,0:T(8,128)(2,1)S(1)}, bf16[4,24,128]{2,1,0:T(8,128)(2,1)S(1)}, u32[]{:S(2)}, u32[]{:S(2)}) collective-permute-start(bf16[4,24,128]{2,1,0:T(8,128)(2,1)S(1)} %pad_maximum_fusion.4), channel_id=1, source_target_pairs={{1,0},{2,1},{3,2},{4,3},{5,4},{6,5},{7,6},{9,8},{10,9},{11,10},{12... | collective-permute-start | bytes 73736 | tf_op jit(solution)/shard_map/ppermute | solution.py:259

commit v6 on v5

--- a/solution.py
+++ b/solution.py
@@ -299,13 +299,16 @@
     for lo, hi in spans:
         mine.append([block[:, lo:hi]])
         others.append([])
-    for r in range(2, n_wa // 2 + 1):
+    for r in range(2, n_wa // 2):
         for q in range(2):
-            part = mine[q][-1]
-            if r == n_wa // 2:
-                part = lax.dynamic_slice_in_dim(part, core * (n_ha // 2), n_ha // 2, axis=0)
-            mine[q].append(lax.ppermute(part, ("ta", "wa"), around))
+            mine[q].append(lax.ppermute(mine[q][-1], ("ta", "wa"), around))
             others[q].append(lax.ppermute(mine[q][-1], "ta", swap))
+    halves = [lax.dynamic_slice_in_dim(m[-1], core * (n_ha // 2), n_ha // 2, axis=0) for m in mine]
+    lasts = [lax.ppermute(x, ("ta", "wa"), around) for x in halves]
+    lasts[0], _ = lax.optimization_barrier((lasts[0], halves[1]))
+    for q in range(2):
+        mine[q].append(lasts[q])
+        others[q].append(lax.ppermute(lasts[q], "ta", swap))
     whole = [groups, block, swapped]
     slab = lax.all_to_all(slab, "ha", 0, 0)
     early, late = mine[0][1:] + others[0], mine[1][1:] + others[1]

time: 104 us -> 103 us (level)
    ppermute x6 -> x8, waiting for transfers between devices: 19.5 us -> 21.5 us  [the longest x4 17.2 us: on_device(): mine[q].append(lax.ppermute(mine[q][-1], ('ta', 'wa'), around))]
    ppermute x6 -> x4, waiting for transfers between devices: 1.28 us -> 0.01 us  [on_device(): others[q].append(lax.ppermute(mine[q][-1], 'ta', swap))]
  transfers between devices with their start and end apart: 23 -> 23, of which waited for: 11 -> 12; matrix products, arithmetic and copies ran while one was open for 2% -> 1% of each run, Pallas kernels for 10% -> 10%
where the time goes in v6:
time: 103 us; the launch traced here: 102 us
  waiting for transfers between devices  36 us (35%)
  starting transfers between devices  34.6 us (34%)
  Pallas kernels  15.8 us (15%)
  blocking collectives  12.6 us (12%)
  local copies, waits for them, and re-layouts  2.18 us (2%)
    ppermute x6, starting transfers between devices, shifted(): lax.ppermute(x, axis, [(i, i + step) for i in range(n) if 0 <= i + step <...  18.1 us
    ppermute x4, waiting for transfers between devices, on_device(): mine[q].append(lax.ppermute(mine[q][-1], ('ta', 'wa'), around))  17.2 us
    all_to_all x1, blocking collectives, on_device(): out = lax.all_to_all(out, 'ha', 0, 0)  12.6 us
    ppermute x6, waiting for transfers between devices, shifted(): lax.ppermute(x, axis, [(i, i + step) for i in range(n) if 0 <= i + step <...  8.15 us
    all_to_all x1, starting transfers between devices, on_device(): act = lax.all_to_all(act, 'ha', 0, 0)  4.81 us
    pallas_call x1, Pallas kernels, on_device(): call(fwd_kernel, (jax.ShapeDtypeStruct((cols, n_ha, frames * rows, LANES)...  4.52 us
    all_to_all x1, starting transfers between devices, on_device(): groups = lax.all_to_all(groups, 'ha', 0, 0)  4.29 us
    all_to_all x1, starting transfers between devices, on_device(): slab = lax.all_to_all(slab, 'ha', 0, 0)  3.93 us
  transfers between devices with their start and end apart: 23, of which 12 were waited for; matrix products, arithmetic and copies ran while one was open for 1% of the time, Pallas kernels for 10%

profile of v6, /device:TPU:104, one launch (start us, length us, event | category | flops | bytes accessed | tf_op | source)
XLA Modules:
  0.0 101.7 jit_solution(13214605779049933431)
XLA Ops:
  0.0 0.0 slice-start
  0.0 2.1 %shard_map.56 = bf16[4,12,16,384]{3,2,1,0:T(8,128)(2,1)} custom-call(bf16[3,3,3,16,512]{4,3,2,1,0:T(8,128)(2,1)} %conv_ref.1, bf16[3,3,16,512]{3,2,1,0:T(8,128)(2,1)} %up_ref.1), custom_call_target="tpu_custom_call" | custom-call | tf_op jit(solution)/shard_map/pallas_call | solution.py:270
  2.1 4.3 %all-to-all-start.1 = ((bf16[4,12,16,384]{3,2,1,0:T(8,128)(2,1)}), bf16[4,12,16,384]{3,2,1,0:T(8,128)(2,1)S(1)}, u32[]{:S(2)}, u32[]{:S(2)}) async-start(bf16[4,12,16,384]{3,2,1,0:T(8,128)(2,1)} %shard_map.56), calls=%async_computation.1 | async-start | bytes 1179648 | tf_op jit(solution)/shard_map/all_to_all | solution.py:285
  6.4 0.3 slice_reduce_fusion.1
  6.7 0.2 slice_reduce_fusion.3
  6.9 2.0 %collective-permute-start.1 = (bf16[48,512]{1,0:T(8,128)(2,1)S(1)}, bf16[48,512]{1,0:T(8,128)(2,1)S(1)}, u32[]{:S(2)}, u32[]{:S(2)}) collective-permute-start(bf16[48,512]{1,0:T(8,128)(2,1)S(1)} %pad_maximum_fusion.2), channel_id=1, source_target_pairs={{1,0},{2,1},{3,2},{4,3},{5,4},{6,5},{7,6},{9,8},{10,9},{11,10},{12... | collective-permute-start | bytes 147464 | tf_op jit(solution)/shard_map/ppermute | solution.py:259
  9.0 5.0 %collective-permute-start = (bf16[48,512]{1,0:T(8,128)(2,1)S(1)}, bf16[48,512]{1,0:T(8,128)(2,1)S(1)}, u32[]{:S(2)}, u32[]{:S(2)}) collective-permute-start(bf16[48,512]{1,0:T(8,128)(2,1)S(1)} %pad_maximum_fusion.1), channel_id=1, source_target_pairs={{0,1},{1,2},{2,3},{3,4},{4,5},{5,6},{6,7},{8,9},{9,10},{10,11},{11... | collective-permute-start | bytes 147464 | tf_op jit(solution)/shard_map/ppermute | solution.py:259
  14.1 2.5 %all-to-all-done.1.refs_0_ = bf16[4,12,16,384]{3,2,1,0:T(8,128)(2,1)S(1)} async-done(((bf16[4,12,16,384]{3,2,1,0:T(8,128)(2,1)}), bf16[4,12,16,384]{3,2,1,0:T(8,128)(2,1)S(1)}, u32[]{:S(2)}, u32[]{:S(2)}) %all-to-all-start.1) | async-done | bytes 589856 | tf_op jit(solution)/shard_map/all_to_all | solution.py:285
  16.6 0.1 collective-permute-start.3
  16.7 3.3 %collective-permute-start.2 = (bf16[10,8,512]{2,1,0:T(8,128)(2,1)S(1)}, bf16[10,8,512]{2,1,0:T(8,128)(2,1)S(1)}, u32[]{:S(2)}, u32[]{:S(2)}) collective-permute-start(bf16[10,8,512]{2,1,0:T(8,128)(2,1)S(1)} %pad_maximum_fusion), channel_id=1, source_target_pairs={{0,32},{32,64},{64,96},{96,128},{128,160},{160,192},{192,224},{1,3... | collective-permute-start | bytes 245768 | tf_op jit(solution)/shard_map/ppermute | solution.py:259
  20.0 2.5 %collective-permute-done.2.past_ref = bf16[10,8,512]{2,1,0:T(8,128)(2,1)S(1)} collective-permute-done((bf16[10,8,512]{2,1,0:T(8,128)(2,1)S(1)}, bf16[10,8,512]{2,1,0:T(8,128)(2,1)S(1)}, u32[]{:S(2)}, u32[]{:S(2)}) %collective-permute-start.2) | collective-permute-done | bytes 81952 | tf_op jit(solution)/shard_map/ppermute | solution.py:259
  22.5 1.6 %shard_map.55 = bf16[4,384,512]{2,1,0:T(8,128)(2,1)} custom-call(bf16[4,4,8,512]{3,2,1,0:T(8,128)(2,1)S(1)} %copy-done.2, bf16[10,8,512]{2,1,0:T(8,128)(2,1)S(1)} %collective-permute-done.2.past_ref, bf16[4,8,16,512]{3,2,1,0:T(8,128)(2,1)S(1)} %copy-done.1, bf16[48,512]{1,0:T(8,128)(2,1)S(1)} %collective-permute-done.left_ref, ...), custom_call_target="tpu_custom_call" | custom-call | tf_op jit(solution)/shard_map/pallas_call | solution.py:287
  24.0 3.9 %all-to-all-start = ((bf16[4,384,512]{2,1,0:T(8,128)(2,1)}), bf16[4,384,512]{2,1,0:T(8,128)(2,1)S(1)}, u32[]{:S(2)}, u32[]{:S(2)}) async-start(bf16[4,384,512]{2,1,0:T(8,128)(2,1)} %shard_map.55), calls=%async_computation | async-start | bytes 3145728 | tf_op jit(solution)/shard_map/all_to_all | solution.py:313
  28.0 0.0 collective-permute-done.3.refs_1_
  28.0 0.1 fusion
  28.0 0.1 collective-permute-start.5
  28.1 0.1 collective-permute-start.8
  28.2 8.3 %collective-permute-done.5.refs_3_ = bf16[4,6,16,384]{3,2,1,0:T(8,128)(2,1)S(1)} collective-permute-done((bf16[4,6,16,384]{3,2,1,0:T(8,128)(2,1)S(1)}, bf16[4,6,16,384]{3,2,1,0:T(8,128)(2,1)S(1)}, u32[]{:S(2)}, u32[]{:S(2)}) %collective-permute-start.5) | collective-permute-done | bytes 294944 | tf_op jit(solution)/shard_map/ppermute | solution.py:304
  36.5 0.0 collective-permute-start.6
  36.5 1.1 %collective-permute-start.4 = (bf16[4,12,16,384]{3,2,1,0:T(8,128)(2,1)S(1)}, bf16[4,12,16,384]{3,2,1,0:T(8,128)(2,1)}, u32[]{:S(2)}, u32[]{:S(2)}) collective-permute-start(bf16[4,12,16,384]{3,2,1,0:T(8,128)(2,1)S(1)} %collective-permute-done.3.refs_1_), channel_id=1, source_target_pairs={{0,32},{32,0},{64,96},{96,64},{128,160},{160,128},{192,224},{224,1... | collective-permute-start | bytes 1769480 | tf_op jit(solution)/shard_map/ppermute | solution.py:297
  37.6 2.1 %collective-permute-done.8.refs_9_ = bf16[4,6,16,384]{3,2,1,0:T(8,128)(2,1)} collective-permute-done((bf16[4,6,16,384]{3,2,1,0:T(8,128)(2,1)S(1)}, bf16[4,6,16,384]{3,2,1,0:T(8,128)(2,1)}, u32[]{:S(2)}, u32[]{:S(2)}) %collective-permute-start.8) | collective-permute-done | bytes 294944 | tf_op jit(solution)/shard_map/ppermute | solution.py:304
  39.8 1.0 %collective-permute-start.10 = (bf16[4,6,16,384]{3,2,1,0:T(8,128)(2,1)S(1)}, bf16[4,6,16,384]{3,2,1,0:T(8,128)(2,1)}, u32[]{:S(2)}, u32[]{:S(2)}) collective-permute-start(bf16[4,6,16,384]{3,2,1,0:T(8,128)(2,1)S(1)} %collective-permute-done.5.refs_3_), channel_id=1, source_target_pairs={{0,32},{32,0},{64,96},{96,64},{128,160},{160,128},{192,224},{224,1... | collective-permute-start | bytes 884744 | tf_op jit(solution)/shard_map/ppermute | solution.py:305
  40.8 3.6 %collective-permute-done.6.refs_4_ = bf16[4,6,16,384]{3,2,1,0:T(8,128)(2,1)S(1)} collective-permute-done((bf16[4,6,16,384]{3,2,1,0:T(8,128)(2,1)S(1)}, bf16[4,6,16,384]{3,2,1,0:T(8,128)(2,1)S(1)}, u32[]{:S(2)}, u32[]{:S(2)}) %collective-permute-start.6) | collective-permute-done | bytes 294944 | tf_op jit(solution)/shard_map/ppermute | solution.py:304
  44.5 0.1 collective-permute-start.7
  44.6 0.2 collective-permute-start.11
  44.8 3.1 %collective-permute-done.9.refs_10_ = bf16[4,6,16,384]{3,2,1,0:T(8,128)(2,1)S(1)} collective-permute-done((bf16[4,6,16,384]{3,2,1,0:T(8,128)(2,1)}, bf16[4,6,16,384]{3,2,1,0:T(8,128)(2,1)S(1)}, u32[]{:S(2)}, u32[]{:S(2)}) %collective-permute-start.9) | collective-permute-done | bytes 294944 | tf_op jit(solution)/shard_map/ppermute | solution.py:304
  47.9 0.7 copy-done.7
  48.6 2.3 %collective-permute-done.7.refs_5_ = bf16[2,6,16,384]{3,2,1,0:T(8,128)(2,1)S(1)} collective-permute-done((bf16[2,6,16,384]{3,2,1,0:T(8,128)(2,1)S(1)}, bf16[2,6,16,384]{3,2,1,0:T(8,128)(2,1)S(1)}, u32[]{:S(2)}, u32[]{:S(2)}) %collective-permute-start.7) | collective-permute-done | bytes 147488 | tf_op jit(solution)/shard_map/ppermute | solution.py:307
  50.9 0.5 collective-permute-start.14
  51.4 0.0 collective-permute-start.15
  51.4 0.3 collective-permute-start.13
  51.7 0.7 collective-permute-done.12.refs_8_
  52.5 3.8 %shard_map.58 = bf16[4,512,128]{2,1,0:T(8,128)(2,1)} custom-call(bf16[4,384,512]{2,1,0:T(8,128)(2,1)S(1)} %all-to-all-done.slab_ref, bf16[4,12,16,384]{3,2,1,0:T(8,128)(2,1)} %copy-done.3, bf16[4,12,16,384]{3,2,1,0:T(8,128)(2,1)} %copy-done.4, bf16[4,12,16,384]{3,2,1,0:T(8,128)(2,1)} %collective-permute-done.4.refs_2_, bf16[4,6,16,384]{3,2,1,0:T(8,128)(2,1)} %copy-done.6, ...), custom_call_target="tpu_custom_call" | custom-call | tf_op jit(solution)/shard_map/pallas_call | solution.py:319
  56.2 4.8 %all-to-all-start.2 = ((bf16[4,512,128]{2,1,0:T(8,128)(2,1)}), bf16[4,512,128]{2,1,0:T(8,128)(2,1)S(1)}, u32[]{:S(2)}, u32[]{:S(2)}) async-start(bf16[4,512,128]{2,1,0:T(8,128)(2,1)} %shard_map.58), calls=%async_computation.2 | async-start | bytes 1048576 | tf_op jit(solution)/shard_map/all_to_all | solution.py:329
  61.1 0.1 dynamic-slice_bitcast_fusion.bias_ref
  61.2 1.3 %collective-permute-done.16.refs_14_ = bf16[2,6,16,384]{3,2,1,0:T(8,128)(2,1)S(1)} collective-permute-done((bf16[2,6,16,384]{3,2,1,0:T(8,128)(2,1)S(1)}, bf16[2,6,16,384]{3,2,1,0:T(8,128)(2,1)S(1)}, u32[]{:S(2)}, u32[]{:S(2)}) %collective-permute-start.16) | collective-permute-done | bytes 147488 | tf_op jit(solution)/shard_map/ppermute | solution.py:311
  62.4 4.5 %shard_map.57 = (f32[8,4,16,128]{3,2,1,0:T(8,128)S(1)}, bf16[9,512,384]{2,1,0:T(8,128)(2,1)}) custom-call(bf16[4,384,512]{2,1,0:T(8,128)(2,1)S(1)} %all-to-all-done.slab_ref, f32[1,128]{1,0:T(1,128)S(1)} %dynamic-slice_bitcast_fusion.bias_ref, bf16[4,12,16,384]{3,2,1,0:T(8,128)(2,1)} %copy-done.3, bf16[4,12,16,384]{3,2,1,0:T(8,128)(2,1)} %copy-done.4, ...), custom_call_target="tpu_custom_call" | custom-call | flops 1811939328 | bytes 5242880 | tf_op jit(solution)/shard_map/pallas_call | solution.py:334
  67.0 3.9 %all-to-all-done.2.act_ref = bf16[4,512,128]{2,1,0:T(8,128)(2,1)S(1)} async-done(((bf16[4,512,128]{2,1,0:T(8,128)(2,1)}), bf16[4,512,128]{2,1,0:T(8,128)(2,1)S(1)}, u32[]{:S(2)}, u32[]{:S(2)}) %all-to-all-start.2) | async-done | bytes 524320 | tf_op jit(solution)/shard_map/all_to_all | solution.py:329
  70.8 0.1 shard_map.59
  70.9 1.9 %collective-permute-start.17 = (bf16[8,4,8,128]{3,2,1,0:T(8,128)(2,1)S(1)}, bf16[8,4,8,128]{3,2,1,0:T(8,128)(2,1)S(1)}, u32[]{:S(2)}, u32[]{:S(2)}) collective-permute-start(bf16[8,4,8,128]{3,2,1,0:T(8,128)(2,1)S(1)} %get-tuple-element.15), channel_id=1, source_target_pairs={{32,0},{64,32},{96,64},{128,96},{160,128},{192,160},{224,192},{33,... | collective-permute-start | bytes 196616 | tf_op jit(solution)/shard_map/ppermute | solution.py:259
  72.8 1.9 %collective-permute-done.17.later_ref = bf16[8,4,8,128]{3,2,1,0:T(8,128)(2,1)S(1)} collective-permute-done((bf16[8,4,8,128]{3,2,1,0:T(8,128)(2,1)S(1)}, bf16[8,4,8,128]{3,2,1,0:T(8,128)(2,1)S(1)}, u32[]{:S(2)}, u32[]{:S(2)}) %collective-permute-start.17) | collective-permute-done | bytes 65568 | tf_op jit(solution)/shard_map/ppermute | solution.py:259
  74.7 2.7 %collective-permute-start.18 = (bf16[4,24,128]{2,1,0:T(8,128)(2,1)S(1)}, bf16[4,24,128]{2,1,0:T(8,128)(2,1)S(1)}, u32[]{:S(2)}, u32[]{:S(2)}) collective-permute-start(bf16[4,24,128]{2,1,0:T(8,128)(2,1)S(1)} %pad_maximum_fusion.3), channel_id=1, source_target_pairs={{0,1},{1,2},{2,3},{3,4},{4,5},{5,6},{6,7},{8,9},{9,10},{10,11},{11... | collective-permute-start | bytes 73736 | tf_op jit(solution)/shard_map/ppermute | solution.py:259
  77.5 3.1 %collective-permute-start.19 = (bf16[4,24,128]{2,1,0:T(8,128)(2,1)S(1)}, bf16[4,24,128]{2,1,0:T(8,128)(2,1)S(1)}, u32[]{:S(2)}, u32[]{:S(2)}) collective-permute-start(bf16[4,24,128]{2,1,0:T(8,128)(2,1)S(1)} %pad_maximum_fusion.4), channel_id=1, source_target_pairs={{1,0},{2,1},{3,2},{4,3},{5,4},{6,5},{7,6},{9,8},{10,9},{11,10},{12... | collective-permute-start | bytes 73736 | tf_op jit(solution)/shard_map/ppermute | solution.py:259
  80.6 3.8 %collective-permute-done.19.right_ref = bf16[4,24,128]{2,1,0:T(8,128)(2,1)S(1)} collective-permute-done((bf16[4,24,128]{2,1,0:T(8,128)(2,1)S(1)}, bf16[4,24,128]{2,1,0:T(8,128)(2,1)S(1)}, u32[]{:S(2)}, u32[]{:S(2)}) %collective-permute-start.19) | collective-permute-done | bytes 24608 | tf_op jit(solution)/shard_map/ppermute | solution.py:259
  84.4 3.8 %shard_map.60 = bf16[4,8,16,512]{3,2,1,0:T(8,128)(2,1)S(1)} custom-call(bf16[8,4,16,128]{3,2,1,0:T(8,128)(2,1)S(1)} %get-tuple-element.14.g_ref, bf16[8,4,8,128]{3,2,1,0:T(8,128)(2,1)S(1)} %collective-permute-done.17.later_ref, bf16[4,24,128]{2,1,0:T(8,128)(2,1)S(1)} %collective-permute-done.18.left_ref, ...), custom_call_target="tpu_custom_call" | custom-call | tf_op jit(solution)/shard_map/pallas_call | solution.py:358
  88.2 12.6 %all_to_all.20 = bf16[4,8,16,512]{3,2,1,0:T(8,128)(2,1)S(1)} all-to-all(bf16[4,8,16,512]{3,2,1,0:T(8,128)(2,1)S(1)} %shard_map.60), channel_id=1, replica_groups=mesh['ta'=8,'ha'=4,'wa'=8] {'ha'}, dimensions={0} | all-to-all | bytes 1048576 | tf_op jit(solution)/shard_map/all_to_all | solution.py:364
  100.8 0.1 reduce_sum.12
  100.9 0.7 copy.17
  (46 shorter events, 0.2 us)
Async XLA Ops:
  0.0 61.1 %copy-start = (f32[512]{0:T(512)S(1)}, f32[512]{0:T(512)}, u32[]{:S(2)}) copy-start(f32[512]{0:T(512)} %param.7) | copy-start | bytes 6148
  0.0 6.4 %copy-start.1 = (bf16[4,8,16,512]{3,2,1,0:T(8,128)(2,1)S(1)}, bf16[4,8,16,512]{3,2,1,0:T(8,128)(2,1)}, u32[]{:S(2)}) copy-start(bf16[4,8,16,512]{3,2,1,0:T(8,128)(2,1)} %cot_ref.1) | copy-start | bytes 1572868
  0.0 6.7 %copy-start.2 = (bf16[4,4,8,512]{3,2,1,0:T(8,128)(2,1)S(1)}, bf16[4,4,8,512]{3,2,1,0:T(8,128)(2,1)}, u32[]{:S(2)}) copy-start(bf16[4,4,8,512]{3,2,1,0:T(8,128)(2,1)} %lat_ref.1) | copy-start | bytes 393220
  0.0 14.0 %slice-start = ((bf16[4,4,8,512]{3,2,1,0:T(8,128)(2,1)}), bf16[2,4,8,512]{3,2,1,0:T(8,128)(2,1)S(1)}, s32[]{:S(2)}) async-start(bf16[4,4,8,512]{3,2,1,0:T(8,128)(2,1)} %lat_ref.1), calls=%async_computation.4 | async-start | bytes 131072 | tf_op jit(solution)/shard_map/slice | solution.py:283
  2.1 14.5 %all-to-all-start.1 = ((bf16[4,12,16,384]{3,2,1,0:T(8,128)(2,1)}), bf16[4,12,16,384]{3,2,1,0:T(8,128)(2,1)S(1)}, u32[]{:S(2)}, u32[]{:S(2)}) async-start(bf16[4,12,16,384]{3,2,1,0:T(8,128)(2,1)} %shard_map.56), calls=%async_computation.1 | async-start | bytes 1179648 | tf_op jit(solution)/shard_map/all_to_all | solution.py:285
  6.9 9.8 %collective-permute-start.1 = (bf16[48,512]{1,0:T(8,128)(2,1)S(1)}, bf16[48,512]{1,0:T(8,128)(2,1)S(1)}, u32[]{:S(2)}, u32[]{:S(2)}) collective-permute-start(bf16[48,512]{1,0:T(8,128)(2,1)S(1)} %pad_maximum_fusion.2), channel_id=1, source_target_pairs={{1,0},{2,1},{3,2},{4,3},{5,4},{6,5},{7,6},{9,8},{10,9},{11,10},{12... | collective-permute-start | bytes 147464 | tf_op jit(solution)/shard_map/ppermute | solution.py:259
  9.0 7.7 %collective-permute-start = (bf16[48,512]{1,0:T(8,128)(2,1)S(1)}, bf16[48,512]{1,0:T(8,128)(2,1)S(1)}, u32[]{:S(2)}, u32[]{:S(2)}) collective-permute-start(bf16[48,512]{1,0:T(8,128)(2,1)S(1)} %pad_maximum_fusion.1), channel_id=1, source_target_pairs={{0,1},{1,2},{2,3},{3,4},{4,5},{5,6},{6,7},{8,9},{9,10},{10,11},{11... | collective-permute-start | bytes 147464 | tf_op jit(solution)/shard_map/ppermute | solution.py:259
  16.6 7.5 %copy-start.3 = (bf16[4,12,16,384]{3,2,1,0:T(8,128)(2,1)}, bf16[4,12,16,384]{3,2,1,0:T(8,128)(2,1)S(1)}, u32[]{:S(2)}) copy-start(bf16[4,12,16,384]{3,2,1,0:T(8,128)(2,1)S(1)} %all-to-all-done.1.refs_0_) | copy-start | bytes 1769476
  16.6 11.4 %collective-permute-start.3 = (bf16[4,12,16,384]{3,2,1,0:T(8,128)(2,1)S(1)}, bf16[4,12,16,384]{3,2,1,0:T(8,128)(2,1)S(1)}, u32[]{:S(2)}, u32[]{:S(2)}) collective-permute-start(bf16[4,12,16,384]{3,2,1,0:T(8,128)(2,1)S(1)} %all-to-all-done.1.refs_0_), channel_id=1, source_target_pairs={{1,0},{2,1},{3,2},{4,3},{5,4},{6,5},{7,6},{0,7},{39,32},{32,33},{3... | collective-permute-start | bytes 1769480 | tf_op jit(solution)/shard_map/ppermute | solution.py:296
  16.7 5.8 %collective-permute-start.2 = (bf16[10,8,512]{2,1,0:T(8,128)(2,1)S(1)}, bf16[10,8,512]{2,1,0:T(8,128)(2,1)S(1)}, u32[]{:S(2)}, u32[]{:S(2)}) collective-permute-start(bf16[10,8,512]{2,1,0:T(8,128)(2,1)S(1)} %pad_maximum_fusion), channel_id=1, source_target_pairs={{0,32},{32,64},{64,96},{96,128},{128,160},{160,192},{192,224},{1,3... | collective-permute-start | bytes 245768 | tf_op jit(solution)/shard_map/ppermute | solution.py:259
  24.0 27.7 %all-to-all-start = ((bf16[4,384,512]{2,1,0:T(8,128)(2,1)}), bf16[4,384,512]{2,1,0:T(8,128)(2,1)S(1)}, u32[]{:S(2)}, u32[]{:S(2)}) async-start(bf16[4,384,512]{2,1,0:T(8,128)(2,1)} %shard_map.55), calls=%async_computation | async-start | bytes 3145728 | tf_op jit(solution)/shard_map/all_to_all | solution.py:313
  28.0 24.5 %copy-start.4 = (bf16[4,12,16,384]{3,2,1,0:T(8,128)(2,1)}, bf16[4,12,16,384]{3,2,1,0:T(8,128)(2,1)S(1)}, u32[]{:S(2)}) copy-start(bf16[4,12,16,384]{3,2,1,0:T(8,128)(2,1)S(1)} %collective-permute-done.3.refs_1_) | copy-start | bytes 1769476
  28.0 8.5 %collective-permute-start.5 = (bf16[4,6,16,384]{3,2,1,0:T(8,128)(2,1)S(1)}, bf16[4,6,16,384]{3,2,1,0:T(8,128)(2,1)S(1)}, u32[]{:S(2)}, u32[]{:S(2)}) collective-permute-start(bf16[4,6,16,384]{3,2,1,0:T(8,128)(2,1)S(1)} %get-tuple-element.24), channel_id=1, source_target_pairs={{1,0},{2,1},{3,2},{4,3},{5,4},{6,5},{7,6},{0,7},{39,32},{32,33},{3... | collective-permute-start | bytes 884744 | tf_op jit(solution)/shard_map/ppermute | solution.py:304
  28.1 11.6 %collective-permute-start.8 = (bf16[4,6,16,384]{3,2,1,0:T(8,128)(2,1)S(1)}, bf16[4,6,16,384]{3,2,1,0:T(8,128)(2,1)}, u32[]{:S(2)}, u32[]{:S(2)}) collective-permute-start(bf16[4,6,16,384]{3,2,1,0:T(8,128)(2,1)S(1)} %get-tuple-element.23), channel_id=1, source_target_pairs={{1,0},{2,1},{3,2},{4,3},{5,4},{6,5},{7,6},{0,7},{39,32},{32,33},{3... | collective-permute-start | bytes 884744 | tf_op jit(solution)/shard_map/ppermute | solution.py:304
  36.5 15.9 %copy-start.6 = (bf16[4,6,16,384]{3,2,1,0:T(8,128)(2,1)}, bf16[4,6,16,384]{3,2,1,0:T(8,128)(2,1)S(1)}, u32[]{:S(2)}) copy-start(bf16[4,6,16,384]{3,2,1,0:T(8,128)(2,1)S(1)} %collective-permute-done.5.refs_3_) | copy-start | bytes 884740
  36.5 7.9 %collective-permute-start.6 = (bf16[4,6,16,384]{3,2,1,0:T(8,128)(2,1)S(1)}, bf16[4,6,16,384]{3,2,1,0:T(8,128)(2,1)S(1)}, u32[]{:S(2)}, u32[]{:S(2)}) collective-permute-start(bf16[4,6,16,384]{3,2,1,0:T(8,128)(2,1)S(1)} %collective-permute-done.5.refs_3_), channel_id=1, source_target_pairs={{1,0},{2,1},{3,2},{4,3},{5,4},{6,5},{7,6},{0,7},{39,32},{32,33},{3... | collective-permute-start | bytes 884744 | tf_op jit(solution)/shard_map/ppermute | solution.py:304
  36.5 14.9 %collective-permute-start.4 = (bf16[4,12,16,384]{3,2,1,0:T(8,128)(2,1)S(1)}, bf16[4,12,16,384]{3,2,1,0:T(8,128)(2,1)}, u32[]{:S(2)}, u32[]{:S(2)}) collective-permute-start(bf16[4,12,16,384]{3,2,1,0:T(8,128)(2,1)S(1)} %collective-permute-done.3.refs_1_), channel_id=1, source_target_pairs={{0,32},{32,0},{64,96},{96,64},{128,160},{160,128},{192,224},{224,1... | collective-permute-start | bytes 1769480 | tf_op jit(solution)/shard_map/ppermute | solution.py:297
  39.8 8.1 %collective-permute-start.9 = (bf16[4,6,16,384]{3,2,1,0:T(8,128)(2,1)}, bf16[4,6,16,384]{3,2,1,0:T(8,128)(2,1)S(1)}, u32[]{:S(2)}, u32[]{:S(2)}) collective-permute-start(bf16[4,6,16,384]{3,2,1,0:T(8,128)(2,1)} %collective-permute-done.8.refs_9_), channel_id=1, source_target_pairs={{1,0},{2,1},{3,2},{4,3},{5,4},{6,5},{7,6},{0,7},{39,32},{32,33},{3... | collective-permute-start | bytes 884744 | tf_op jit(solution)/shard_map/ppermute | solution.py:304
  39.8 11.6 %collective-permute-start.10 = (bf16[4,6,16,384]{3,2,1,0:T(8,128)(2,1)S(1)}, bf16[4,6,16,384]{3,2,1,0:T(8,128)(2,1)}, u32[]{:S(2)}, u32[]{:S(2)}) collective-permute-start(bf16[4,6,16,384]{3,2,1,0:T(8,128)(2,1)S(1)} %collective-permute-done.5.refs_3_), channel_id=1, source_target_pairs={{0,32},{32,0},{64,96},{96,64},{128,160},{160,128},{192,224},{224,1... | collective-permute-start | bytes 884744 | tf_op jit(solution)/shard_map/ppermute | solution.py:305
  44.5 8.0 %copy-start.5 = (bf16[4,6,16,384]{3,2,1,0:T(8,128)(2,1)}, bf16[4,6,16,384]{3,2,1,0:T(8,128)(2,1)S(1)}, u32[]{:S(2)}) copy-start(bf16[4,6,16,384]{3,2,1,0:T(8,128)(2,1)S(1)} %collective-permute-done.6.refs_4_) | copy-start | bytes 884740
  44.5 6.4 %collective-permute-start.7 = (bf16[2,6,16,384]{3,2,1,0:T(8,128)(2,1)S(1)}, bf16[2,6,16,384]{3,2,1,0:T(8,128)(2,1)S(1)}, u32[]{:S(2)}, u32[]{:S(2)}) collective-permute-start(bf16[2,6,16,384]{3,2,1,0:T(8,128)(2,1)S(1)} %constant_dynamic-slice_fusion.1), channel_id=1, source_target_pairs={{1,0},{2,1},{3,2},{4,3},{5,4},{6,5},{7,6},{0,7},{39,32},{32,33},{3... | collective-permute-start | bytes 442376 | tf_op jit(solution)/shard_map/ppermute | solution.py:307
  44.6 7.1 %collective-permute-start.11 = (bf16[4,6,16,384]{3,2,1,0:T(8,128)(2,1)S(1)}, bf16[4,6,16,384]{3,2,1,0:T(8,128)(2,1)}, u32[]{:S(2)}, u32[]{:S(2)}) collective-permute-start(bf16[4,6,16,384]{3,2,1,0:T(8,128)(2,1)S(1)} %collective-permute-done.6.refs_4_), channel_id=1, source_target_pairs={{0,32},{32,0},{64,96},{96,64},{128,160},{160,128},{192,224},{224,1... | collective-permute-start | bytes 884744 | tf_op jit(solution)/shard_map/ppermute | solution.py:305
  47.9 0.7 copy-start.7
  50.9 1.5 %collective-permute-start.12 = (bf16[2,6,16,384]{3,2,1,0:T(8,128)(2,1)S(1)}, bf16[2,6,16,384]{3,2,1,0:T(8,128)(2,1)S(1)}, u32[]{:S(2)}, u32[]{:S(2)}) collective-permute-start(bf16[2,6,16,384]{3,2,1,0:T(8,128)(2,1)S(1)} %collective-permute-done.7.refs_5_), channel_id=1, source_target_pairs={{0,32},{32,0},{64,96},{96,64},{128,160},{160,128},{192,224},{224,1... | collective-permute-start | bytes 442376 | tf_op jit(solution)/shard_map/ppermute | solution.py:311
  50.9 10.2 %collective-permute-start.14 = (bf16[4,6,16,384]{3,2,1,0:T(8,128)(2,1)}, bf16[4,6,16,384]{3,2,1,0:T(8,128)(2,1)}, u32[]{:S(2)}, u32[]{:S(2)}) collective-permute-start(bf16[4,6,16,384]{3,2,1,0:T(8,128)(2,1)} %collective-permute-done.8.refs_9_), channel_id=1, source_target_pairs={{0,32},{32,0},{64,96},{96,64},{128,160},{160,128},{192,224},{224,1... | collective-permute-start | bytes 884744 | tf_op jit(solution)/shard_map/ppermute | solution.py:305
  51.4 9.7 %collective-permute-start.15 = (bf16[4,6,16,384]{3,2,1,0:T(8,128)(2,1)}, bf16[4,6,16,384]{3,2,1,0:T(8,128)(2,1)}, u32[]{:S(2)}, u32[]{:S(2)}) collective-permute-start(bf16[4,6,16,384]{3,2,1,0:T(8,128)(2,1)} %copy-done.7), channel_id=1, source_target_pairs={{0,32},{32,0},{64,96},{96,64},{128,160},{160,128},{192,224},{224,1... | collective-permute-start | bytes 884744 | tf_op jit(solution)/shard_map/ppermute | solution.py:305
  51.4 9.6 %collective-permute-start.13 = (bf16[2,6,16,384]{3,2,1,0:T(8,128)(2,1)S(1)}, bf16[2,6,16,384]{3,2,1,0:T(8,128)(2,1)S(1)}, u32[]{:S(2)}, u32[]{:S(2)}) collective-permute-start(bf16[2,6,16,384]{3,2,1,0:T(8,128)(2,1)S(1)} %constant_dynamic-slice_fusion), channel_id=1, source_target_pairs={{1,0},{2,1},{3,2},{4,3},{5,4},{6,5},{7,6},{0,7},{39,32},{32,33},{3... | collective-permute-start | bytes 442376 | tf_op jit(solution)/shard_map/ppermute | solution.py:307
  56.2 14.6 %all-to-all-start.2 = ((bf16[4,512,128]{2,1,0:T(8,128)(2,1)}), bf16[4,512,128]{2,1,0:T(8,128)(2,1)S(1)}, u32[]{:S(2)}, u32[]{:S(2)}) async-start(bf16[4,512,128]{2,1,0:T(8,128)(2,1)} %shard_map.58), calls=%async_computation.2 | async-start | bytes 1048576 | tf_op jit(solution)/shard_map/all_to_all | solution.py:329
  61.1 1.4 %collective-permute-start.16 = (bf16[2,6,16,384]{3,2,1,0:T(8,128)(2,1)S(1)}, bf16[2,6,16,384]{3,2,1,0:T(8,128)(2,1)S(1)}, u32[]{:S(2)}, u32[]{:S(2)}) collective-permute-start(bf16[2,6,16,384]{3,2,1,0:T(8,128)(2,1)S(1)} %collective-permute-done.13.refs_11_), channel_id=1, source_target_pairs={{0,32},{32,0},{64,96},{96,64},{128,160},{160,128},{192,224},{224,1... | collective-permute-start | bytes 442376 | tf_op jit(solution)/shard_map/ppermute | solution.py:311
  70.9 3.8 %collective-permute-start.17 = (bf16[8,4,8,128]{3,2,1,0:T(8,128)(2,1)S(1)}, bf16[8,4,8,128]{3,2,1,0:T(8,128)(2,1)S(1)}, u32[]{:S(2)}, u32[]{:S(2)}) collective-permute-start(bf16[8,4,8,128]{3,2,1,0:T(8,128)(2,1)S(1)} %get-tuple-element.15), channel_id=1, source_target_pairs={{32,0},{64,32},{96,64},{128,96},{160,128},{192,160},{224,192},{33,... | collective-permute-start | bytes 196616 | tf_op jit(solution)/shard_map/ppermute | solution.py:259
  74.7 5.9 %collective-permute-start.18 = (bf16[4,24,128]{2,1,0:T(8,128)(2,1)S(1)}, bf16[4,24,128]{2,1,0:T(8,128)(2,1)S(1)}, u32[]{:S(2)}, u32[]{:S(2)}) collective-permute-start(bf16[4,24,128]{2,1,0:T(8,128)(2,1)S(1)} %pad_maximum_fusion.3), channel_id=1, source_target_pairs={{0,1},{1,2},{2,3},{3,4},{4,5},{5,6},{6,7},{8,9},{9,10},{10,11},{11... | collective-permute-start | bytes 73736 | tf_op jit(solution)/shard_map/ppermute | solution.py:259
  77.5 6.9 %collective-permute-start.19 = (bf16[4,24,128]{2,1,0:T(8,128)(2,1)S(1)}, bf16[4,24,128]{2,1,0:T(8,128)(2,1)S(1)}, u32[]{:S(2)}, u32[]{:S(2)}) collective-permute-start(bf16[4,24,128]{2,1,0:T(8,128)(2,1)S(1)} %pad_maximum_fusion.4), channel_id=1, source_target_pairs={{1,0},{2,1},{3,2},{4,3},{5,4},{6,5},{7,6},{9,8},{10,9},{11,10},{12... | collective-permute-start | bytes 73736 | tf_op jit(solution)/shard_map/ppermute | solution.py:259

commit v7 on v6

--- a/solution.py
+++ b/solution.py
@@ -32,7 +32,7 @@
     return jnp.where(row_in_block(x.shape) == 3, roll_rows(later, 3), roll_rows(x, n - 1))
 
 
-def weight_copies(whole, refs, lo, first, groups, to, w_ref, sem, base=0):
+def weight_copies(whole, refs, lo, first, groups, to, w_ref, sem, base=0, stages=(0, 1)):
     core = lax.rem(lax.axis_index("ta"), 2)
     wa = lax.axis_index("wa")
     way = 1 - 2 * core
@@ -54,14 +54,14 @@
     def behind(r):
         return lax.rem(wa + n_wa + way * r, n_wa)
 
-    for at in range(n_ha):
+    for at in range(n_ha if 0 in stages else 0):
         copy(whole[0], at, first, at, wa)
         copy(whole[1], at, first, at, behind(1))
         copy(whole[2], at, first, at, behind(-1))
         for r in range(2, rounds):
             copy(refs[r - 2], at, first - lo, at, behind(r))
             copy(refs[rounds - 1 + r - 2], at, first - lo, at, behind(-r))
-    for at in range(half):
+    for at in range(half if 1 in stages else 0):
         copy(refs[rounds - 2], at, first - lo, core * half + at, behind(rounds))
         copy(refs[-1], at, first - lo, (1 - core) * half + at, behind(rounds))
     for one in copies:
@@ -112,9 +112,13 @@
                 out_ref[x, rows, to : to + LANES] = column[:, x * LANES : (x + 1) * LANES]
 
 
-def up_kernel(slab_ref, *refs):
-    *blocks, out_ref, w_ref, rows_ref, sem = refs
-    wait = weight_copies(blocks[:3], blocks[3:], 6, 9, 3, 0, w_ref, sem)
+def up_early_kernel(*refs):
+    *blocks, out_ref, sem = refs
+    mine, others = blocks[3 : 3 + (len(blocks) - 3) // 2], blocks[3 + (len(blocks) - 3) // 2 :]
+    weight_copies(blocks[:3], [*mine, None, *others, None], 6, 9, 3, 0, out_ref, sem, stages=(0,))()
+
+
+def box_kernel(slab_ref, out_ref, rows_ref):
     n_ha = slab_ref.shape[0]
     for par in range(2):
         cot = jnp.stack([slab_ref[x, 240:384, :] for x in range(n_ha)], axis=0)
@@ -124,8 +128,6 @@
         rows_ref[par, :, :, :, 0:LANES] = odd + from_below(even)
         rows_ref[par, :, :, :, LANES : 2 * LANES] = even + odd
         rows_ref[par, :, :, :, 2 * LANES : 3 * LANES] = even + from_above(odd)
-    wait()
-    total = None
     for b in range(3):
         box = None
         for e in (1 - b, 2 - b):
@@ -134,15 +136,25 @@
             box = part if box is None else box + part
         box = box.reshape(-1, 3 * LANES)
         high = box.astype(BF16)
-        low = (box - high.astype(F32)).astype(BF16)
+        out_ref[b, :, : 3 * LANES] = high
+        out_ref[b, :, 3 * LANES :] = (box - high.astype(F32)).astype(BF16)
+
+
+def up_kernel(box_ref, early_ref, *refs):
+    *blocks, out_ref, w_ref, sem = refs
+    w_ref[...] = early_ref[...]
+    wait = weight_copies(blocks[:3], blocks[3:], 6, 9, 3, 0, w_ref, sem, stages=(1,))
+    wait()
+    total = None
+    for b in range(3):
         term = lax.dot_general(
-            jnp.concatenate([high, low], axis=1),
+            box_ref[b],
             jnp.concatenate([w_ref[b], w_ref[b]], axis=1),
             (((1,), (1,)), ((), ())),
             preferred_element_type=F32,
         )
         total = term if total is None else total + term
-    for x in range(n_ha):
+    for x in range(out_ref.shape[0]):
         out_ref[x] = total[:, x * LANES : (x + 1) * LANES].astype(BF16)
 
 
@@ -205,17 +217,16 @@
     grad = jnp.concatenate(
         [left_ref[...].astype(F32)[None], grad, right_ref[...].astype(F32)[None]], axis=0
     )
-    zero, one, two = grad[:, :, 0:4], grad[:, :, 4:8], grad[:, :, 8:12]
-    windows = [
-        grad[:, :, 0:16],
-        jnp.concatenate([one + at_start * zero, grad[:, :, 8:20]], axis=2),
-        jnp.concatenate([two + at_start * (zero + one), grad[:, :, 12:24]], axis=2),
-    ]
-    for shift in range(3):
-        x = windows[shift]
-        win_ref[shift, :, :, :, 0:LANES] = from_below(x).astype(BF16)
-        win_ref[shift, :, :, :, LANES : 2 * LANES] = x.astype(BF16)
-        win_ref[shift, :, :, :, 2 * LANES : 3 * LANES] = from_above(x).astype(BF16)
+    shifted_rows = (from_below(grad), grad, from_above(grad))
+    for a, x in enumerate(shifted_rows):
+        zero, one, two = x[:, :, 0:4], x[:, :, 4:8], x[:, :, 8:12]
+        windows = (
+            x[:, :, 0:16],
+            jnp.concatenate([one + at_start * zero, x[:, :, 8:20]], axis=2),
+            jnp.concatenate([two + at_start * (zero + one), x[:, :, 12:24]], axis=2),
+        )
+        for shift, window in enumerate(windows):
+            win_ref[shift, :, :, :, a * LANES : (a + 1) * LANES] = window.astype(BF16)
     total = None
     taps = [(k, b) for k in range(3) for b in range(3)]
     for few in (taps[0:2], taps[2:4], taps[4:6], taps[6:8], taps[8:9]):
@@ -305,12 +316,26 @@
             others[q].append(lax.ppermute(mine[q][-1], "ta", swap))
     halves = [lax.dynamic_slice_in_dim(m[-1], core * (n_ha // 2), n_ha // 2, axis=0) for m in mine]
     lasts = [lax.ppermute(x, ("ta", "wa"), around) for x in halves]
-    lasts[0], _ = lax.optimization_barrier((lasts[0], halves[1]))
+    before = [groups, block, swapped, *mine[0][1:], *others[0]]
+    up_early = call(
+        up_early_kernel,
+        jax.ShapeDtypeStruct((3, chans, 3 * LANES), BF16),
+        [anywhere] * len(before),
+        [pltpu.SemaphoreType.DMA((n_wa * n_ha,))],
+    )(*map(in_hbm, before))
+    slab = lax.all_to_all(slab, "ha", 0, 0)
+    points = cols * n_ha * frames * rows
+    boxes = call(
+        box_kernel,
+        jax.ShapeDtypeStruct((3, points, 6 * LANES), BF16),
+        [vmem],
+        [pltpu.VMEM((2, cols + 1, n_ha, frames * rows, 3 * LANES), F32)],
+    )(slab)
+    lasts[0], up_early, boxes, _ = lax.optimization_barrier((lasts[0], up_early, boxes, halves[1]))
     for q in range(2):
         mine[q].append(lasts[q])
         others[q].append(lax.ppermute(lasts[q], "ta", swap))
     whole = [groups, block, swapped]
-    slab = lax.all_to_all(slab, "ha", 0, 0)
     early, late = mine[0][1:] + others[0], mine[1][1:] + others[1]
 
     points = cols * n_ha * frames * rows
@@ -319,13 +344,12 @@
     act = call(
         up_kernel,
         jax.ShapeDtypeStruct((n_ha, points, LANES), BF16),
-        [vmem] + [anywhere] * len(whole + early),
+        [vmem, vmem] + [anywhere] * len(whole + early),
         [
             pltpu.VMEM((3, chans, 3 * LANES), BF16),
-            pltpu.VMEM((2, cols + 1, n_ha, frames * rows, 3 * LANES), F32),
             dma((copies,)),
         ],
-    )(slab, *settled(whole + early))
+    )(boxes, up_early, *settled(whole + early))
     act = lax.all_to_all(act, "ha", 0, 0)
 
     bias = lax.dynamic_slice_in_dim(conv_bias, ha * LANES, LANES).reshape(1, LANES)

time: 103 us -> 104 us (level); the launches traced: 102 us -> 104 us
  starting transfers between devices: 34.6 us -> 40.7 us
  waiting for transfers between devices: 36 us -> 30.1 us
    ppermute x4, waiting for transfers between devices: 17.2 us -> 12.2 us  [on_device(): mine[q].append(lax.ppermute(mine[q][-1], ('ta', 'wa'), around))]
    all_to_all x1, waiting for transfers between devices: 0.01 us -> 3.28 us  [on_device(): slab = lax.all_to_all(slab, 'ha', 0, 0)]
    ppermute x2, starting transfers between devices: 0.01 us -> 2.68 us  [on_device(): others[q].append(lax.ppermute(lasts[q], 'ta', swap))]
    all_to_all x1, waiting for transfers between devices: 3.86 us -> 1.19 us  [on_device(): act = lax.all_to_all(act, 'ha', 0, 0)]
    ppermute x6, starting transfers between devices: 18.1 us -> 20.4 us  [shifted(): lax.ppermute(x, axis, [(i, i + step) for i in range(n) if 0 <= i + step <...]
    ppermute x2, waiting for transfers between devices: 2.27 us -> 0.01 us  [on_device(): lasts = [lax.ppermute(x, ('ta', 'wa'), around) for x in halves]]
    ppermute x1, starting transfers between devices: 1.12 us -> 3.35 us  [on_device(): swapped = lax.ppermute(block, 'ta', swap)]
    ppermute x6, waiting for transfers between devices: 8.15 us -> 9.34 us  [shifted(): lax.ppermute(x, axis, [(i, i + step) for i in range(n) if 0 <= i + step <...]
  transfers between devices with their start and end apart: 23 -> 23, of which waited for: 12 -> 11; matrix products, arithmetic and copies ran while one was open for 1% -> 2% of each run, Pallas kernels for 10% -> 10%
where the time goes in v7:
time: 104 us
  starting transfers between devices  40.7 us (39%)
  waiting for transfers between devices  30.1 us (29%)
  Pallas kernels  16.8 us (16%)
  blocking collectives  12.5 us (12%)
  local copies, waits for them, and re-layouts  3.21 us (3%)
    ppermute x6, starting transfers between devices, shifted(): lax.ppermute(x, axis, [(i, i + step) for i in range(n) if 0 <= i + step <...  20.4 us
    all_to_all x1, blocking collectives, on_device(): out = lax.all_to_all(out, 'ha', 0, 0)  12.5 us
    ppermute x4, waiting for transfers between devices, on_device(): mine[q].append(lax.ppermute(mine[q][-1], ('ta', 'wa'), around))  12.2 us
    ppermute x6, waiting for transfers between devices, shifted(): lax.ppermute(x, axis, [(i, i + step) for i in range(n) if 0 <= i + step <...  9.34 us
    pallas_call x1, Pallas kernels, on_device(): call(fwd_kernel, (jax.ShapeDtypeStruct((cols, n_ha, frames * rows, LANES)...  4.53 us
    all_to_all x1, starting transfers between devices, on_device(): groups = lax.all_to_all(groups, 'ha', 0, 0)  4.29 us
    all_to_all x1, starting transfers between devices, on_device(): act = lax.all_to_all(act, 'ha', 0, 0)  4.06 us
    all_to_all x1, starting transfers between devices, on_device(): slab = lax.all_to_all(slab, 'ha', 0, 0)  3.93 us
  transfers between devices with their start and end apart: 23, of which 11 were waited for; matrix products, arithmetic and copies ran while one was open for 2% of the time, Pallas kernels for 10%

profile of v7, /device:TPU:104, one launch (start us, length us, event | category | flops | bytes accessed | tf_op | source)
XLA Modules:
  0.0 103.8 jit_solution(3644626432584932022)
XLA Ops:
  0.0 2.1 %shard_map.56 = bf16[4,12,16,384]{3,2,1,0:T(8,128)(2,1)} custom-call(bf16[3,3,3,16,512]{4,3,2,1,0:T(8,128)(2,1)} %conv_ref.1, bf16[3,3,16,512]{3,2,1,0:T(8,128)(2,1)} %up_ref.1), custom_call_target="tpu_custom_call" | custom-call | tf_op jit(solution)/shard_map/pallas_call | solution.py:281
  2.1 4.3 %all-to-all-start.1 = ((bf16[4,12,16,384]{3,2,1,0:T(8,128)(2,1)}), bf16[4,12,16,384]{3,2,1,0:T(8,128)(2,1)S(1)}, u32[]{:S(2)}, u32[]{:S(2)}) async-start(bf16[4,12,16,384]{3,2,1,0:T(8,128)(2,1)} %shard_map.56), calls=%async_computation.1 | async-start | bytes 1179648 | tf_op jit(solution)/shard_map/all_to_all | solution.py:296
  6.4 0.2 slice_reduce_fusion.3
  6.6 0.3 slice_reduce_fusion.1
  6.9 2.0 %collective-permute-start.1 = (bf16[48,512]{1,0:T(8,128)(2,1)S(1)}, bf16[48,512]{1,0:T(8,128)(2,1)S(1)}, u32[]{:S(2)}, u32[]{:S(2)}) collective-permute-start(bf16[48,512]{1,0:T(8,128)(2,1)S(1)} %pad_maximum_fusion.2), channel_id=1, source_target_pairs={{1,0},{2,1},{3,2},{4,3},{5,4},{6,5},{7,6},{9,8},{10,9},{11,10},{12... | collective-permute-start | bytes 147464 | tf_op jit(solution)/shard_map/ppermute | solution.py:270
  9.0 5.0 %collective-permute-start = (bf16[48,512]{1,0:T(8,128)(2,1)S(1)}, bf16[48,512]{1,0:T(8,128)(2,1)S(1)}, u32[]{:S(2)}, u32[]{:S(2)}) collective-permute-start(bf16[48,512]{1,0:T(8,128)(2,1)S(1)} %pad_maximum_fusion.1), channel_id=1, source_target_pairs={{0,1},{1,2},{2,3},{3,4},{4,5},{5,6},{6,7},{8,9},{9,10},{10,11},{11... | collective-permute-start | bytes 147464 | tf_op jit(solution)/shard_map/ppermute | solution.py:270
  14.1 2.5 %all-to-all-done.1.refs_0_ = bf16[4,12,16,384]{3,2,1,0:T(8,128)(2,1)S(1)} async-done(((bf16[4,12,16,384]{3,2,1,0:T(8,128)(2,1)}), bf16[4,12,16,384]{3,2,1,0:T(8,128)(2,1)S(1)}, u32[]{:S(2)}, u32[]{:S(2)}) %all-to-all-start.1) | async-done | bytes 589856 | tf_op jit(solution)/shard_map/all_to_all | solution.py:296
  16.6 0.1 collective-permute-start.3
  16.7 3.3 %collective-permute-start.2 = (bf16[10,8,512]{2,1,0:T(8,128)(2,1)S(1)}, bf16[10,8,512]{2,1,0:T(8,128)(2,1)S(1)}, u32[]{:S(2)}, u32[]{:S(2)}) collective-permute-start(bf16[10,8,512]{2,1,0:T(8,128)(2,1)S(1)} %pad_maximum_fusion), channel_id=1, source_target_pairs={{0,32},{32,64},{64,96},{96,128},{128,160},{160,192},{192,224},{1,3... | collective-permute-start | bytes 245768 | tf_op jit(solution)/shard_map/ppermute | solution.py:270
  20.0 2.5 %collective-permute-done.2.past_ref = bf16[10,8,512]{2,1,0:T(8,128)(2,1)S(1)} collective-permute-done((bf16[10,8,512]{2,1,0:T(8,128)(2,1)S(1)}, bf16[10,8,512]{2,1,0:T(8,128)(2,1)S(1)}, u32[]{:S(2)}, u32[]{:S(2)}) %collective-permute-start.2) | collective-permute-done | bytes 81952 | tf_op jit(solution)/shard_map/ppermute | solution.py:270
  22.5 1.6 %shard_map.55 = bf16[4,384,512]{2,1,0:T(8,128)(2,1)} custom-call(bf16[4,4,8,512]{3,2,1,0:T(8,128)(2,1)S(1)} %copy-done.2, bf16[10,8,512]{2,1,0:T(8,128)(2,1)S(1)} %collective-permute-done.2.past_ref, bf16[4,8,16,512]{3,2,1,0:T(8,128)(2,1)S(1)} %copy-done.1, bf16[48,512]{1,0:T(8,128)(2,1)S(1)} %collective-permute-done.left_ref, ...), custom_call_target="tpu_custom_call" | custom-call | tf_op jit(solution)/shard_map/pallas_call | solution.py:298
  24.0 3.9 %all-to-all-start = ((bf16[4,384,512]{2,1,0:T(8,128)(2,1)}), bf16[4,384,512]{2,1,0:T(8,128)(2,1)S(1)}, u32[]{:S(2)}, u32[]{:S(2)}) async-start(bf16[4,384,512]{2,1,0:T(8,128)(2,1)} %shard_map.55), calls=%async_computation | async-start | bytes 3145728 | tf_op jit(solution)/shard_map/all_to_all | solution.py:326
  28.0 0.1 fusion
  28.0 0.1 collective-permute-start.5
  28.1 0.1 collective-permute-start.10
  28.2 3.3 %collective-permute-start.4 = (bf16[4,12,16,384]{3,2,1,0:T(8,128)(2,1)S(1)}, bf16[4,12,16,384]{3,2,1,0:T(8,128)(2,1)S(1)}, u32[]{:S(2)}, u32[]{:S(2)}) collective-permute-start(bf16[4,12,16,384]{3,2,1,0:T(8,128)(2,1)S(1)} %collective-permute-done.3.refs_1_), channel_id=1, source_target_pairs={{0,32},{32,0},{64,96},{96,64},{128,160},{160,128},{192,224},{224,1... | collective-permute-start | bytes 1769480 | tf_op jit(solution)/shard_map/ppermute | solution.py:308
  31.6 5.0 %collective-permute-done.5.refs_3_ = bf16[4,6,16,384]{3,2,1,0:T(8,128)(2,1)} collective-permute-done((bf16[4,6,16,384]{3,2,1,0:T(8,128)(2,1)S(1)}, bf16[4,6,16,384]{3,2,1,0:T(8,128)(2,1)}, u32[]{:S(2)}, u32[]{:S(2)}) %collective-permute-start.5) | collective-permute-done | bytes 294944 | tf_op jit(solution)/shard_map/ppermute | solution.py:315
  36.6 3.2 %collective-permute-done.10.refs_9_ = bf16[4,6,16,384]{3,2,1,0:T(8,128)(2,1)} collective-permute-done((bf16[4,6,16,384]{3,2,1,0:T(8,128)(2,1)S(1)}, bf16[4,6,16,384]{3,2,1,0:T(8,128)(2,1)}, u32[]{:S(2)}, u32[]{:S(2)}) %collective-permute-start.10) | collective-permute-done | bytes 294944 | tf_op jit(solution)/shard_map/ppermute | solution.py:315
  39.8 1.0 collective-permute-start.8
  40.8 4.0 %collective-permute-done.6.refs_4_ = bf16[4,6,16,384]{3,2,1,0:T(8,128)(2,1)S(1)} collective-permute-done((bf16[4,6,16,384]{3,2,1,0:T(8,128)(2,1)}, bf16[4,6,16,384]{3,2,1,0:T(8,128)(2,1)S(1)}, u32[]{:S(2)}, u32[]{:S(2)}) %collective-permute-start.6) | collective-permute-done | bytes 294944 | tf_op jit(solution)/shard_map/ppermute | solution.py:315
  44.8 0.1 collective-permute-start.7
  44.9 3.3 %all-to-all-done.slab_ref = bf16[4,384,512]{2,1,0:T(8,128)(2,1)S(1)} async-done(((bf16[4,384,512]{2,1,0:T(8,128)(2,1)}), bf16[4,384,512]{2,1,0:T(8,128)(2,1)S(1)}, u32[]{:S(2)}, u32[]{:S(2)}) %all-to-all-start) | async-done | bytes 1572896 | tf_op jit(solution)/shard_map/all_to_all | solution.py:326
  48.2 0.6 shard_map.58.box_ref
  48.8 0.9 constant_dynamic-slice_fusion
  49.7 0.8 copy-done.5
  50.6 1.5 %shard_map.57.early_ref = bf16[3,512,384]{2,1,0:T(8,128)(2,1)S(1)} custom-call(bf16[4,12,16,384]{3,2,1,0:T(8,128)(2,1)} %copy-done.3, bf16[4,12,16,384]{3,2,1,0:T(8,128)(2,1)} %copy-done.4, bf16[4,12,16,384]{3,2,1,0:T(8,128)(2,1)} %copy-done.5, bf16[4,6,16,384]{3,2,1,0:T(8,128)(2,1)} %collective-permute-done.5.refs_3_, bf16[4,6,16,384]{3,2,1,0:T(8,128)(2,1)} %copy-done.6, ...), custom_call_target="tpu_custom_call" | custom-call | tf_op jit(solution)/shard_map/pallas_call | solution.py:320
  52.0 0.1 collective-permute-start.12
  52.1 0.5 collective-permute-start.14
  52.6 0.1 collective-permute-start.15
  52.7 0.0 collective-permute-start.13
  52.7 0.8 collective-permute-done.12.refs_8_
  53.5 2.7 %shard_map.60 = bf16[4,512,128]{2,1,0:T(8,128)(2,1)} custom-call(bf16[3,512,768]{2,1,0:T(8,128)(2,1)S(1)} %shard_map.58.box_ref, bf16[3,512,384]{2,1,0:T(8,128)(2,1)S(1)} %shard_map.57.early_ref, bf16[4,12,16,384]{3,2,1,0:T(8,128)(2,1)} %copy-done.3, bf16[4,12,16,384]{3,2,1,0:T(8,128)(2,1)} %copy-done.4, bf16[4,12,16,384]{3,2,1,0:T(8,128)(2,1)} %copy-done.5, ...), custom_call_target="tpu_custom_call" | custom-call | tf_op jit(solution)/shard_map/pallas_call | solution.py:344
  56.2 4.1 %all-to-all-start.2 = ((bf16[4,512,128]{2,1,0:T(8,128)(2,1)}), bf16[4,512,128]{2,1,0:T(8,128)(2,1)S(1)}, u32[]{:S(2)}, u32[]{:S(2)}) async-start(bf16[4,512,128]{2,1,0:T(8,128)(2,1)} %shard_map.60), calls=%async_computation.2 | async-start | bytes 1048576 | tf_op jit(solution)/shard_map/all_to_all | solution.py:353
  60.2 2.6 %collective-permute-start.16 = (bf16[2,6,16,384]{3,2,1,0:T(8,128)(2,1)S(1)}, bf16[2,6,16,384]{3,2,1,0:T(8,128)(2,1)S(1)}, u32[]{:S(2)}, u32[]{:S(2)}) collective-permute-start(bf16[2,6,16,384]{3,2,1,0:T(8,128)(2,1)S(1)} %collective-permute-done.13.refs_11_), channel_id=1, source_target_pairs={{0,32},{32,0},{64,96},{96,64},{128,160},{160,128},{192,224},{224,1... | collective-permute-start | bytes 442376 | tf_op jit(solution)/shard_map/ppermute | solution.py:337
  62.8 0.1 dynamic-slice_bitcast_fusion.bias_ref
  62.9 0.9 collective-permute-done.16.refs_14_
  63.8 4.5 %shard_map.59 = (f32[8,4,16,128]{3,2,1,0:T(8,128)S(1)}, bf16[9,512,384]{2,1,0:T(8,128)(2,1)}) custom-call(bf16[4,384,512]{2,1,0:T(8,128)(2,1)S(1)} %all-to-all-done.slab_ref, f32[1,128]{1,0:T(1,128)S(1)} %dynamic-slice_bitcast_fusion.bias_ref, bf16[4,12,16,384]{3,2,1,0:T(8,128)(2,1)} %copy-done.3, bf16[4,12,16,384]{3,2,1,0:T(8,128)(2,1)} %copy-done.4, ...), custom_call_target="tpu_custom_call" | custom-call | flops 1811939328 | bytes 5242880 | tf_op jit(solution)/shard_map/pallas_call | solution.py:358
  68.4 1.2 %all-to-all-done.2.act_ref = bf16[4,512,128]{2,1,0:T(8,128)(2,1)S(1)} async-done(((bf16[4,512,128]{2,1,0:T(8,128)(2,1)}), bf16[4,512,128]{2,1,0:T(8,128)(2,1)S(1)}, u32[]{:S(2)}, u32[]{:S(2)}) %all-to-all-start.2) | async-done | bytes 524320 | tf_op jit(solution)/shard_map/all_to_all | solution.py:353
  69.6 0.1 shard_map.61
  69.7 2.8 %collective-permute-start.17 = (bf16[8,4,8,128]{3,2,1,0:T(8,128)(2,1)S(1)}, bf16[8,4,8,128]{3,2,1,0:T(8,128)(2,1)S(1)}, u32[]{:S(2)}, u32[]{:S(2)}) collective-permute-start(bf16[8,4,8,128]{3,2,1,0:T(8,128)(2,1)S(1)} %get-tuple-element.19), channel_id=1, source_target_pairs={{32,0},{64,32},{96,64},{128,96},{160,128},{192,160},{224,192},{33,... | collective-permute-start | bytes 196616 | tf_op jit(solution)/shard_map/ppermute | solution.py:270
  72.5 1.9 %collective-permute-done.17.later_ref = bf16[8,4,8,128]{3,2,1,0:T(8,128)(2,1)S(1)} collective-permute-done((bf16[8,4,8,128]{3,2,1,0:T(8,128)(2,1)S(1)}, bf16[8,4,8,128]{3,2,1,0:T(8,128)(2,1)S(1)}, u32[]{:S(2)}, u32[]{:S(2)}) %collective-permute-start.17) | collective-permute-done | bytes 65568 | tf_op jit(solution)/shard_map/ppermute | solution.py:270
  74.4 5.3 %collective-permute-start.18 = (bf16[4,24,128]{2,1,0:T(8,128)(2,1)S(1)}, bf16[4,24,128]{2,1,0:T(8,128)(2,1)S(1)}, u32[]{:S(2)}, u32[]{:S(2)}) collective-permute-start(bf16[4,24,128]{2,1,0:T(8,128)(2,1)S(1)} %pad_maximum_fusion.3), channel_id=1, source_target_pairs={{0,1},{1,2},{2,3},{3,4},{4,5},{5,6},{6,7},{8,9},{9,10},{10,11},{11... | collective-permute-start | bytes 73736 | tf_op jit(solution)/shard_map/ppermute | solution.py:270
  79.7 1.9 %collective-permute-start.19 = (bf16[4,24,128]{2,1,0:T(8,128)(2,1)S(1)}, bf16[4,24,128]{2,1,0:T(8,128)(2,1)S(1)}, u32[]{:S(2)}, u32[]{:S(2)}) collective-permute-start(bf16[4,24,128]{2,1,0:T(8,128)(2,1)S(1)} %pad_maximum_fusion.4), channel_id=1, source_target_pairs={{1,0},{2,1},{3,2},{4,3},{5,4},{6,5},{7,6},{9,8},{10,9},{11,10},{12... | collective-permute-start | bytes 73736 | tf_op jit(solution)/shard_map/ppermute | solution.py:270
  81.6 5.0 %collective-permute-done.19.right_ref = bf16[4,24,128]{2,1,0:T(8,128)(2,1)S(1)} collective-permute-done((bf16[4,24,128]{2,1,0:T(8,128)(2,1)S(1)}, bf16[4,24,128]{2,1,0:T(8,128)(2,1)S(1)}, u32[]{:S(2)}, u32[]{:S(2)}) %collective-permute-start.19) | collective-permute-done | bytes 24608 | tf_op jit(solution)/shard_map/ppermute | solution.py:270
  86.6 3.8 %shard_map.62 = bf16[4,8,16,512]{3,2,1,0:T(8,128)(2,1)S(1)} custom-call(bf16[8,4,16,128]{3,2,1,0:T(8,128)(2,1)S(1)} %get-tuple-element.18.g_ref, bf16[8,4,8,128]{3,2,1,0:T(8,128)(2,1)S(1)} %collective-permute-done.17.later_ref, bf16[4,24,128]{2,1,0:T(8,128)(2,1)S(1)} %collective-permute-done.18.left_ref, ...), custom_call_target="tpu_custom_call" | custom-call | tf_op jit(solution)/shard_map/pallas_call | solution.py:382
  90.4 12.5 %all_to_all.20 = bf16[4,8,16,512]{3,2,1,0:T(8,128)(2,1)S(1)} all-to-all(bf16[4,8,16,512]{3,2,1,0:T(8,128)(2,1)S(1)} %shard_map.62), channel_id=1, replica_groups=mesh['ta'=8,'ha'=4,'wa'=8] {'ha'}, dimensions={0} | all-to-all | bytes 1048576 | tf_op jit(solution)/shard_map/all_to_all | solution.py:388
  103.0 0.1 reduce_sum.12
  103.0 0.7 copy.17
  (50 shorter events, 0.2 us)
Async XLA Ops:
  0.0 62.8 %copy-start = (f32[512]{0:T(512)S(1)}, f32[512]{0:T(512)}, u32[]{:S(2)}) copy-start(f32[512]{0:T(512)} %param.7) | copy-start | bytes 6148
  0.0 6.4 %copy-start.2 = (bf16[4,4,8,512]{3,2,1,0:T(8,128)(2,1)S(1)}, bf16[4,4,8,512]{3,2,1,0:T(8,128)(2,1)}, u32[]{:S(2)}) copy-start(bf16[4,4,8,512]{3,2,1,0:T(8,128)(2,1)} %lat_ref.1) | copy-start | bytes 393220
  0.0 14.0 %slice-start = ((bf16[4,4,8,512]{3,2,1,0:T(8,128)(2,1)}), bf16[2,4,8,512]{3,2,1,0:T(8,128)(2,1)S(1)}, s32[]{:S(2)}) async-start(bf16[4,4,8,512]{3,2,1,0:T(8,128)(2,1)} %lat_ref.1), calls=%async_computation.4 | async-start | bytes 131072 | tf_op jit(solution)/shard_map/slice | solution.py:294
  0.0 6.5 %copy-start.1 = (bf16[4,8,16,512]{3,2,1,0:T(8,128)(2,1)S(1)}, bf16[4,8,16,512]{3,2,1,0:T(8,128)(2,1)}, u32[]{:S(2)}) copy-start(bf16[4,8,16,512]{3,2,1,0:T(8,128)(2,1)} %cot_ref.1) | copy-start | bytes 1572868
  2.1 14.5 %all-to-all-start.1 = ((bf16[4,12,16,384]{3,2,1,0:T(8,128)(2,1)}), bf16[4,12,16,384]{3,2,1,0:T(8,128)(2,1)S(1)}, u32[]{:S(2)}, u32[]{:S(2)}) async-start(bf16[4,12,16,384]{3,2,1,0:T(8,128)(2,1)} %shard_map.56), calls=%async_computation.1 | async-start | bytes 1179648 | tf_op jit(solution)/shard_map/all_to_all | solution.py:296
  6.9 9.8 %collective-permute-start.1 = (bf16[48,512]{1,0:T(8,128)(2,1)S(1)}, bf16[48,512]{1,0:T(8,128)(2,1)S(1)}, u32[]{:S(2)}, u32[]{:S(2)}) collective-permute-start(bf16[48,512]{1,0:T(8,128)(2,1)S(1)} %pad_maximum_fusion.2), channel_id=1, source_target_pairs={{1,0},{2,1},{3,2},{4,3},{5,4},{6,5},{7,6},{9,8},{10,9},{11,10},{12... | collective-permute-start | bytes 147464 | tf_op jit(solution)/shard_map/ppermute | solution.py:270
  9.0 7.7 %collective-permute-start = (bf16[48,512]{1,0:T(8,128)(2,1)S(1)}, bf16[48,512]{1,0:T(8,128)(2,1)S(1)}, u32[]{:S(2)}, u32[]{:S(2)}) collective-permute-start(bf16[48,512]{1,0:T(8,128)(2,1)S(1)} %pad_maximum_fusion.1), channel_id=1, source_target_pairs={{0,1},{1,2},{2,3},{3,4},{4,5},{5,6},{6,7},{8,9},{9,10},{10,11},{11... | collective-permute-start | bytes 147464 | tf_op jit(solution)/shard_map/ppermute | solution.py:270
  16.6 7.5 %copy-start.3 = (bf16[4,12,16,384]{3,2,1,0:T(8,128)(2,1)}, bf16[4,12,16,384]{3,2,1,0:T(8,128)(2,1)S(1)}, u32[]{:S(2)}) copy-start(bf16[4,12,16,384]{3,2,1,0:T(8,128)(2,1)S(1)} %all-to-all-done.1.refs_0_) | copy-start | bytes 1769476
  16.6 11.4 %collective-permute-start.3 = (bf16[4,12,16,384]{3,2,1,0:T(8,128)(2,1)S(1)}, bf16[4,12,16,384]{3,2,1,0:T(8,128)(2,1)S(1)}, u32[]{:S(2)}, u32[]{:S(2)}) collective-permute-start(bf16[4,12,16,384]{3,2,1,0:T(8,128)(2,1)S(1)} %all-to-all-done.1.refs_0_), channel_id=1, source_target_pairs={{1,0},{2,1},{3,2},{4,3},{5,4},{6,5},{7,6},{0,7},{39,32},{32,33},{3... | collective-permute-start | bytes 1769480 | tf_op jit(solution)/shard_map/ppermute | solution.py:307
  16.7 5.8 %collective-permute-start.2 = (bf16[10,8,512]{2,1,0:T(8,128)(2,1)S(1)}, bf16[10,8,512]{2,1,0:T(8,128)(2,1)S(1)}, u32[]{:S(2)}, u32[]{:S(2)}) collective-permute-start(bf16[10,8,512]{2,1,0:T(8,128)(2,1)S(1)} %pad_maximum_fusion), channel_id=1, source_target_pairs={{0,32},{32,64},{64,96},{96,128},{128,160},{160,192},{192,224},{1,3... | collective-permute-start | bytes 245768 | tf_op jit(solution)/shard_map/ppermute | solution.py:270
  24.0 24.1 %all-to-all-start = ((bf16[4,384,512]{2,1,0:T(8,128)(2,1)}), bf16[4,384,512]{2,1,0:T(8,128)(2,1)S(1)}, u32[]{:S(2)}, u32[]{:S(2)}) async-start(bf16[4,384,512]{2,1,0:T(8,128)(2,1)} %shard_map.55), calls=%async_computation | async-start | bytes 3145728 | tf_op jit(solution)/shard_map/all_to_all | solution.py:326
  28.0 20.8 %copy-start.4 = (bf16[4,12,16,384]{3,2,1,0:T(8,128)(2,1)}, bf16[4,12,16,384]{3,2,1,0:T(8,128)(2,1)S(1)}, u32[]{:S(2)}) copy-start(bf16[4,12,16,384]{3,2,1,0:T(8,128)(2,1)S(1)} %collective-permute-done.3.refs_1_) | copy-start | bytes 1769476
  28.0 8.6 %collective-permute-start.5 = (bf16[4,6,16,384]{3,2,1,0:T(8,128)(2,1)S(1)}, bf16[4,6,16,384]{3,2,1,0:T(8,128)(2,1)}, u32[]{:S(2)}, u32[]{:S(2)}) collective-permute-start(bf16[4,6,16,384]{3,2,1,0:T(8,128)(2,1)S(1)} %get-tuple-element.28), channel_id=1, source_target_pairs={{1,0},{2,1},{3,2},{4,3},{5,4},{6,5},{7,6},{0,7},{39,32},{32,33},{3... | collective-permute-start | bytes 884744 | tf_op jit(solution)/shard_map/ppermute | solution.py:315
  28.1 11.6 %collective-permute-start.10 = (bf16[4,6,16,384]{3,2,1,0:T(8,128)(2,1)S(1)}, bf16[4,6,16,384]{3,2,1,0:T(8,128)(2,1)}, u32[]{:S(2)}, u32[]{:S(2)}) collective-permute-start(bf16[4,6,16,384]{3,2,1,0:T(8,128)(2,1)S(1)} %get-tuple-element.27), channel_id=1, source_target_pairs={{1,0},{2,1},{3,2},{4,3},{5,4},{6,5},{7,6},{0,7},{39,32},{32,33},{3... | collective-permute-start | bytes 884744 | tf_op jit(solution)/shard_map/ppermute | solution.py:315
  28.2 21.5 %collective-permute-start.4 = (bf16[4,12,16,384]{3,2,1,0:T(8,128)(2,1)S(1)}, bf16[4,12,16,384]{3,2,1,0:T(8,128)(2,1)S(1)}, u32[]{:S(2)}, u32[]{:S(2)}) collective-permute-start(bf16[4,12,16,384]{3,2,1,0:T(8,128)(2,1)S(1)} %collective-permute-done.3.refs_1_), channel_id=1, source_target_pairs={{0,32},{32,0},{64,96},{96,64},{128,160},{160,128},{192,224},{224,1... | collective-permute-start | bytes 1769480 | tf_op jit(solution)/shard_map/ppermute | solution.py:308
  36.6 8.1 %collective-permute-start.6 = (bf16[4,6,16,384]{3,2,1,0:T(8,128)(2,1)}, bf16[4,6,16,384]{3,2,1,0:T(8,128)(2,1)S(1)}, u32[]{:S(2)}, u32[]{:S(2)}) collective-permute-start(bf16[4,6,16,384]{3,2,1,0:T(8,128)(2,1)} %collective-permute-done.5.refs_3_), channel_id=1, source_target_pairs={{1,0},{2,1},{3,2},{4,3},{5,4},{6,5},{7,6},{0,7},{39,32},{32,33},{3... | collective-permute-start | bytes 884744 | tf_op jit(solution)/shard_map/ppermute | solution.py:315
  39.8 9.0 %collective-permute-start.11 = (bf16[4,6,16,384]{3,2,1,0:T(8,128)(2,1)}, bf16[4,6,16,384]{3,2,1,0:T(8,128)(2,1)}, u32[]{:S(2)}, u32[]{:S(2)}) collective-permute-start(bf16[4,6,16,384]{3,2,1,0:T(8,128)(2,1)} %collective-permute-done.10.refs_9_), channel_id=1, source_target_pairs={{1,0},{2,1},{3,2},{4,3},{5,4},{6,5},{7,6},{0,7},{39,32},{32,33},{3... | collective-permute-start | bytes 884744 | tf_op jit(solution)/shard_map/ppermute | solution.py:315
  39.8 9.9 %collective-permute-start.8 = (bf16[4,6,16,384]{3,2,1,0:T(8,128)(2,1)}, bf16[4,6,16,384]{3,2,1,0:T(8,128)(2,1)}, u32[]{:S(2)}, u32[]{:S(2)}) collective-permute-start(bf16[4,6,16,384]{3,2,1,0:T(8,128)(2,1)} %collective-permute-done.5.refs_3_), channel_id=1, source_target_pairs={{0,32},{32,0},{64,96},{96,64},{128,160},{160,128},{192,224},{224,1... | collective-permute-start | bytes 884744 | tf_op jit(solution)/shard_map/ppermute | solution.py:316
  44.8 4.0 %copy-start.6 = (bf16[4,6,16,384]{3,2,1,0:T(8,128)(2,1)}, bf16[4,6,16,384]{3,2,1,0:T(8,128)(2,1)S(1)}, u32[]{:S(2)}) copy-start(bf16[4,6,16,384]{3,2,1,0:T(8,128)(2,1)S(1)} %collective-permute-done.6.refs_4_) | copy-start | bytes 884740
  44.8 5.0 %collective-permute-start.9 = (bf16[4,6,16,384]{3,2,1,0:T(8,128)(2,1)S(1)}, bf16[4,6,16,384]{3,2,1,0:T(8,128)(2,1)}, u32[]{:S(2)}, u32[]{:S(2)}) collective-permute-start(bf16[4,6,16,384]{3,2,1,0:T(8,128)(2,1)S(1)} %collective-permute-done.6.refs_4_), channel_id=1, source_target_pairs={{0,32},{32,0},{64,96},{96,64},{128,160},{160,128},{192,224},{224,1... | collective-permute-start | bytes 884744 | tf_op jit(solution)/shard_map/ppermute | solution.py:316
  44.8 7.2 %collective-permute-start.7 = (bf16[2,6,16,384]{3,2,1,0:T(8,128)(2,1)S(1)}, bf16[2,6,16,384]{3,2,1,0:T(8,128)(2,1)S(1)}, u32[]{:S(2)}, u32[]{:S(2)}) collective-permute-start(bf16[2,6,16,384]{3,2,1,0:T(8,128)(2,1)S(1)} %constant_dynamic-slice_fusion.1), channel_id=1, source_target_pairs={{1,0},{2,1},{3,2},{4,3},{5,4},{6,5},{7,6},{0,7},{39,32},{32,33},{3... | collective-permute-start | bytes 442376 | tf_op jit(solution)/shard_map/ppermute | solution.py:318
  49.7 0.8 copy-start.5
  52.0 1.5 %collective-permute-start.12 = (bf16[2,6,16,384]{3,2,1,0:T(8,128)(2,1)S(1)}, bf16[2,6,16,384]{3,2,1,0:T(8,128)(2,1)S(1)}, u32[]{:S(2)}, u32[]{:S(2)}) collective-permute-start(bf16[2,6,16,384]{3,2,1,0:T(8,128)(2,1)S(1)} %collective-permute-done.7.refs_5_), channel_id=1, source_target_pairs={{0,32},{32,0},{64,96},{96,64},{128,160},{160,128},{192,224},{224,1... | collective-permute-start | bytes 442376 | tf_op jit(solution)/shard_map/ppermute | solution.py:337
  52.1 10.8 %collective-permute-start.14 = (bf16[4,6,16,384]{3,2,1,0:T(8,128)(2,1)}, bf16[4,6,16,384]{3,2,1,0:T(8,128)(2,1)S(1)}, u32[]{:S(2)}, u32[]{:S(2)}) collective-permute-start(bf16[4,6,16,384]{3,2,1,0:T(8,128)(2,1)} %collective-permute-done.10.refs_9_), channel_id=1, source_target_pairs={{0,32},{32,0},{64,96},{96,64},{128,160},{160,128},{192,224},{224,1... | collective-permute-start | bytes 884744 | tf_op jit(solution)/shard_map/ppermute | solution.py:316
  52.6 10.3 %collective-permute-start.15 = (bf16[4,6,16,384]{3,2,1,0:T(8,128)(2,1)}, bf16[4,6,16,384]{3,2,1,0:T(8,128)(2,1)S(1)}, u32[]{:S(2)}, u32[]{:S(2)}) collective-permute-start(bf16[4,6,16,384]{3,2,1,0:T(8,128)(2,1)} %collective-permute-done.11.refs_10_), channel_id=1, source_target_pairs={{0,32},{32,0},{64,96},{96,64},{128,160},{160,128},{192,224},{224,1... | collective-permute-start | bytes 884744 | tf_op jit(solution)/shard_map/ppermute | solution.py:316
  52.7 7.5 %collective-permute-start.13 = (bf16[2,6,16,384]{3,2,1,0:T(8,128)(2,1)S(1)}, bf16[2,6,16,384]{3,2,1,0:T(8,128)(2,1)S(1)}, u32[]{:S(2)}, u32[]{:S(2)}) collective-permute-start(bf16[2,6,16,384]{3,2,1,0:T(8,128)(2,1)S(1)} %constant_dynamic-slice_fusion), channel_id=1, source_target_pairs={{1,0},{2,1},{3,2},{4,3},{5,4},{6,5},{7,6},{0,7},{39,32},{32,33},{3... | collective-permute-start | bytes 442376 | tf_op jit(solution)/shard_map/ppermute | solution.py:318
  56.2 13.4 %all-to-all-start.2 = ((bf16[4,512,128]{2,1,0:T(8,128)(2,1)}), bf16[4,512,128]{2,1,0:T(8,128)(2,1)S(1)}, u32[]{:S(2)}, u32[]{:S(2)}) async-start(bf16[4,512,128]{2,1,0:T(8,128)(2,1)} %shard_map.60), calls=%async_computation.2 | async-start | bytes 1048576 | tf_op jit(solution)/shard_map/all_to_all | solution.py:353
  60.2 3.6 %collective-permute-start.16 = (bf16[2,6,16,384]{3,2,1,0:T(8,128)(2,1)S(1)}, bf16[2,6,16,384]{3,2,1,0:T(8,128)(2,1)S(1)}, u32[]{:S(2)}, u32[]{:S(2)}) collective-permute-start(bf16[2,6,16,384]{3,2,1,0:T(8,128)(2,1)S(1)} %collective-permute-done.13.refs_11_), channel_id=1, source_target_pairs={{0,32},{32,0},{64,96},{96,64},{128,160},{160,128},{192,224},{224,1... | collective-permute-start | bytes 442376 | tf_op jit(solution)/shard_map/ppermute | solution.py:337
  62.9 0.9 copy-start.7
  62.9 0.9 copy-start.8
  69.7 4.7 %collective-permute-start.17 = (bf16[8,4,8,128]{3,2,1,0:T(8,128)(2,1)S(1)}, bf16[8,4,8,128]{3,2,1,0:T(8,128)(2,1)S(1)}, u32[]{:S(2)}, u32[]{:S(2)}) collective-permute-start(bf16[8,4,8,128]{3,2,1,0:T(8,128)(2,1)S(1)} %get-tuple-element.19), channel_id=1, source_target_pairs={{32,0},{64,32},{96,64},{128,96},{160,128},{192,160},{224,192},{33,... | collective-permute-start | bytes 196616 | tf_op jit(solution)/shard_map/ppermute | solution.py:270
  74.4 7.2 %collective-permute-start.18 = (bf16[4,24,128]{2,1,0:T(8,128)(2,1)S(1)}, bf16[4,24,128]{2,1,0:T(8,128)(2,1)S(1)}, u32[]{:S(2)}, u32[]{:S(2)}) collective-permute-start(bf16[4,24,128]{2,1,0:T(8,128)(2,1)S(1)} %pad_maximum_fusion.3), channel_id=1, source_target_pairs={{0,1},{1,2},{2,3},{3,4},{4,5},{5,6},{6,7},{8,9},{9,10},{10,11},{11... | collective-permute-start | bytes 73736 | tf_op jit(solution)/shard_map/ppermute | solution.py:270
  79.7 6.9 %collective-permute-start.19 = (bf16[4,24,128]{2,1,0:T(8,128)(2,1)S(1)}, bf16[4,24,128]{2,1,0:T(8,128)(2,1)S(1)}, u32[]{:S(2)}, u32[]{:S(2)}) collective-permute-start(bf16[4,24,128]{2,1,0:T(8,128)(2,1)S(1)} %pad_maximum_fusion.4), channel_id=1, source_target_pairs={{1,0},{2,1},{3,2},{4,3},{5,4},{6,5},{7,6},{9,8},{10,9},{11,10},{12... | collective-permute-start | bytes 73736 | tf_op jit(solution)/shard_map/ppermute | solution.py:270
